TPU v7x, 32 devices: a whole 2x2x4 slice. The times are simulated.
32 devices in a mesh: grid: 8 (over z, x), sub: 4 (over y, core).
Axes of the slice: x: 2, y: 2, z: 4, core: 2. Of those that a mesh axis runs over, the one named last changes fastest.
Arguments:
- fine_residual: float32 [8, 32, 5, 16, 256], P('grid', 'sub'), may hold values from -16 to 16
- fine_solution: float32 [8, 32, 5, 16, 256], P('grid', 'sub'), may hold values from -6 to 6
- plane_of_slot: int32 [8, 32], P('grid', 'sub'), may hold values from 0 to 31, as said below
- coarse_diagonal: float32 [8, 16, 5, 8, 128], P('grid', 'sub'), may hold values from 0.5 to 8
- coupling: float32 [5, 5], replicated, may hold values from -2.5 to 2.5
- donor_cells: int32 [8, 4, 64], P('grid', 'sub'), may hold values from 0 to 2942, as said below
- donor_offsets: float32 [8, 4, 3, 64], P('grid', 'sub'), may hold values from 0 to 1
- receptor_cells: int32 [8, 4, 64], P('grid', 'sub'), may hold values from 0 to 4095, as said below
- fringe_counts: int32 [8, 8], replicated, may hold values from 0 to 8, as said below
Outputs:
- corrected: float32 [8, 32, 5, 16, 256], P('grid', 'sub')
Inputs may be any that keep to these rules, and one draw needn't show every extreme that they name: `plane_of_slot`: each row holds every fine plane number of its grid once. The 8 slots of one device (slots 8 s to 8 s + 7) hold at most 2 fine planes whose coarse planes belong to any one sub index, and exactly 2 for some pair. `donor_cells`: A donor base cell's local plane, row and column are below 3, 7 and 127, so its eight corners lie on the same device. `receptor_cells`: the 64 receptor cells of one device are distinct. `fringe_counts`: entry [g, h] counts the live rows that every device of grid g sends to the device of grid h with the same sub index; the diagonal is 0.
All inputs are finite; a program needn't handle non-finite values.
Results may differ from a plain program's by a relative error of at most 0.0003.
Values sent between devices are 32-bit elements; how exact they have to be, the bound alone decides.
No kernel may reach another device: no remote copies, remote signals or barrier semaphores. Data moves between devices by JAX's collectives and lax.ppermute only.
A program may use at most 64 MiB of HBM per device.

v0:
```python
import jax
import jax.numpy as jnp
from jax import lax
from jax.sharding import PartitionSpec as P

FRINGE = 8
SWEEPS = 2


OMEGA = 0.8


def padded_2(block, sides, width):
    for axis, dim in sides:
        count = lax.axis_size(axis)
        forward = [(i, i + 1) for i in range(count - 1)]
        backward = [(target, source) for source, target in forward]
        low = lax.ppermute(
            lax.slice_in_dim(block, block.shape[dim] - width, None, axis=dim), axis, forward
        )
        high = lax.ppermute(lax.slice_in_dim(block, 0, width, axis=dim), axis, backward)
        block = jnp.concatenate([low, block, high], axis=dim)
    return block


def restrict_planes(fine_field):
    dims_in = fine_field.shape
    split_cells = fine_field.reshape(dims_in[:-2] + (dims_in[-2] // 2, 2, dims_in[-1] // 2, 2))
    return 0.125 * jnp.sum(split_cells, axis=(-3, -1))


def pair_sum(field, axis):
    which = axis % field.ndim
    length = field.shape[which]
    empty = jnp.zeros_like(lax.slice_in_dim(field, 0, 1, axis=which))
    below_side = jnp.concatenate(
        [empty, lax.slice_in_dim(field, 0, length - 1, axis=which)], axis=which
    )
    above_side = jnp.concatenate(
        [lax.slice_in_dim(field, 1, length, axis=which), empty], axis=which
    )
    return below_side + above_side


def operate(field, padded, diagonal, coupling):
    which = field.ndim - 4
    length = padded.shape[which]
    beside = lax.slice_in_dim(padded, 2, length, axis=which) + lax.slice_in_dim(
        padded, 0, length - 2, axis=which
    )
    beside = beside + pair_sum(field, field.ndim - 2)
    beside = beside + pair_sum(field, field.ndim - 1)
    coupled = jnp.einsum("vw,...wyz->...vyz", coupling, field, precision=lax.Precision.HIGHEST)
    return (6.0 + diagonal) * field - beside + 2.0 * jnp.tanh(coupled)


def apply_operator(field, diagonal, coupling):
    padded = padded_2(field, (("sub", 0),), 1)
    return operate(field, padded, diagonal, coupling)


def corner_values(flat_field, donor_base, height, depth):
    corners = []
    for step_x in (0, 1):
        for step_y in (0, 1):
            for step_z in (0, 1):
                where_cells = donor_base + step_x * height * depth + step_y * depth + step_z
                corners.append(jnp.take_along_axis(flat_field, where_cells[..., None, :], axis=-1))
    return corners


def blend(corners, offsets):
    frac_x = offsets[..., 0:1, :]
    frac_y = offsets[..., 1:2, :]
    frac_z = offsets[..., 2:3, :]
    summed = None
    number = 0
    for step_x in (0, 1):
        for step_y in (0, 1):
            for step_z in (0, 1):
                weight_x = frac_x if step_x else 1.0 - frac_x
                weight_y = frac_y if step_y else 1.0 - frac_y
                weight_z = frac_z if step_z else 1.0 - frac_z
                term = weight_x * weight_y * weight_z * corners[number]
                summed = term if summed is None else summed + term
                number = number + 1
    return summed


def refine(field, axis):
    which = axis % field.ndim
    length = field.shape[which]
    empty = jnp.zeros_like(lax.slice_in_dim(field, 0, 1, axis=which))
    below_side = jnp.concatenate(
        [empty, lax.slice_in_dim(field, 0, length - 1, axis=which)], axis=which
    )
    above_side = jnp.concatenate(
        [lax.slice_in_dim(field, 1, length, axis=which), empty], axis=which
    )
    first_half = 0.75 * field + 0.25 * below_side
    second_half = 0.75 * field + 0.25 * above_side
    joined = jnp.stack([first_half, second_half], axis=which + 1)
    new_dims = list(field.shape)
    new_dims[which] = 2 * length
    return joined.reshape(new_dims)


def shards(
    fine_residual,
    fine_solution,
    plane_of_slot,
    coarse_diagonal,
    coupling,
    donor_cells,
    donor_offsets,
    receptor_cells,
    fringe_counts,
):
    grid_index = lax.axis_index("grid")
    sub_index = lax.axis_index("sub")
    diagonal = coarse_diagonal[0]
    planes, variables, height, depth_cells = diagonal.shape
    cell_count = planes * height * depth_cells
    plane_ids = plane_of_slot[0]
    blocks = plane_ids.shape[0]
    solution_planes = restrict_planes(fine_solution[0])
    residual_planes = restrict_planes(fine_residual[0])
    contrib = jnp.stack([solution_planes, residual_planes], axis=1).reshape(blocks, -1)
    targets = plane_ids // 2
    wanted = sub_index * planes + jnp.arange(planes, dtype=jnp.int32)
    gathered, gathered_ids = (
        lax.all_gather(contrib, "sub", axis=0, tiled=True),
        lax.all_gather(plane_ids, "sub", axis=0, tiled=True),
    )
    select = ((gathered_ids // 2)[None, :] == wanted[:, None]).astype(jnp.float32)
    owned_sums = jnp.dot(
        select, gathered, precision=lax.Precision.HIGHEST, preferred_element_type=jnp.float32
    )
    owned_sums = owned_sums.reshape(planes, 2, variables, height, depth_cells)
    restricted_solution = owned_sums[:, 0]
    restricted_residual = owned_sums[:, 1]
    forcing = apply_operator(restricted_solution, diagonal, coupling) + restricted_residual
    slot_count = donor_cells.shape[-1]
    column = lax.dynamic_index_in_dim(fringe_counts, grid_index, 1, keepdims=False)
    allowed = jnp.repeat(column, FRINGE)
    live_slot = jnp.arange(slot_count, dtype=jnp.int32) % FRINGE < allowed
    target_cells = jnp.where(live_slot, receptor_cells[0, 0], cell_count)
    receptor_mask = jnp.zeros((cell_count,), jnp.float32).at[target_cells].set(1.0, mode="drop")
    receptor_mask = receptor_mask.reshape(planes, 1, height, depth_cells)
    donor_base = donor_cells[0, 0]
    offsets = donor_offsets[0, 0]
    field = restricted_solution
    for sweep_index in range(SWEEPS):
        flat_field = field.transpose(1, 0, 2, 3).reshape(variables, cell_count)
        corners = corner_values(flat_field, donor_base, height, depth_cells)
        arrived = lax.all_to_all(
            blend(corners, offsets), "grid", split_axis=1, concat_axis=1, tiled=True
        )
        flat_field = flat_field.at[:, target_cells].set(arrived, mode="drop")
        field = flat_field.reshape(variables, planes, height, depth_cells).transpose(1, 0, 2, 3)
        update = field + OMEGA * (forcing - apply_operator(field, diagonal, coupling)) / (
            6.0 + diagonal
        )
        field = jnp.where(receptor_mask > 0.5, field, update)
    correction = (field - restricted_solution).reshape(planes, -1)
    neighbour = targets - 1 + 2 * (plane_ids % 2)
    shard_rows = lax.all_gather(correction, "sub", axis=0, tiled=True)
    row_ids = jnp.arange(shard_rows.shape[0], dtype=jnp.int32)
    weights = 0.75 * (targets[:, None] == row_ids[None, :]).astype(jnp.float32)
    weights = weights + 0.25 * (neighbour[:, None] == row_ids[None, :]).astype(jnp.float32)
    along_x = jnp.dot(
        weights, shard_rows, precision=lax.Precision.HIGHEST, preferred_element_type=jnp.float32
    )
    along_x = along_x.reshape(blocks, variables, height, depth_cells)
    prolonged = refine(refine(along_x, -2), -1)
    return (fine_solution[0] + prolonged)[None]


def solution(mesh):
    in_specs = (
        P("grid", "sub", None, None, None),
        P("grid", "sub", None, None, None),
        P("grid", "sub"),
        P("grid", "sub", None, None, None),
        P(),
        P("grid", "sub", None),
        P("grid", "sub", None, None),
        P("grid", "sub", None),
        P(),
    )
    out_specs = P("grid", "sub", None, None, None)
    return jax.shard_map(shards, mesh=mesh, in_specs=in_specs, out_specs=out_specs, check_vma=False)
```

profile of v0, /device:TPU:0, one launch (start us, length us, event | category | flops | bytes accessed | tf_op | source)
XLA Modules:
  0.0 167.8 jit_solution(9197063399181304504)
XLA Ops:
  6.5 6.6 %copy.239 = f32[1,8,5,16,256]{1,4,3,2,0:T(8,128)} copy(f32[1,8,5,16,256]{4,3,2,1,0:T(8,128)} %param.11) | data formatting | bytes 1310720 | tf_op args[0]
  13.2 11.7 %reduce_sum.19 = f32[8,5,8,128]{0,3,2,1:T(8,128)S(1)} reduce(f32[8,5,8,2,128,2]{0,5,4,3,2,1:T(2,128)} %bitcast.406, f32[]{:T(128)} %constant.103.clone.1), dimensions={3,5}, to_apply=%region_2.3 | reduce | flops 122880 | bytes 819204 | tf_op jit(solution)/shard_map/reduce_sum | solution.py:29
  24.9 1.7 multiply_bitcast_fusion
  26.5 2.5 %copy.241 = f32[8,1,5,8,128]{4,3,2,1,0:T(8,128)S(1)} copy(f32[8,1,5,8,128]{0,4,3,2,1:T(8,128)} %multiply_bitcast_fusion) | data formatting | bytes 327680 | tf_op jit(solution)/shard_map/mul | solution.py:29
  29.1 5.5 %copy.238 = f32[1,8,5,16,256]{1,4,3,2,0:T(8,128)} copy(f32[1,8,5,16,256]{4,3,2,1,0:T(8,128)S(1)} %copy-done.1) | data formatting | bytes 1310720 | tf_op args[1]
  34.6 11.7 %reduce_sum.18 = f32[8,5,8,128]{0,3,2,1:T(8,128)S(1)} reduce(f32[8,5,8,2,128,2]{0,5,4,3,2,1:T(2,128)} %bitcast.407, f32[]{:T(128)} %constant.103.clone.1), dimensions={3,5}, to_apply=%region_1.0 | reduce | flops 122880 | bytes 819204 | tf_op jit(solution)/shard_map/reduce_sum | solution.py:29
  46.3 1.7 multiply_bitcast_fusion.1
  48.0 2.5 %copy.240 = f32[8,1,5,8,128]{4,3,2,1,0:T(8,128)S(1)} copy(f32[8,1,5,8,128]{0,4,3,2,1:T(8,128)} %multiply_bitcast_fusion.1) | data formatting | bytes 327680 | tf_op jit(solution)/shard_map/mul | solution.py:29
  54.6 6.4 %all-reduce.16 = s32[32]{0:T(128)S(1)} all-reduce(s32[32]{0:T(128)S(1)} %get-tuple-element.46), channel_id=2, replica_groups=mesh['grid'=8,'sub'=4] {'sub'}, use_global_device_ids=true, to_apply=%add.16 | all-reduce | flops 32 | bytes 256 | tf_op jit(solution)/shard_map/all_gather | solution.py:133
  63.5 8.9 %all-gather.4.cloned.1.call-done = f32[32,10240]{1,0:T(8,128)} async-done(((f32[8,10240]{1,0:T(8,128)}), f32[32,10240]{1,0:T(8,128)}) %all-gather.4.cloned.1.call-update) | async-done | bytes 1310736 | tf_op jit(solution)/shard_map/all_gather | solution.py:132
  72.4 1.8 %convolution_bitcast_fusion = f32[1,4,80,128]{3,1,2,0:T(4,128)S(1)} fusion(f32[32,10240]{1,0:T(8,128)} %all-gather.4.cloned.1.call-done, s32[32]{0:T(128)S(1)} %and_select_fusion, s32[4]{0:T(128)S(1)} %iota_add_fusion), kind=kOutput, calls=%fused_computation.21 | convolution fusion | flops 15728768 | bytes 1474704 | tf_op jit(solution)/shard_map/dot_general | solution.py:136
  94.1 5.5 %all-to-all-start = ((f32[5,8,8]{2,0,1:T(8,128)}), f32[5,8,8]{2,0,1:T(8,128)}, u32[]{:S(2)}, u32[]{:S(2)}) async-start(f32[5,8,8]{2,0,1:T(8,128)} %copy.259), calls=%async_computation | async-start | bytes 65536 | tf_op jit(solution)/shard_map/all_to_all | solution.py:156
  100.2 1.8 %collective-permute-start.1 = (f32[1,5,8,128]{3,1,2,0:T(8,128)}, f32[1,5,8,128]{3,1,2,0:T(8,128)S(1)}, u32[]{:S(2)}, u32[]{:S(2)}) collective-permute-start(f32[1,5,8,128]{3,1,2,0:T(8,128)} %bitcast.403), channel_id=1, source_target_pairs={{0,1},{1,2},{2,3},{4,5},{5,6},{6,7},{8,9},{9,10},{10,11},{12,13},{... | collective-permute-start | bytes 61448 | tf_op jit(solution)/shard_map/ppermute | solution.py:18
  104.0 2.4 %all-to-all-done = f32[5,8,8]{2,0,1:T(8,128)} async-done(((f32[5,8,8]{2,0,1:T(8,128)}), f32[5,8,8]{2,0,1:T(8,128)}, u32[]{:S(2)}, u32[]{:S(2)}) %all-to-all-start) | async-done | bytes 1312 | tf_op jit(solution)/shard_map/all_to_all | solution.py:156
  107.3 1.6 scatter_fusion
  111.0 1.3 collective-permute-start.2
  122.6 12.5 %all_to_all.24 = f32[5,8,8]{2,0,1:T(8,128)S(1)} all-to-all(f32[5,8,8]{2,0,1:T(8,128)S(1)} %copy.285), channel_id=1, replica_groups=mesh['grid'=8,'sub'=4] {'grid'}, dimensions={1} | all-to-all | bytes 2560 | tf_op jit(solution)/shard_map/all_to_all | solution.py:156
  135.3 1.5 scatter_fusion.1
  137.6 3.1 %collective-permute-start.5 = (f32[1,5,8,128]{3,1,2,0:T(8,128)S(1)}, f32[1,5,8,128]{3,1,2,0:T(8,128)S(1)}, u32[]{:S(2)}, u32[]{:S(2)}) collective-permute-start(f32[1,5,8,128]{3,1,2,0:T(8,128)S(1)} %get-tuple-element.25), channel_id=1, source_target_pairs={{0,1},{1,2},{2,3},{4,5},{5,6},{6,7},{8,9},{9,10},{10,11},{12,13},{... | collective-permute-start | bytes 61448 | tf_op jit(solution)/shard_map/ppermute | solution.py:18
  140.7 1.3 collective-permute-start.4
  142.0 2.7 %collective-permute-done.4 = f32[1,5,8,128]{3,1,2,0:T(8,128)S(1)} collective-permute-done((f32[1,5,8,128]{3,1,2,0:T(8,128)S(1)}, f32[1,5,8,128]{3,1,2,0:T(8,128)S(1)}, u32[]{:S(2)}, u32[]{:S(2)}) %collective-permute-start.4) | collective-permute-done | bytes 20512 | tf_op jit(solution)/shard_map/ppermute | solution.py:21
  145.1 7.5 %all-gather.1 = f32[4,4,5120]{2,1,0:T(4,128)S(1)} all-gather(f32[1,4,5120]{2,1,0:T(4,128)S(1)} %reshape.599), channel_id=1, replica_groups=mesh['grid'=8,'sub'=4] {'sub'}, dimensions={0}, use_global_device_ids=true | all-gather | bytes 409600 | tf_op jit(solution)/shard_map/all_gather | solution.py:167
  153.6 3.2 %copy.295 = f32[8,5,16,128,2]{2,0,4,3,1:T(8,128)} copy(f32[8,5,16,128,2]{3,0,2,1,4:T(8,128)S(1)} %pad_maximum_fusion) | data formatting | bytes 1310720 | tf_op jit(solution)/shard_map/stack | solution.py:102
  156.8 3.2 %copy.296 = f32[1,8,5,16,256]{4,3,2,1,0:T(8,128)S(1)} copy(f32[1,8,5,16,256]{3,1,4,2,0:T(8,128)} %bitcast.408) | data formatting | bytes 1310720 | tf_op jit(solution)/shard_map/reshape | solution.py:105
  (193 shorter events, 44.1 us)
Async XLA Ops:
  6.5 105.8 %copy-start = (f32[5,5]{1,0:T(8,128)S(1)}, f32[5,5]{1,0:T(8,128)}, u32[]{:S(2)}) copy-start(f32[5,5]{1,0:T(8,128)} %param.15) | copy-start | bytes 304
  6.5 65.9 %all-gather.4.cloned.1.call-start = ((), (), s32[]{:S(2)}) async-start(), calls=%async_computation.2 | async-start | bytes 1638400 | tf_op jit(solution)/shard_map/all_gather | solution.py:132
  48.0 13.2 %copy-start.15 = (f32[1,1,3,64]{3,1,2,0:T(1,128)S(1)}, f32[1,1,3,64]{3,1,2,0:T(1,128)}, u32[]{:S(2)}) copy-start(f32[1,1,3,64]{3,1,2,0:T(1,128)} %param.17) | copy-start | bytes 2308
  61.0 15.3 %copy-start.8 = (s32[1024]{0:T(1024)}, s32[1024]{0:T(1024)S(1)}, u32[]{:S(2)}) copy-start(s32[1024]{0:T(1024)S(1)} %get-tuple-element.63) | copy-start | bytes 12292
  61.0 19.4 %copy-start.10 = (s32[1024]{0:T(1024)}, s32[1024]{0:T(1024)S(1)}, u32[]{:S(2)}) copy-start(s32[1024]{0:T(1024)S(1)} %get-tuple-element.65) | copy-start | bytes 12292
  61.1 21.4 %copy-start.9 = (s32[1024]{0:T(1024)}, s32[1024]{0:T(1024)S(1)}, u32[]{:S(2)}) copy-start(s32[1024]{0:T(1024)S(1)} %get-tuple-element.66) | copy-start | bytes 12292
  61.1 23.4 %copy-start.12 = (s32[1024]{0:T(1024)}, s32[1024]{0:T(1024)S(1)}, u32[]{:S(2)}) copy-start(s32[1024]{0:T(1024)S(1)} %get-tuple-element.67) | copy-start | bytes 12292
  61.1 25.4 %copy-start.11 = (s32[1024]{0:T(1024)}, s32[1024]{0:T(1024)S(1)}, u32[]{:S(2)}) copy-start(s32[1024]{0:T(1024)S(1)} %get-tuple-element.68) | copy-start | bytes 12292
  61.1 27.4 %copy-start.14 = (s32[1024]{0:T(1024)}, s32[1024]{0:T(1024)S(1)}, u32[]{:S(2)}) copy-start(s32[1024]{0:T(1024)S(1)} %get-tuple-element.69) | copy-start | bytes 12292
  61.1 29.5 %copy-start.13 = (s32[1024]{0:T(1024)}, s32[1024]{0:T(1024)S(1)}, u32[]{:S(2)}) copy-start(s32[1024]{0:T(1024)S(1)} %get-tuple-element.70) | copy-start | bytes 12292
  61.7 30.9 %copy-start.16 = (f32[64]{0:T(128)}, f32[64]{0:T(128)S(1)}, u32[]{:S(2)}) copy-start(f32[64]{0:T(128)S(1)} %get-tuple-element.44) | copy-start | bytes 772
  94.1 12.3 %all-to-all-start = ((f32[5,8,8]{2,0,1:T(8,128)}), f32[5,8,8]{2,0,1:T(8,128)}, u32[]{:S(2)}, u32[]{:S(2)}) async-start(f32[5,8,8]{2,0,1:T(8,128)} %copy.259), calls=%async_computation | async-start | bytes 65536 | tf_op jit(solution)/shard_map/all_to_all | solution.py:156
  100.2 12.1 %collective-permute-start.1 = (f32[1,5,8,128]{3,1,2,0:T(8,128)}, f32[1,5,8,128]{3,1,2,0:T(8,128)S(1)}, u32[]{:S(2)}, u32[]{:S(2)}) collective-permute-start(f32[1,5,8,128]{3,1,2,0:T(8,128)} %bitcast.403), channel_id=1, source_target_pairs={{0,1},{1,2},{2,3},{4,5},{5,6},{6,7},{8,9},{9,10},{10,11},{12,13},{... | collective-permute-start | bytes 61448 | tf_op jit(solution)/shard_map/ppermute | solution.py:18
  102.7 9.7 %collective-permute-start = (f32[1,5,8,128]{3,1,2,0:T(8,128)}, f32[1,5,8,128]{3,1,2,0:T(8,128)}, u32[]{:S(2)}, u32[]{:S(2)}) collective-permute-start(f32[1,5,8,128]{3,1,2,0:T(8,128)} %bitcast.404), channel_id=1, source_target_pairs={{1,0},{2,1},{3,2},{5,4},{6,5},{7,6},{9,8},{10,9},{11,10},{13,12},{... | collective-permute-start | bytes 61448 | tf_op jit(solution)/shard_map/ppermute | solution.py:21
  109.7 4.1 %collective-permute-start.3 = (f32[1,5,8,128]{3,1,2,0:T(8,128)S(1)}, f32[1,5,8,128]{3,1,2,0:T(8,128)S(1)}, u32[]{:S(2)}, u32[]{:S(2)}) collective-permute-start(f32[1,5,8,128]{3,1,2,0:T(8,128)S(1)} %get-tuple-element.31), channel_id=1, source_target_pairs={{0,1},{1,2},{2,3},{4,5},{5,6},{6,7},{8,9},{9,10},{10,11},{12,13},{... | collective-permute-start | bytes 61448 | tf_op jit(solution)/shard_map/ppermute | solution.py:18
  111.0 3.9 %collective-permute-start.2 = (f32[1,5,8,128]{3,1,2,0:T(8,128)S(1)}, f32[1,5,8,128]{3,1,2,0:T(8,128)S(1)}, u32[]{:S(2)}, u32[]{:S(2)}) collective-permute-start(f32[1,5,8,128]{3,1,2,0:T(8,128)S(1)} %get-tuple-element.30), channel_id=1, source_target_pairs={{1,0},{2,1},{3,2},{5,4},{6,5},{7,6},{9,8},{10,9},{11,10},{13,12},{... | collective-permute-start | bytes 61448 | tf_op jit(solution)/shard_map/ppermute | solution.py:21
  115.0 20.3 %copy-start.36 = (s32[64]{0:T(128)S(1)}, s32[64]{0:T(128)}, u32[]{:S(2)}) copy-start(s32[64]{0:T(128)} %copy-done.35) | copy-start | bytes 772
  118.7 26.0 %copy-start.3 = (f32[4,1,5,8,128]{4,3,2,1,0:T(8,128)S(1)}, f32[4,1,5,8,128]{4,3,2,1,0:T(8,128)}, u32[]{:S(2)}) copy-start(f32[4,1,5,8,128]{4,3,2,1,0:T(8,128)} %copy-done.2) | copy-start | bytes 245764
  118.7 26.0 %copy-start.5 = (f32[1,4,5,8,128]{4,3,2,1,0:T(8,128)S(1)}, f32[1,4,5,8,128]{4,3,2,1,0:T(8,128)}, u32[]{:S(2)}) copy-start(f32[1,4,5,8,128]{4,3,2,1,0:T(8,128)} %param.14) | copy-start | bytes 245764
  118.7 26.0 %copy-start.7 = (f32[4,5,8,128]{3,1,2,0:T(8,128)S(1)}, f32[4,5,8,128]{3,1,2,0:T(8,128)}, u32[]{:S(2)}) copy-start(f32[4,5,8,128]{3,1,2,0:T(8,128)} %copy-done.6) | copy-start | bytes 245764
  137.4 15.3 %copy-start.38 = (s32[8]{0:T(128)S(1)}, s32[8]{0:T(128)}, u32[]{:S(2)}) copy-start(s32[8]{0:T(128)} %get-tuple-element.6) | copy-start | bytes 100
  137.4 15.3 %copy-start.39 = (s32[8]{0:T(128)S(1)}, s32[8]{0:T(128)}, u32[]{:S(2)}) copy-start(s32[8]{0:T(128)} %get-tuple-element.7) | copy-start | bytes 100
  137.6 4.4 %collective-permute-start.5 = (f32[1,5,8,128]{3,1,2,0:T(8,128)S(1)}, f32[1,5,8,128]{3,1,2,0:T(8,128)S(1)}, u32[]{:S(2)}, u32[]{:S(2)}) collective-permute-start(f32[1,5,8,128]{3,1,2,0:T(8,128)S(1)} %get-tuple-element.25), channel_id=1, source_target_pairs={{0,1},{1,2},{2,3},{4,5},{5,6},{6,7},{8,9},{9,10},{10,11},{12,13},{... | collective-permute-start | bytes 61448 | tf_op jit(solution)/shard_map/ppermute | solution.py:18
  140.7 4.1 %collective-permute-start.4 = (f32[1,5,8,128]{3,1,2,0:T(8,128)S(1)}, f32[1,5,8,128]{3,1,2,0:T(8,128)S(1)}, u32[]{:S(2)}, u32[]{:S(2)}) collective-permute-start(f32[1,5,8,128]{3,1,2,0:T(8,128)S(1)} %get-tuple-element.24), channel_id=1, source_target_pairs={{1,0},{2,1},{3,2},{5,4},{6,5},{7,6},{9,8},{10,9},{11,10},{13,12},{... | collective-permute-start | bytes 61448 | tf_op jit(solution)/shard_map/ppermute | solution.py:21
  (27 other events, 194.0 us)
Sparse Core Ops, SparseCore 0:
  51.5 20.8 all-gather.3
where the time goes:
time: 169 us; the launch traced here: 168 us
  local copies, waits for them, and re-layouts  59.7 us (35%)
  other arithmetic  31.8 us (19%)
  blocking collectives  26.4 us (16%)
  starting transfers between devices  15.6 us (9%)
  waiting for transfers between devices  15.2 us (9%)
  between operations  15 us (9%)
  matrix products  4.06 us (2%)
    reduce_sum x2, other arithmetic, restrict_planes(): return 0.125 * jnp.sum(split_cells, axis=(-3, -1))  23.4 us
    gather x32, local copies, waits for them, and re-layouts, corner_values(): jnp.take_along_axis(flat_field, where_cells[..., None, :], axis=-1)  22.6 us
    unnamed x96, local copies, waits for them, and re-layouts  15.8 us
    all_to_all x1, blocking collectives, shards(): lax.all_to_all(blend(corners, offsets), 'grid', split_axis=1, concat_axis...  12.5 us
    all_gather x1, waiting for transfers between devices, shards(): lax.all_gather(contrib, 'sub', axis=0, tiled=True)  8.93 us
    all_gather x1, blocking collectives, shards(): shard_rows = lax.all_gather(correction, 'sub', axis=0, tiled=True)  7.46 us
    all_gather x1, blocking collectives, shards(): lax.all_gather(plane_ids, 'sub', axis=0, tiled=True)  6.41 us
    ppermute x3, starting transfers between devices, padded_2(): lax.ppermute(lax.slice_in_dim(block, block.shape[dim] - width, None, axis...  6.24 us
  transfers between devices with their start and end apart: 8, of which 4 were waited for; matrix products, arithmetic and copies ran while one was open for 6% of the time, Pallas kernels for 0%

commit v1 on v0

--- a/solution.py
+++ b/solution.py
@@ -1,6 +1,10 @@
+import functools
+
 import jax
 import jax.numpy as jnp
 from jax import lax
+from jax.experimental import pallas as pl
+from jax.experimental.pallas import tpu as pltpu
 from jax.sharding import PartitionSpec as P
 
 FRINGE = 8
@@ -176,6 +180,375 @@
     return (fine_solution[0] + prolonged)[None]
 
 
+FRINGE_LANES = 64
+BF16 = jnp.bfloat16
+F32 = jnp.float32
+HIGHEST = lax.Precision.HIGHEST
+VMEM = pl.BlockSpec(memory_space=pltpu.VMEM)
+SMEM = pl.BlockSpec(memory_space=pltpu.SMEM)
+
+
+def dot_exact(values, matrix):
+    high = values.astype(BF16)
+    rest = values - high.astype(F32)
+    middle = rest.astype(BF16)
+    low = (rest - middle.astype(F32)).astype(BF16)
+    total = jnp.dot(low, matrix, preferred_element_type=F32)
+    total = total + jnp.dot(middle, matrix, preferred_element_type=F32)
+    return total + jnp.dot(high, matrix, preferred_element_type=F32)
+
+
+def iota(shape, dim):
+    return lax.broadcasted_iota(jnp.int32, shape, dim)
+
+
+def restrict_kernel(
+    sizes, counts, residual, fine, diagonal, donors, offsets, receptors, ids, first, second, wide
+):
+    planes, variables, height, depth = sizes["coarse"]
+    blocks = sizes["blocks"]
+    grids = sizes["grids"]
+    slots = sizes["slots"]
+    grid_index = lax.axis_index("grid")
+    base = lax.axis_index("sub") * (planes * height * depth)
+    pair = jnp.where(
+        iota((2 * depth, depth), 0) // 2 == iota((2 * depth, depth), 1), 0.125, 0.0
+    ).astype(BF16)
+    count = blocks * variables
+    for source, target in ((fine, first), (residual, second)):
+        rows = source[0].reshape(count * 2 * height, 2 * depth)
+        wide[...] = dot_exact(rows, pair).reshape(count, 2 * height, depth)
+        target[0:count] = (
+            wide[:, pl.ds(0, height, stride=2), :] + wide[:, pl.ds(1, height, stride=2), :]
+        )
+    second[count : count + planes * variables] = diagonal[0].reshape(
+        planes * variables, height, depth
+    )
+    lane = iota((1, slots), 1)
+    allowed = jnp.zeros((1, slots), jnp.int32)
+    for g in range(grids):
+        allowed = jnp.where(lane // FRINGE == g, counts[g, grid_index], allowed)
+    cell = jnp.where(lane % FRINGE < allowed, receptors[0] + base, -1)
+    first[count] = jnp.zeros((height, depth), F32)
+    first[count, 0:1, 0:slots] = (donors[0] + base).astype(F32)
+    first[count, 1:4, 0:slots] = offsets[0, 0]
+    first[count, 4:5, 0:slots] = cell.astype(F32)
+    first[count, 5:6, 0:blocks] = ids[...].astype(F32)
+
+
+def gather_rows(parts, at, rows, slots):
+    for i, part in enumerate(parts):
+        rows[:, i * slots : (i + 1) * slots] = part[at, :, 0:slots]
+
+
+def split_cell(cell, height, depth):
+    return cell // (height * depth), cell // depth % height, cell % depth
+
+
+def interpolate(field, rows, sizes):
+    total, variables, height, depth = field.shape
+    count = rows.shape[1]
+    cell = rows[0:1, :].astype(jnp.int32)
+    plane, row, column = split_cell(cell, height, depth)
+    frac_x, frac_y, frac_z = rows[1:2, :], rows[2:3, :], rows[3:4, :]
+
+    def hats(shape, dim, start, frac):
+        at = iota(shape, dim)
+        return jnp.where(at == start, 1.0 - frac, 0.0) + jnp.where(at == start + 1, frac, 0.0)
+
+    weight_z = hats((depth, count), 0, column, frac_z)
+    weight_y = hats((height, count), 0, row, frac_y)
+    along_z = jnp.dot(
+        field.reshape(total * variables * height, depth),
+        weight_z,
+        precision=HIGHEST,
+        preferred_element_type=F32,
+    ).reshape(total, variables, height, count)
+    summed = None
+    for p in range(total):
+        weight_x = jnp.where(plane == p, 1.0 - frac_x, 0.0) + jnp.where(
+            plane + 1 == p, frac_x, 0.0
+        )
+        term = along_z[p] * (weight_x * weight_y)[None]
+        summed = term if summed is None else summed + term
+    return jnp.sum(summed, axis=1)
+
+
+def send_fringe(values, out, grids):
+    variables, count = values.shape
+    lane = iota((8, 128), 1)
+    padded = jnp.concatenate([values, jnp.zeros((8 - variables, count), F32)], axis=0)
+    left, right = padded[:, 0:128], padded[:, 128:256]
+    for h in range(grids):
+        at_left = pltpu.roll(left, (128 - 8 * h) % 128, 1)
+        at_right = pltpu.roll(right, (128 + 8 - 8 * h) % 128, 1)
+        out[h] = jnp.where(lane % 64 < 8, at_left, at_right)
+
+
+def receive_fringe(arrived, grids):
+    lane = iota((8, 128), 1)
+    left = jnp.zeros((8, 128), F32)
+    right = jnp.zeros((8, 128), F32)
+    for g in range(grids):
+        mine = lane % 64 // 8 == g
+        left = left + jnp.where(mine, pltpu.roll(arrived[g], 8 * g, 1), 0.0)
+        right = right + jnp.where(mine, pltpu.roll(arrived[g], (128 + 8 * g - 8) % 128, 1), 0.0)
+    return jnp.concatenate([left, right], axis=1)
+
+
+def spread(values, rows, shape):
+    total, variables, height, depth = shape
+    count = rows.shape[1]
+    cell = rows[4:5, :].astype(jnp.int32)
+    plane, row, column = split_cell(cell, height, depth)
+    onehot = jnp.where(
+        (iota((depth, count), 0) == column) & (cell >= 0), 1.0, 0.0
+    ).astype(BF16)
+    row_here = (iota((height, count), 0) == row) & (cell >= 0)
+    here = jnp.concatenate([jnp.where(row_here & (plane == p), 1.0, 0.0) for p in range(total)], 0)
+    contract = (((1,), (1,)), ((), ()))
+    mask = lax.dot_general(here.astype(BF16), onehot, contract, preferred_element_type=F32)
+    mask = mask.reshape(total, 1, height, depth)
+    stacked = here.reshape(total, 1, height, count) * values[:variables][None, :, None, :]
+    rows_in = stacked.reshape(total * variables * height, count)
+    high = rows_in.astype(BF16)
+    rest = rows_in - high.astype(F32)
+    middle = rest.astype(BF16)
+    low = (rest - middle.astype(F32)).astype(BF16)
+    field = lax.dot_general(low, onehot, contract, preferred_element_type=F32)
+    field = field + lax.dot_general(middle, onehot, contract, preferred_element_type=F32)
+    field = field + lax.dot_general(high, onehot, contract, preferred_element_type=F32)
+    return field.reshape(shape), mask
+
+
+def neighbour_sum(field):
+    total, variables, height, depth = field.shape
+    flat = field.reshape(total * variables, height, depth)
+    at_row = iota(flat.shape, 1)
+    at_column = iota(flat.shape, 2)
+    beside = jnp.where(at_row > 0, pltpu.roll(flat, 1, 1), 0.0)
+    beside = beside + jnp.where(at_row < height - 1, pltpu.roll(flat, height - 1, 1), 0.0)
+    beside = beside + jnp.where(at_column > 0, pltpu.roll(flat, 1, 2), 0.0)
+    beside = beside + jnp.where(at_column < depth - 1, pltpu.roll(flat, depth - 1, 2), 0.0)
+    beside = beside.reshape(field.shape)
+    empty = jnp.zeros((1, variables, height, depth), F32)
+    beside = beside + jnp.concatenate([empty, field[: total - 1]], axis=0)
+    return beside + jnp.concatenate([field[1:], empty], axis=0)
+
+
+def plane_numbers(parts, at, numbers, sems):
+    copies = [
+        pltpu.make_async_copy(part.at[at, 5:6, :], numbers.at[i : i + 1, :], sems.at[i])
+        for i, part in enumerate(parts)
+    ]
+    for copy in copies:
+        copy.start()
+    return copies
+
+
+def assemble(parts, numbers, blocks, out):
+    variables = out.shape[1]
+    out[...] = jnp.zeros(out.shape, F32)
+    for i, part in enumerate(parts):
+        for q in range(blocks):
+            coarse = numbers[i, q].astype(jnp.int32) // 2
+            out[pl.ds(coarse, 1)] += part[q * variables : (q + 1) * variables][None]
+
+
+def first_fringe_kernel(sizes, *refs):
+    subs = sizes["subs"]
+    parts = refs[:subs]
+    out, restricted, rows, numbers, sems = refs[subs:]
+    count = sizes["blocks"] * sizes["coarse"][1]
+    copies = plane_numbers(parts, count, numbers, sems)
+    gather_rows(parts, count, rows, sizes["slots"])
+    for copy in copies:
+        copy.wait()
+    assemble(parts, numbers, sizes["blocks"], restricted)
+    send_fringe(interpolate(restricted[...], rows, sizes), out, sizes["grids"])
+
+
+def second_fringe_kernel(sizes, *refs):
+    subs = sizes["subs"]
+    sub_index = lax.axis_index("sub")
+    planes, variables, height, depth = sizes["coarse"]
+    parts = refs[:subs]
+    seconds = refs[subs : 2 * subs]
+    restricted, arrived = refs[2 * subs : 2 * subs + 2]
+    out, field, residual, gain, rows, numbers, sems = refs[2 * subs + 2 :]
+    count = sizes["blocks"] * variables
+    copies = plane_numbers(parts, count, numbers, sems)
+    gather_rows(parts, count, rows, sizes["slots"])
+    values = receive_fringe(arrived, sizes["grids"])
+    shape = restricted.shape
+    landed, mask = spread(values, rows, shape)
+    for i, part in enumerate(seconds):
+        owner = (sub_index ^ sizes["order"][i]) * planes
+        own = part[count : count + planes * variables].reshape(planes, variables, height, depth)
+        gain[pl.ds(owner, planes)] = OMEGA / (6.0 + own)
+    for copy in copies:
+        copy.wait()
+    assemble(seconds, numbers, sizes["blocks"], residual)
+    start = restricted[...]
+    change = jnp.where(mask > 0.5, landed - start, 0.0)
+    update = gain[...] * (residual[...] + neighbour_sum(change))
+    now = start + jnp.where(mask > 0.5, change, update)
+    field[...] = now
+    send_fringe(interpolate(now, rows, sizes), out, sizes["grids"])
+
+
+def couple(coupling, field):
+    variables = field.shape[1]
+    outs = []
+    for v in range(variables):
+        summed = coupling[v, 0] * field[:, 0]
+        for x in range(1, variables):
+            summed = summed + coupling[v, x] * field[:, x]
+        outs.append(jnp.tanh(summed)[:, None])
+    return jnp.concatenate(outs, axis=1)
+
+
+def prolong_kernel(sizes, *refs):
+    subs = sizes["subs"]
+    planes, variables, height, depth = sizes["coarse"]
+    blocks = sizes["blocks"]
+    parts = refs[:subs]
+    coupling, ids, restricted, field, residual, gain, arrived, fine = refs[subs : subs + 8]
+    out, rows, padded, tall = refs[subs + 8 :]
+    count = blocks * variables
+    gather_rows(parts, count, rows, sizes["slots"])
+    values = receive_fringe(arrived, sizes["grids"])
+    landed, mask = spread(values, rows, restricted.shape)
+    start = restricted[...]
+    now = jnp.where(mask > 0.5, landed, field[...])
+    change = now - start
+    source = couple(coupling, start) - couple(coupling, now)
+    update = gain[...] * (residual[...] + neighbour_sum(change) + 2.0 * source)
+    correction = jnp.where(mask > 0.5, change, (1.0 - OMEGA) * change + update)
+    total = correction.shape[0]
+    padded[0:1] = jnp.zeros((1, variables, height, depth), F32)
+    padded[total + 1 : total + 2] = jnp.zeros((1, variables, height, depth), F32)
+    padded[1 : total + 1] = correction
+    at_row = iota((variables, height, depth), 1)
+    for q in range(blocks):
+        number = ids[0, q]
+        coarse = number // 2
+        along = 0.75 * padded[coarse + 1] + 0.25 * padded[coarse + 2 * (number % 2)]
+        below = jnp.where(at_row > 0, pltpu.roll(along, 1, 1), 0.0)
+        above = jnp.where(at_row < height - 1, pltpu.roll(along, height - 1, 1), 0.0)
+        here = slice(q * variables, (q + 1) * variables)
+        tall[here, pl.ds(0, height, stride=2), :] = 0.75 * along + 0.25 * below
+        tall[here, pl.ds(1, height, stride=2), :] = 0.75 * along + 0.25 * above
+    coarse_at = iota((depth, 2 * depth), 0)
+    fine_at = iota((depth, 2 * depth), 1)
+    beside = fine_at // 2 - 1 + 2 * (fine_at % 2)
+    widen = jnp.where(
+        coarse_at == fine_at // 2, 0.75, jnp.where(coarse_at == beside, 0.25, 0.0)
+    ).astype(BF16)
+    prolonged = dot_exact(tall[...].reshape(count * 2 * height, depth), widen)
+    out[...] = fine[...] + prolonged.reshape(fine.shape)
+
+
+def spread_over_sub(block, order_bits):
+    held = [block]
+    count = lax.axis_size("sub")
+    for bit in order_bits:
+        pairs = [(i, i ^ bit) for i in range(count)]
+        held = held + [lax.ppermute(one, "sub", pairs) for one in held]
+    return held
+
+
+def fast_shards(
+    fine_residual,
+    fine_solution,
+    plane_of_slot,
+    coarse_diagonal,
+    coupling,
+    donor_cells,
+    donor_offsets,
+    receptor_cells,
+    fringe_counts,
+):
+    subs = lax.axis_size("sub")
+    grids = lax.axis_size("grid")
+    coarse = coarse_diagonal.shape[1:]
+    planes, variables, height, depth = coarse
+    blocks = plane_of_slot.shape[1]
+    slots = donor_cells.shape[-1]
+    bits = [1 << k for k in reversed(range(subs.bit_length() - 1))]
+    order = [0]
+    for bit in bits:
+        order = order + [one ^ bit for one in order]
+    sizes = dict(
+        coarse=coarse, blocks=blocks, slots=slots, grids=grids, subs=subs, order=tuple(order)
+    )
+    count = blocks * variables
+    total = subs * planes
+    whole = (total, variables, height, depth)
+    params = pltpu.CompilerParams(vmem_limit_bytes=48 * 1024 * 1024)
+    tile = jax.ShapeDtypeStruct((grids, 8, 128), F32)
+    full = jax.ShapeDtypeStruct(whole, F32)
+    numbers = [pltpu.SMEM((subs, depth), F32), pltpu.SemaphoreType.DMA((subs,))]
+    rows = pltpu.VMEM((8, subs * slots), F32)
+
+    first, second = pl.pallas_call(
+        functools.partial(restrict_kernel, sizes),
+        out_shape=[
+            jax.ShapeDtypeStruct((count + 1, height, depth), F32),
+            jax.ShapeDtypeStruct((count + planes * variables, height, depth), F32),
+        ],
+        in_specs=[SMEM] + [VMEM] * 7,
+        out_specs=[VMEM] * 2,
+        scratch_shapes=[pltpu.VMEM((count, 2 * height, depth), F32)],
+        compiler_params=params,
+        name="restrict",
+    )(
+        fringe_counts,
+        fine_residual,
+        fine_solution,
+        coarse_diagonal,
+        donor_cells,
+        donor_offsets,
+        receptor_cells,
+        plane_of_slot,
+    )
+    firsts = spread_over_sub(first, bits)
+    out, restricted = pl.pallas_call(
+        functools.partial(first_fringe_kernel, sizes),
+        out_shape=[tile, full],
+        in_specs=[VMEM] * subs,
+        out_specs=[VMEM] * 2,
+        scratch_shapes=[rows] + numbers,
+        compiler_params=params,
+        name="first_fringe",
+    )(*firsts)
+    seconds = spread_over_sub(second, bits)
+    arrived = lax.all_to_all(out, "grid", 0, 0, tiled=True)
+    out, field, residual, gain = pl.pallas_call(
+        functools.partial(second_fringe_kernel, sizes),
+        out_shape=[tile, full, full, full],
+        in_specs=[VMEM] * (2 * subs + 2),
+        out_specs=[VMEM] * 4,
+        scratch_shapes=[rows] + numbers,
+        compiler_params=params,
+        name="second_fringe",
+    )(*firsts, *seconds, restricted, arrived)
+    arrived = lax.all_to_all(out, "grid", 0, 0, tiled=True)
+    return pl.pallas_call(
+        functools.partial(prolong_kernel, sizes),
+        out_shape=jax.ShapeDtypeStruct(fine_solution.shape, F32),
+        in_specs=[VMEM] * subs + [SMEM] * 2 + [VMEM] * 6,
+        out_specs=VMEM,
+        scratch_shapes=[
+            rows,
+            pltpu.VMEM((total + 2, variables, height, depth), F32),
+            pltpu.VMEM((count, 2 * height, depth), F32),
+        ],
+        compiler_params=params,
+        name="prolong",
+    )(*firsts, coupling, plane_of_slot, restricted, field, residual, gain, arrived, fine_solution)
+
+
 def solution(mesh):
     in_specs = (
         P("grid", "sub", None, None, None),
@@ -189,4 +562,6 @@
         P(),
     )
     out_specs = P("grid", "sub", None, None, None)
-    return jax.shard_map(shards, mesh=mesh, in_specs=in_specs, out_specs=out_specs, check_vma=False)
+    small = mesh.shape["sub"] == 4 and mesh.shape["grid"] * FRINGE == 64
+    body = fast_shards if small else shards
+    return jax.shard_map(body, mesh=mesh, in_specs=in_specs, out_specs=out_specs, check_vma=False)

time: 169 us -> 50.2 us (0.30)
  local copies, waits for them, and re-layouts: 59.7 us -> 5.16 us
  other arithmetic: 31.8 us -> 0 us
  blocking collectives: 26.4 us -> 9.06 us
  between operations: 15 us -> 0.05 us
  Pallas kernels: 0 us -> 8.8 us
  starting transfers between devices: 15.6 us -> 9.67 us
  matrix products: 4.06 us -> 0 us
  waiting for transfers between devices: 15.2 us -> 17 us
    reduce_sum x2 -> x0, other arithmetic: 23.4 us -> none  [restrict_planes(): return 0.125 * jnp.sum(split_cells, axis=(-3, -1))]
    gather x32 -> x0, local copies, waits for them, and re-layouts: 22.6 us -> none  [corner_values(): jnp.take_along_axis(flat_field, where_cells[..., None, :], axis=-1)]
    all_gather x2 -> x0, blocking collectives: 13.9 us -> none  [the longest x1 7.46 us: shards(): shard_rows = lax.all_gather(correction, 'sub', axis=0, tiled=True)]
    unnamed x96 -> x19, local copies, waits for them, and re-layouts: 15.8 us -> 5.16 us
    all_gather x1 -> x0, waiting for transfers between devices: 8.93 us -> none  [shards(): lax.all_gather(contrib, 'sub', axis=0, tiled=True)]
    pallas_call x0 -> x4, Pallas kernels: none -> 8.8 us  [the longest x1 3.15 us: fast_shards(): pl.pallas_call(functools.partial(prolong_kernel, sizes), out_shape=jax.Sh...]
    ppermute x6, starting transfers between devices: 10.1 us -> 3.63 us  [spread_over_sub(): held = held + [lax.ppermute(one, 'sub', pairs) for one in held]]
    ppermute x6, waiting for transfers between devices: 3.89 us -> 10.4 us  [spread_over_sub(): held = held + [lax.ppermute(one, 'sub', pairs) for one in held]]
  transfers between devices with their start and end apart: 8 -> 7, of which waited for: 4 -> 4; matrix products, arithmetic and copies ran while one was open for 6% -> 0% of each run, Pallas kernels for 0% -> 4%
where the time goes in v1:
time: 50.2 us; the launch traced here: 49.8 us
  waiting for transfers between devices  17 us (34%)
  starting transfers between devices  9.67 us (19%)
  blocking collectives  9.06 us (18%)
  Pallas kernels  8.8 us (18%)
  local copies, waits for them, and re-layouts  5.16 us (10%)
    ppermute x6, waiting for transfers between devices, spread_over_sub(): held = held + [lax.ppermute(one, 'sub', pairs) for one in held]  10.4 us
    all_to_all x1, blocking collectives, fast_shards(): arrived = lax.all_to_all(out, 'grid', 0, 0, tiled=True)  9.06 us
    all_to_all x1, waiting for transfers between devices, fast_shards(): arrived = lax.all_to_all(out, 'grid', 0, 0, tiled=True)  6.68 us
    all_to_all x1, starting transfers between devices, fast_shards(): arrived = lax.all_to_all(out, 'grid', 0, 0, tiled=True)  6.04 us
    unnamed x19, local copies, waits for them, and re-layouts  5.16 us
    ppermute x6, starting transfers between devices, spread_over_sub(): held = held + [lax.ppermute(one, 'sub', pairs) for one in held]  3.63 us
    pallas_call x1, Pallas kernels, fast_shards(): pl.pallas_call(functools.partial(prolong_kernel, sizes), out_shape=jax.Sh...  3.15 us
    pallas_call x1, Pallas kernels, fast_shards(): pl.pallas_call(functools.partial(first_fringe_kernel, sizes), out_shape=[...  2.2 us
  transfers between devices with their start and end apart: 7, of which 4 were waited for; matrix products, arithmetic and copies ran while one was open for 0% of the time, Pallas kernels for 4%

profile of v1, /device:TPU:0, one launch (start us, length us, event | category | flops | bytes accessed | tf_op | source)
XLA Modules:
  0.0 49.8 jit_solution(15123270148816877502)
XLA Ops:
  0.0 0.7 %copy.10.offsets = f32[1,1,3,64]{3,2,1,0:T(4,128)S(1)} copy(f32[1,1,3,64]{3,1,2,0:T(1,128)} %param.15) | data formatting | bytes 1536 | tf_op args[6]
  0.7 0.0 copy-start
  0.8 1.1 %copy-done = f32[1,8,5,16,256]{4,3,2,1,0:T(8,128)S(1)} copy-done((f32[1,8,5,16,256]{4,3,2,1,0:T(8,128)S(1)}, f32[1,8,5,16,256]{4,3,2,1,0:T(8,128)}, u32[]{:S(2)}) %copy-start) | copy-done | bytes 655384
  1.8 1.1 %copy-done.2 = f32[1,8,5,16,256]{4,3,2,1,0:T(8,128)S(1)} copy-done((f32[1,8,5,16,256]{4,3,2,1,0:T(8,128)S(1)}, f32[1,8,5,16,256]{4,3,2,1,0:T(8,128)}, u32[]{:S(2)}) %copy-start.2) | copy-done | bytes 655384
  2.9 0.9 %copy-done.3 = f32[1,4,5,8,128]{4,3,2,1,0:T(8,128)S(1)} copy-done((f32[1,4,5,8,128]{4,3,2,1,0:T(8,128)S(1)}, f32[1,4,5,8,128]{4,3,2,1,0:T(8,128)}, u32[]{:S(2)}) %copy-start.3) | copy-done | bytes 81944
  3.8 0.7 %copy-done.4 = s32[8,8]{1,0:T(8,128)S(1)} copy-done((s32[8,8]{1,0:T(8,128)S(1)}, s32[8,8]{1,0:T(8,128)}, u32[]{:S(2)}) %copy-start.4) | copy-done | bytes 280
  4.5 1.4 %restrict.1 = (f32[41,8,128]{2,1,0:T(8,128)S(1)}, f32[60,8,128]{2,1,0:T(8,128)S(1)}) custom-call(s32[8,8]{1,0:T(8,128)S(1)} %copy-done.4, f32[1,8,5,16,256]{4,3,2,1,0:T(8,128)S(1)} %copy-done.2, f32[1,8,5,16,256]{4,3,2,1,0:T(8,128)S(1)} %copy-done, f32[1,4,5,8,128]{4,3,2,1,0:T(8,128)S(1)} %copy-done.3, s32[1,1,64]{2,1,0:T(1,128)S(1)} %copy-done.7, ...), custom_call_target="tpu_custom_call" | custom-call | tf_op jit(solution)/shard_map/restrict/pallas_call | solution.py:494
  5.9 3.0 %collective-permute-start.3 = (f32[60,8,128]{2,1,0:T(8,128)S(1)}, f32[60,8,128]{2,1,0:T(8,128)S(1)}, u32[]{:S(2)}, u32[]{:S(2)}) collective-permute-start(f32[60,8,128]{2,1,0:T(8,128)S(1)} %get-tuple-element.15.refs_4_), channel_id=1, source_target_pairs={{0,2},{1,3},{2,0},{3,1},{4,6},{5,7},{6,4},{7,5},{8,10},{9,11},{10,... | collective-permute-start | bytes 737288 | tf_op jit(solution)/shard_map/ppermute | solution.py:457
  8.9 0.1 collective-permute-start
  9.0 0.0 collective-permute-start.4
  9.0 6.7 %collective-permute-done.3.refs_5_ = f32[60,8,128]{2,1,0:T(8,128)S(1)} collective-permute-done((f32[60,8,128]{2,1,0:T(8,128)S(1)}, f32[60,8,128]{2,1,0:T(8,128)S(1)}, u32[]{:S(2)}, u32[]{:S(2)}) %collective-permute-start.3) | collective-permute-done | bytes 245792 | tf_op jit(solution)/shard_map/ppermute | solution.py:457
  15.7 0.0 collective-permute-start.5
  15.7 0.5 %collective-permute-start.1 = (f32[41,8,128]{2,1,0:T(8,128)S(1)}, f32[41,8,128]{2,1,0:T(8,128)S(1)}, u32[]{:S(2)}, u32[]{:S(2)}) collective-permute-start(f32[41,8,128]{2,1,0:T(8,128)S(1)} %get-tuple-element.13.refs_0_), channel_id=1, source_target_pairs={{0,1},{1,0},{2,3},{3,2},{4,5},{5,4},{6,7},{7,6},{8,9},{9,8},{10,11... | collective-permute-start | bytes 503816 | tf_op jit(solution)/shard_map/ppermute | solution.py:457
  16.2 2.3 %collective-permute-done.refs_1_ = f32[41,8,128]{2,1,0:T(8,128)S(1)} collective-permute-done((f32[41,8,128]{2,1,0:T(8,128)S(1)}, f32[41,8,128]{2,1,0:T(8,128)S(1)}, u32[]{:S(2)}, u32[]{:S(2)}) %collective-permute-start) | collective-permute-done | bytes 167968 | tf_op jit(solution)/shard_map/ppermute | solution.py:457
  18.4 0.0 collective-permute-start.2
  18.4 1.4 %collective-permute-done.2.refs_3_ = f32[41,8,128]{2,1,0:T(8,128)S(1)} collective-permute-done((f32[41,8,128]{2,1,0:T(8,128)S(1)}, f32[41,8,128]{2,1,0:T(8,128)S(1)}, u32[]{:S(2)}, u32[]{:S(2)}) %collective-permute-start.2) | collective-permute-done | bytes 167968 | tf_op jit(solution)/shard_map/ppermute | solution.py:457
  19.8 2.2 %first_fringe.1 = (f32[8,8,128]{2,1,0:T(8,128)}, f32[16,5,8,128]{3,2,1,0:T(8,128)S(1)}) custom-call(f32[41,8,128]{2,1,0:T(8,128)S(1)} %get-tuple-element.13.refs_0_, f32[41,8,128]{2,1,0:T(8,128)S(1)} %collective-permute-done.refs_1_, f32[41,8,128]{2,1,0:T(8,128)S(1)} %collective-permute-done.1.refs_2_, f32[41,8,128]{2,1,0:T(8,128)S(1)} %collective-permute-done.2.refs_3_), custom_call_target="tpu_custom_call" | custom-call | tf_op jit(solution)/shard_map/first_fringe/pallas_call | solution.py:516
  22.1 6.0 %all-to-all-start = ((f32[8,8,128]{2,1,0:T(8,128)}), f32[8,8,128]{2,1,0:T(8,128)S(1)}, u32[]{:S(2)}, u32[]{:S(2)}) async-start(f32[8,8,128]{2,1,0:T(8,128)} %get-tuple-element.16), calls=%async_computation | async-start | bytes 65536 | tf_op jit(solution)/shard_map/all_to_all | solution.py:526
  28.1 0.0 collective-permute-done.4.refs_6_
  28.1 6.7 %all-to-all-done.refs_9_ = f32[8,8,128]{2,1,0:T(8,128)S(1)} async-done(((f32[8,8,128]{2,1,0:T(8,128)}), f32[8,8,128]{2,1,0:T(8,128)S(1)}, u32[]{:S(2)}, u32[]{:S(2)}) %all-to-all-start) | async-done | bytes 32800 | tf_op jit(solution)/shard_map/all_to_all | solution.py:526
  34.8 2.1 %second_fringe.1 = (f32[8,8,128]{2,1,0:T(8,128)S(1)}, f32[16,5,8,128]{3,2,1,0:T(8,128)S(1)}, f32[16,5,8,128]{3,2,1,0:T(8,128)S(1)}, f32[16,5,8,128]{3,2,1,0:T(8,128)S(1)}) custom-call(f32[41,8,128]{2,1,0:T(8,128)S(1)} %get-tuple-element.13.refs_0_, f32[41,8,128]{2,1,0:T(8,128)S(1)} %collective-permute-done.refs_1_, ...), custom_call_target="tpu_custom_call" | custom-call | tf_op jit(solution)/shard_map/second_fringe/pallas_call | solution.py:527
  36.9 9.1 %all_to_all.10.refs_10_ = f32[8,8,128]{2,1,0:T(8,128)S(1)} all-to-all(f32[8,8,128]{2,1,0:T(8,128)S(1)} %get-tuple-element.20), channel_id=1, replica_groups=mesh['grid'=8,'sub'=4] {'grid'}, dimensions={0} | all-to-all | bytes 65536 | tf_op jit(solution)/shard_map/all_to_all | solution.py:536
  46.0 0.7 %copy-done.5 = f32[5,5]{1,0:T(8,128)S(1)} copy-done((f32[5,5]{1,0:T(8,128)S(1)}, f32[5,5]{1,0:T(8,128)}, u32[]{:S(2)}) %copy-start.5) | copy-done | bytes 124
  46.6 3.2 %prolong.1 = f32[1,8,5,16,256]{4,3,2,1,0:T(8,128)} custom-call(f32[41,8,128]{2,1,0:T(8,128)S(1)} %get-tuple-element.13.refs_0_, f32[41,8,128]{2,1,0:T(8,128)S(1)} %collective-permute-done.refs_1_, f32[41,8,128]{2,1,0:T(8,128)S(1)} %collective-permute-done.1.refs_2_, f32[41,8,128]{2,1,0:T(8,128)S(1)} %collective-permute-done.2.refs_3_, f32[5,5]{1,0:T(8,128)S(1)} %copy-done.5, ...), custom_call_target="tpu_custom_call" | custom-call | tf_op jit(solution)/shard_map/prolong/pallas_call | solution.py:537
  (14 shorter events, 0.0 us)
Async XLA Ops:
  0.0 0.7 %copy-start.6 = (s32[1,8]{1,0:T(1,128)S(1)}, s32[1,8]{1,0:T(1,128)}, u32[]{:S(2)}) copy-start(s32[1,8]{1,0:T(1,128)} %refs_5_.1) | copy-start | bytes 100
  0.0 0.7 %copy-start.8 = (s32[1,1,64]{2,1,0:T(1,128)S(1)}, s32[1,1,64]{2,1,0:T(1,128)}, u32[]{:S(2)}) copy-start(s32[1,1,64]{2,1,0:T(1,128)} %receptors.1) | copy-start | bytes 772
  0.0 0.7 %copy-start.7 = (s32[1,1,64]{2,1,0:T(1,128)S(1)}, s32[1,1,64]{2,1,0:T(1,128)}, u32[]{:S(2)}) copy-start(s32[1,1,64]{2,1,0:T(1,128)} %donors.1) | copy-start | bytes 772
  0.7 1.1 %copy-start = (f32[1,8,5,16,256]{4,3,2,1,0:T(8,128)S(1)}, f32[1,8,5,16,256]{4,3,2,1,0:T(8,128)}, u32[]{:S(2)}) copy-start(f32[1,8,5,16,256]{4,3,2,1,0:T(8,128)} %refs_11_.1) | copy-start | bytes 1966084
  1.8 1.1 %copy-start.2 = (f32[1,8,5,16,256]{4,3,2,1,0:T(8,128)S(1)}, f32[1,8,5,16,256]{4,3,2,1,0:T(8,128)}, u32[]{:S(2)}) copy-start(f32[1,8,5,16,256]{4,3,2,1,0:T(8,128)} %residual.1) | copy-start | bytes 1966084
  2.9 0.9 %copy-start.3 = (f32[1,4,5,8,128]{4,3,2,1,0:T(8,128)S(1)}, f32[1,4,5,8,128]{4,3,2,1,0:T(8,128)}, u32[]{:S(2)}) copy-start(f32[1,4,5,8,128]{4,3,2,1,0:T(8,128)} %diagonal.1) | copy-start | bytes 245764
  3.8 0.7 %copy-start.4 = (s32[8,8]{1,0:T(8,128)S(1)}, s32[8,8]{1,0:T(8,128)}, u32[]{:S(2)}) copy-start(s32[8,8]{1,0:T(8,128)} %counts.1) | copy-start | bytes 772
  5.9 9.8 %collective-permute-start.3 = (f32[60,8,128]{2,1,0:T(8,128)S(1)}, f32[60,8,128]{2,1,0:T(8,128)S(1)}, u32[]{:S(2)}, u32[]{:S(2)}) collective-permute-start(f32[60,8,128]{2,1,0:T(8,128)S(1)} %get-tuple-element.15.refs_4_), channel_id=1, source_target_pairs={{0,2},{1,3},{2,0},{3,1},{4,6},{5,7},{6,4},{7,5},{8,10},{9,11},{10,... | collective-permute-start | bytes 737288 | tf_op jit(solution)/shard_map/ppermute | solution.py:457
  8.9 9.6 %collective-permute-start = (f32[41,8,128]{2,1,0:T(8,128)S(1)}, f32[41,8,128]{2,1,0:T(8,128)S(1)}, u32[]{:S(2)}, u32[]{:S(2)}) collective-permute-start(f32[41,8,128]{2,1,0:T(8,128)S(1)} %get-tuple-element.13.refs_0_), channel_id=1, source_target_pairs={{0,2},{1,3},{2,0},{3,1},{4,6},{5,7},{6,4},{7,5},{8,10},{9,11},{10,... | collective-permute-start | bytes 503816 | tf_op jit(solution)/shard_map/ppermute | solution.py:457
  9.0 19.1 %collective-permute-start.4 = (f32[60,8,128]{2,1,0:T(8,128)S(1)}, f32[60,8,128]{2,1,0:T(8,128)S(1)}, u32[]{:S(2)}, u32[]{:S(2)}) collective-permute-start(f32[60,8,128]{2,1,0:T(8,128)S(1)} %get-tuple-element.15.refs_4_), channel_id=1, source_target_pairs={{0,1},{1,0},{2,3},{3,2},{4,5},{5,4},{6,7},{7,6},{8,9},{9,8},{10,11... | collective-permute-start | bytes 737288 | tf_op jit(solution)/shard_map/ppermute | solution.py:457
  15.7 19.1 %collective-permute-start.5 = (f32[60,8,128]{2,1,0:T(8,128)S(1)}, f32[60,8,128]{2,1,0:T(8,128)S(1)}, u32[]{:S(2)}, u32[]{:S(2)}) collective-permute-start(f32[60,8,128]{2,1,0:T(8,128)S(1)} %collective-permute-done.3.refs_5_), channel_id=1, source_target_pairs={{0,1},{1,0},{2,3},{3,2},{4,5},{5,4},{6,7},{7,6},{8,9},{9,8},{10,11... | collective-permute-start | bytes 737288 | tf_op jit(solution)/shard_map/ppermute | solution.py:457
  15.7 2.8 %collective-permute-start.1 = (f32[41,8,128]{2,1,0:T(8,128)S(1)}, f32[41,8,128]{2,1,0:T(8,128)S(1)}, u32[]{:S(2)}, u32[]{:S(2)}) collective-permute-start(f32[41,8,128]{2,1,0:T(8,128)S(1)} %get-tuple-element.13.refs_0_), channel_id=1, source_target_pairs={{0,1},{1,0},{2,3},{3,2},{4,5},{5,4},{6,7},{7,6},{8,9},{9,8},{10,11... | collective-permute-start | bytes 503816 | tf_op jit(solution)/shard_map/ppermute | solution.py:457
  18.4 1.4 %collective-permute-start.2 = (f32[41,8,128]{2,1,0:T(8,128)S(1)}, f32[41,8,128]{2,1,0:T(8,128)S(1)}, u32[]{:S(2)}, u32[]{:S(2)}) collective-permute-start(f32[41,8,128]{2,1,0:T(8,128)S(1)} %collective-permute-done.refs_1_), channel_id=1, source_target_pairs={{0,1},{1,0},{2,3},{3,2},{4,5},{5,4},{6,7},{7,6},{8,9},{9,8},{10,11... | collective-permute-start | bytes 503816 | tf_op jit(solution)/shard_map/ppermute | solution.py:457
  22.1 12.7 %all-to-all-start = ((f32[8,8,128]{2,1,0:T(8,128)}), f32[8,8,128]{2,1,0:T(8,128)S(1)}, u32[]{:S(2)}, u32[]{:S(2)}) async-start(f32[8,8,128]{2,1,0:T(8,128)} %get-tuple-element.16), calls=%async_computation | async-start | bytes 65536 | tf_op jit(solution)/shard_map/all_to_all | solution.py:526
  34.8 11.2 %copy-start.1 = (f32[1,8,5,16,256]{4,3,2,1,0:T(8,128)S(1)}, f32[1,8,5,16,256]{4,3,2,1,0:T(8,128)}, u32[]{:S(2)}) copy-start(f32[1,8,5,16,256]{4,3,2,1,0:T(8,128)} %refs_11_.1) | copy-start | bytes 1966084
  45.9 0.7 %copy-start.5 = (f32[5,5]{1,0:T(8,128)S(1)}, f32[5,5]{1,0:T(8,128)}, u32[]{:S(2)}) copy-start(f32[5,5]{1,0:T(8,128)} %refs_4_.1) | copy-start | bytes 304

commit v2 on v0

--- a/solution.py
+++ b/solution.py
@@ -1,6 +1,10 @@
+import functools
+
 import jax
 import jax.numpy as jnp
 from jax import lax
+from jax.experimental import pallas as pl
+from jax.experimental.pallas import tpu as pltpu
 from jax.sharding import PartitionSpec as P
 
 FRINGE = 8
@@ -176,6 +180,540 @@
     return (fine_solution[0] + prolonged)[None]
 
 
+BF16 = jnp.bfloat16
+F32 = jnp.float32
+HIGHEST = lax.Precision.HIGHEST
+VMEM = pl.BlockSpec(memory_space=pltpu.VMEM)
+SMEM = pl.BlockSpec(memory_space=pltpu.SMEM)
+LANES = 128
+ROW = 256
+PLANE = 4096
+NOWHERE = -(1 << 20)
+
+
+def pieces(values):
+    high = values.astype(BF16).astype(F32)
+    middle = (values - high).astype(BF16).astype(F32)
+    low = (values - high - middle).astype(BF16).astype(F32)
+    return high, middle, low
+
+
+def dot_exact(values, matrix, contract=(((1,), (0,)), ((), ()))):
+    total = None
+    for piece in reversed(pieces(values)):
+        term = lax.dot_general(piece.astype(BF16), matrix, contract, preferred_element_type=F32)
+        total = term if total is None else total + term
+    return total
+
+
+def iota(shape, dim):
+    return lax.broadcasted_iota(jnp.int32, shape, dim)
+
+
+def split_cell(cell, height, depth):
+    return cell // (height * depth), cell // depth % height, cell % depth
+
+
+def neighbour_sum(field):
+    total, variables, height, depth = field.shape
+    flat = field.reshape(total * variables, height, depth)
+    at_row = iota(flat.shape, 1)
+    at_column = iota(flat.shape, 2)
+    beside = jnp.where(at_row > 0, pltpu.roll(flat, 1, 1), 0.0)
+    beside = beside + jnp.where(at_row < height - 1, pltpu.roll(flat, height - 1, 1), 0.0)
+    beside = beside + jnp.where(at_column > 0, pltpu.roll(flat, 1, 2), 0.0)
+    beside = beside + jnp.where(at_column < depth - 1, pltpu.roll(flat, depth - 1, 2), 0.0)
+    beside = beside.reshape(field.shape)
+    empty = jnp.zeros((1, variables, height, depth), F32)
+    beside = beside + jnp.concatenate([empty, field[: total - 1]], axis=0)
+    return beside + jnp.concatenate([field[1:], empty], axis=0)
+
+
+def live_cells(counts, grid_index, grids, receptors, base):
+    lane = iota(receptors.shape, 1)
+    allowed = jnp.zeros(receptors.shape, jnp.int32)
+    for g in range(grids):
+        allowed = jnp.where(lane // FRINGE == g, counts[g, grid_index], allowed)
+    return jnp.where(lane % FRINGE < allowed, receptors + base, -1)
+
+
+def receptor_mask(cell, total, height, depth):
+    count = cell.shape[1]
+    plane, row, column = split_cell(cell, height, depth)
+    onehot = jnp.where(iota((depth, count), 0) == column, 1.0, 0.0).astype(BF16)
+    row_here = (iota((height, count), 0) == row) & (cell >= 0)
+    here = jnp.concatenate([jnp.where(row_here & (plane == p), 1.0, 0.0) for p in range(total)], 0)
+    contract = (((1,), (1,)), ((), ()))
+    mask = lax.dot_general(here.astype(BF16), onehot, contract, preferred_element_type=F32)
+    return mask.reshape(total, 1, height, depth), here, onehot
+
+
+def pack_kernel(sizes, counts, diagonal, donors, offsets, receptors, out):
+    planes, variables, height, depth = sizes["coarse"]
+    slots = sizes["slots"]
+    base = lax.axis_index("sub") * (planes * height * depth)
+    grid_index = lax.axis_index("grid")
+    count = planes * variables
+    out[0:count] = diagonal[0].reshape(count, height, depth)
+    cell = live_cells(counts, grid_index, sizes["grids"], receptors[0], base)
+    out[count] = jnp.zeros((height, depth), F32)
+    out[count, 0:1, 0:slots] = (donors[0] + base).astype(F32)
+    out[count, 1:4, 0:slots] = offsets[0, 0]
+    out[count, 4:5, 0:slots] = cell.astype(F32)
+
+
+def restrict_kernel(sizes, residual, fine, ids, out, wide):
+    planes, variables, height, depth = sizes["coarse"]
+    blocks = sizes["blocks"]
+    count = blocks * variables
+    pair = jnp.where(
+        iota((2 * depth, depth), 0) // 2 == iota((2 * depth, depth), 1), 0.125, 0.0
+    ).astype(BF16)
+    for at, source in ((0, fine), (count, residual)):
+        rows = source[0].reshape(count * 2 * height, 2 * depth)
+        wide[...] = dot_exact(rows, pair).reshape(count, 2 * height, depth)
+        out[at : at + count] = (
+            wide[:, pl.ds(0, height, stride=2), :] + wide[:, pl.ds(1, height, stride=2), :]
+        )
+    out[2 * count] = jnp.zeros((height, depth), F32)
+    out[2 * count, 0:1, 0:blocks] = ids[...].astype(F32)
+
+
+def corner_kernel(sizes, counts, diagonal, donors, offsets, receptors, out):
+    planes, variables, height, depth = sizes["coarse"]
+    slots, grids = sizes["slots"], sizes["grids"]
+    sub_index = lax.axis_index("sub")
+    cell = live_cells(counts, lax.axis_index("grid"), grids, receptors[0], 0)
+    mask, _, _ = receptor_mask(cell, planes, height, depth)
+    gain = OMEGA / (6.0 + diagonal[0])
+    fields = jnp.concatenate([gain, 1.0 - mask], axis=1)
+    twice = jnp.concatenate([donors[0], donors[0]], axis=1)
+    step_z = iota(twice.shape, 1) // slots
+    plane, row, column = split_cell(twice, height, depth)
+    onehot = jnp.where(iota((depth, LANES), 0) == column + step_z, 1.0, 0.0).astype(BF16)
+    count = planes * (variables + 1) * height
+    at_column = dot_exact(fields.reshape(count, depth), onehot)
+    at_column = at_column.reshape(planes, variables + 1, height, LANES)
+    both = jnp.concatenate([offsets[0, 0], offsets[0, 0]], axis=1)
+    weight_z = jnp.where(step_z == 1, both[2:3], 1.0 - both[2:3])
+    at_row = iota((height, LANES), 0)
+    tiles = []
+    for step_x in (0, 1):
+        weight_x = both[0:1] if step_x else 1.0 - both[0:1]
+        by_plane = None
+        for p in range(planes):
+            term = jnp.where(plane + step_x == p, at_column[p], 0.0)
+            by_plane = term if by_plane is None else by_plane + term
+        for step_y in (0, 1):
+            weight_y = both[1:2] if step_y else 1.0 - both[1:2]
+            here = jnp.where(at_row == row + step_y, 1.0, 0.0)
+            found = jnp.sum(by_plane * here[None], axis=1)
+            weight = weight_x * weight_y * weight_z
+            number = (
+                (plane + step_x + sub_index * planes) * PLANE
+                + (row + step_y) * ROW
+                + column
+                + step_z
+            ).astype(F32)
+            scaled = weight * found[:variables] * found[variables : variables + 1]
+            tiles.append(jnp.concatenate([weight, weight, scaled, number], axis=0))
+    lane = iota((8, LANES), 1)
+    sublane = iota((8, LANES), 0)
+    target_plane, target_row, target_column = split_cell(cell, height, depth)
+    number = (target_plane + sub_index * planes) * PLANE + target_row * ROW + target_column
+    number = jnp.where(cell >= 0, number, NOWHERE).astype(F32)
+    number = jnp.broadcast_to(jnp.concatenate([number, number], axis=1), (8, LANES))
+    half = slots // 2
+    moved = jnp.where(sublane == 2, pltpu.roll(number, half, 1), number)
+    targets = (sublane == 2) | (sublane == 3)
+    targets = targets & (lane >= half) & (lane < slots)
+    for h in range(grids):
+        tile = jnp.zeros((8, LANES), F32)
+        for c in range(8):
+            shift = (64 + 8 * c - (c % 2) * 64 - 8 * h) % LANES
+            tile = jnp.where(lane // 8 == 8 + c, pltpu.roll(tiles[c // 2], shift, 1), tile)
+        weight = pltpu.roll(jnp.broadcast_to(tile[0:1], (8, LANES)), 64, 1)
+        tile = jnp.where((sublane == 7) & (lane < 64), weight, tile)
+        out[h] = jnp.where(targets, moved, tile)
+
+
+def hats(shape, dim, start, frac):
+    at = iota(shape, dim)
+    return jnp.where(at == start, 1.0 - frac, 0.0) + jnp.where(at == start + 1, frac, 0.0)
+
+
+def interpolate(field, rows):
+    total, variables, height, depth = field.shape
+    count = rows.shape[1]
+    plane, row, column = split_cell(rows[0:1, :].astype(jnp.int32), height, depth)
+    frac_x, frac_y, frac_z = rows[1:2, :], rows[2:3, :], rows[3:4, :]
+    weight_z = hats((depth, count), 0, column, frac_z)
+    weight_y = hats((height, count), 0, row, frac_y)
+    along_z = jnp.dot(
+        field.reshape(total * variables * height, depth),
+        weight_z,
+        precision=HIGHEST,
+        preferred_element_type=F32,
+    ).reshape(total, variables, height, count)
+    summed = None
+    for p in range(total):
+        weight_x = jnp.where(plane == p, 1.0 - frac_x, 0.0) + jnp.where(
+            plane + 1 == p, frac_x, 0.0
+        )
+        term = along_z[p] * (weight_x * weight_y)[None]
+        summed = term if summed is None else summed + term
+    return jnp.sum(summed, axis=1)
+
+
+def partial_kernel(sizes, *refs):
+    subs, grids, slots, blocks = sizes["subs"], sizes["grids"], sizes["slots"], sizes["blocks"]
+    planes, variables, height, depth = sizes["coarse"]
+    parts = refs[:subs]
+    ids, own, corners = refs[subs : subs + 3]
+    out, gain, mask_out, rows, stage, both = refs[subs + 3 :]
+    total = subs * planes
+    sub_index = lax.axis_index("sub")
+    count = planes * variables
+    for i, part in enumerate(parts):
+        owner = sub_index ^ sizes["order"][i]
+        stage[owner] = part[count]
+        diagonal = part[0:count].reshape(planes, variables, height, depth)
+        gain[pl.ds(owner * planes, planes)] = OMEGA / (6.0 + diagonal)
+    for j in range(subs):
+        rows[:, j * slots : (j + 1) * slots] = stage[j, :, 0:slots]
+    both[...] = jnp.zeros(both.shape, F32)
+    fine_count = blocks * variables
+    for q in range(blocks):
+        coarse = ids[0, q] // 2
+        for k in range(2):
+            at = k * fine_count + q * variables
+            here = pl.ds(k * variables, variables)
+            both[pl.ds(coarse, 1), here] += own[at : at + variables][None]
+    mask, _, _ = receptor_mask(rows[4:5, :].astype(jnp.int32), total, height, depth)
+    mask_out[...] = mask
+    restricted = both[:, 0:variables]
+    residual = both[:, variables:]
+    wet = mask > 0.5
+    beside = neighbour_sum(jnp.where(wet, restricted, 0.0))
+    swept = jnp.where(wet, 0.0, restricted + gain[...] * (residual - beside))
+    values = interpolate(jnp.concatenate([restricted, swept], axis=1), rows)
+    first, second = values[:variables], values[variables:]
+    top = jnp.concatenate(
+        [first[v : v + 1, k * LANES : (k + 1) * LANES] for v in range(4) for k in range(2)], axis=0
+    )
+    empty = jnp.zeros((1, LANES), F32)
+    last = [first[4:5, k * LANES : (k + 1) * LANES] for k in range(2)]
+    low = jnp.concatenate(last + [second[:, 0:LANES], empty], axis=0)
+    high = jnp.concatenate([empty, empty, second[:, LANES:], empty], axis=0)
+    lane = iota((8, LANES), 1)
+    sublane = iota((8, LANES), 0)
+    values_at = (sublane >= 2) & (sublane < 7)
+    for h in range(grids):
+        tile = jnp.where(sublane < 2, low, corners[h])
+        for s in range(subs):
+            source = low if s < 2 else high
+            moved = pltpu.roll(source, (8 * s - 8 * h - 64 * (s % 2)) % LANES, 1)
+            tile = jnp.where(values_at & (lane // 8 == s), moved, tile)
+        for s in range(subs):
+            out[h * subs + s, 0:8] = top
+            out[h * subs + s, 8:16] = tile
+
+
+def assemble_kernel(sizes, *refs):
+    subs, blocks = sizes["subs"], sizes["blocks"]
+    planes, variables, height, depth = sizes["coarse"]
+    parts = refs[:subs]
+    coupling, restricted, residual, source, numbers, sems = refs[subs:]
+    count = blocks * variables
+    copies = [
+        pltpu.make_async_copy(part.at[2 * count, 0:1, :], numbers.at[i : i + 1, :], sems.at[i])
+        for i, part in enumerate(parts)
+    ]
+    for copy in copies:
+        copy.start()
+    restricted[...] = jnp.zeros(restricted.shape, F32)
+    residual[...] = jnp.zeros(residual.shape, F32)
+    for copy in copies:
+        copy.wait()
+    for i, part in enumerate(parts):
+        for q in range(blocks):
+            coarse = pl.ds(numbers[i, q].astype(jnp.int32) // 2, 1)
+            at = q * variables
+            restricted[coarse] += part[at : at + variables][None]
+            residual[coarse] += part[count + at : count + at + variables][None]
+    source[...] = couple(coupling, restricted[...])
+
+
+def couple(coupling, field):
+    variables = field.shape[1]
+    outs = []
+    for v in range(variables):
+        summed = coupling[v, 0] * field[:, 0]
+        for x in range(1, variables):
+            summed = summed + coupling[v, x] * field[:, x]
+        outs.append(jnp.tanh(summed)[:, None])
+    return jnp.concatenate(outs, axis=1)
+
+
+def fringe_values(sizes, arrived, landing):
+    subs, grids = sizes["subs"], sizes["grids"]
+    lane = iota((8, LANES), 1)
+    sublane = iota((8, LANES), 0)
+    group = lane % 64 // 8
+    firsts = []
+    for g in range(grids):
+        top = arrived[g * subs, 0:8]
+        last = arrived[g * subs, 8:16]
+        for s in range(1, subs):
+            top = top + arrived[g * subs + s, 0:8]
+            last = last + arrived[g * subs + s, 8:16]
+        halves = []
+        for k in range(2):
+            rows = [top[2 * v + k : 2 * v + k + 1] for v in range(4)] + [last[k : k + 1]]
+            halves.append(jnp.concatenate(rows + [jnp.zeros((3, LANES), F32)], axis=0))
+        firsts.append((halves, last))
+    for g in range(grids):
+        for k in range(2):
+            sent = jnp.zeros((8, LANES), F32)
+            for other in range(grids):
+                moved = pltpu.roll(firsts[other][0][k], (8 * other - 8 * g) % LANES, 1)
+                sent = jnp.where(group == other, moved, sent)
+            landing[g, :, k * LANES : (k + 1) * LANES] = sent
+    targets, numbers, scales, weights = [], [], [], []
+    for g in range(grids):
+        tiles = [arrived[g * subs + s, 8:16] for s in range(subs)]
+        target, scale, weight = [], [], []
+        for k in range(2):
+            one, two = tiles[2 * k], tiles[2 * k + 1]
+            scale.append(jnp.where(lane < 64, pltpu.roll(one, 64, 1), two))
+            weight.append(jnp.where(lane < 64, one, pltpu.roll(two, 64, 1))[7:8])
+            left = jnp.where(lane < 32, pltpu.roll(one, 96, 1)[2:3], one[3:4])
+            right = jnp.where(lane < 96, pltpu.roll(two, 32, 1)[2:3], pltpu.roll(two, 64, 1)[3:4])
+            target.append(jnp.where(lane < 64, left, right)[0:1])
+        targets.append(jnp.concatenate(target, axis=1))
+        scales.append(jnp.concatenate(scale, axis=1))
+        weights.append(jnp.concatenate(weight, axis=1))
+    columns = jnp.concatenate(targets, axis=0).T
+    total = [jnp.zeros((8, LANES), F32), jnp.zeros((8, LANES), F32)]
+    for g in range(grids):
+        apart = jnp.abs(columns[:, g : g + 1] - scales[g][7:8])
+        near = (apart == 1.0) | (apart == float(ROW)) | (apart == float(PLANE))
+        beside = jnp.where(near, 1.0, 0.0).astype(BF16)
+        equal = jnp.where(apart == 0.0, 1.0, 0.0).astype(BF16)
+        stacked = jnp.concatenate(pieces(landing[g]), axis=0).astype(BF16)
+        by_side = jnp.dot(stacked, beside, preferred_element_type=F32)
+        by_self = jnp.dot(stacked, equal, preferred_element_type=F32)
+        by_side = by_side[16:24] + by_side[8:16] + by_side[0:8]
+        by_self = by_self[16:24] + by_self[8:16] + by_self[0:8]
+        for k in range(2):
+            here = slice(k * LANES, (k + 1) * LANES)
+            scale = pltpu.roll(scales[g][:, here], 6, 0)
+            value = by_side[:, here] * scale + by_self[:, here] * weights[g][:, here]
+            for step in (32, 16, 8):
+                value = value + pltpu.roll(value, LANES - step, 1)
+            known = pltpu.roll(firsts[g][1], 6, 0)
+            for s in range(2):
+                mine = (group == g) & (lane // 64 == s)
+                moved = pltpu.roll(value, 8 * g, 1)
+                base = pltpu.roll(known, (64 * s + 8 * g - 16 * k - 8 * s) % LANES, 1)
+                total[k] = jnp.where(mine, moved + base, total[k])
+    return landing[lax.axis_index("grid")], jnp.concatenate(total, axis=1)
+
+
+def finish_kernel(sizes, *refs):
+    subs = sizes["subs"]
+    planes, variables, height, depth = sizes["coarse"]
+    blocks = sizes["blocks"]
+    parts = refs[:subs]
+    coupling, ids, arrived, restricted, residual, source, gain, mask = refs[subs : subs + 8]
+    fine, out, landing, stage, rows, padded, tall = refs[subs + 8 :]
+    total = subs * planes
+    slots = sizes["slots"]
+    count = blocks * variables
+    sub_index = lax.axis_index("sub")
+    for i, part in enumerate(parts):
+        stage[sub_index ^ sizes["order"][i]] = part[planes * variables]
+    for j in range(subs):
+        rows[:, j * slots : (j + 1) * slots] = stage[j, :, 0:slots]
+    first, second = fringe_values(sizes, arrived, landing)
+    cell = rows[4:5, :].astype(jnp.int32)
+    _, here, onehot = receptor_mask(cell, total, height, depth)
+    lanes = subs * slots
+    values = jnp.concatenate([first[:variables], second[:variables]], axis=0)
+    stacked = here.reshape(total, 1, height, lanes) * values[None, :, None, :]
+    landed = dot_exact(
+        stacked.reshape(total * 2 * variables * height, lanes),
+        onehot,
+        (((1,), (1,)), ((), ())),
+    ).reshape(total, 2 * variables, height, depth)
+    wet = mask[...] > 0.5
+    start = restricted[...]
+    scale = gain[...]
+    rest = residual[...]
+    change = jnp.where(wet, landed[:, :variables] - start, 0.0)
+    update = scale * (rest + neighbour_sum(change))
+    change = jnp.where(wet, landed[:, variables:] - start, update)
+    apart = source[...] - couple(coupling, start + change)
+    update = scale * (rest + neighbour_sum(change) + 2.0 * apart)
+    correction = jnp.where(wet, change, (1.0 - OMEGA) * change + update)
+    padded[0:1] = jnp.zeros((1, variables, height, depth), F32)
+    padded[total + 1 : total + 2] = jnp.zeros((1, variables, height, depth), F32)
+    padded[1 : total + 1] = correction
+    at_row = iota((variables, height, depth), 1)
+    for q in range(blocks):
+        number = ids[0, q]
+        coarse = number // 2
+        along = 0.75 * padded[coarse + 1] + 0.25 * padded[coarse + 2 * (number % 2)]
+        below = jnp.where(at_row > 0, pltpu.roll(along, 1, 1), 0.0)
+        above = jnp.where(at_row < height - 1, pltpu.roll(along, height - 1, 1), 0.0)
+        block = slice(q * variables, (q + 1) * variables)
+        tall[block, pl.ds(0, height, stride=2), :] = 0.75 * along + 0.25 * below
+        tall[block, pl.ds(1, height, stride=2), :] = 0.75 * along + 0.25 * above
+    coarse_at = iota((depth, 2 * depth), 0)
+    fine_at = iota((depth, 2 * depth), 1)
+    beside = fine_at // 2 - 1 + 2 * (fine_at % 2)
+    widen = jnp.where(
+        coarse_at == fine_at // 2, 0.75, jnp.where(coarse_at == beside, 0.25, 0.0)
+    ).astype(BF16)
+    prolonged = dot_exact(tall[...].reshape(count * 2 * height, depth), widen)
+    out[...] = fine[...] + prolonged.reshape(fine.shape)
+
+
+def spread_over_sub(block, order_bits):
+    held = [block]
+    count = lax.axis_size("sub")
+    for bit in order_bits:
+        pairs = [(i, i ^ bit) for i in range(count)]
+        held = held + [lax.ppermute(one, "sub", pairs) for one in held]
+    return held
+
+
+def fast_shards(
+    fine_residual,
+    fine_solution,
+    plane_of_slot,
+    coarse_diagonal,
+    coupling,
+    donor_cells,
+    donor_offsets,
+    receptor_cells,
+    fringe_counts,
+):
+    subs = lax.axis_size("sub")
+    grids = lax.axis_size("grid")
+    coarse = coarse_diagonal.shape[1:]
+    planes, variables, height, depth = coarse
+    blocks = plane_of_slot.shape[1]
+    slots = donor_cells.shape[-1]
+    bits = [1 << k for k in reversed(range(subs.bit_length() - 1))]
+    order = [0]
+    for bit in bits:
+        order = order + [one ^ bit for one in order]
+    sizes = dict(
+        coarse=coarse, blocks=blocks, slots=slots, grids=grids, subs=subs, order=tuple(order)
+    )
+    count = blocks * variables
+    total = subs * planes
+    whole = (total, variables, height, depth)
+    full = jax.ShapeDtypeStruct(whole, F32)
+    rows = pltpu.VMEM((8, subs * slots), F32)
+    stage = pltpu.VMEM((subs, 8, depth), F32)
+
+    def call(kernel, name, out_shape, scalars, *operands, scratch=()):
+        specs = [SMEM if any(one is s for s in scalars) else VMEM for one in operands]
+        return pl.pallas_call(
+            functools.partial(kernel, sizes),
+            out_shape=out_shape,
+            in_specs=specs,
+            out_specs=jax.tree.map(lambda _: VMEM, out_shape),
+            scratch_shapes=list(scratch),
+            compiler_params=pltpu.CompilerParams(vmem_limit_bytes=48 * 1024 * 1024),
+            name=name,
+        )(*operands)
+
+    scalars = (fringe_counts, coupling)
+    fringe = (donor_cells, donor_offsets, receptor_cells)
+    shared = call(
+        pack_kernel,
+        "pack",
+        jax.ShapeDtypeStruct((planes * variables + 1, height, depth), F32),
+        scalars,
+        fringe_counts,
+        coarse_diagonal,
+        *fringe,
+    )
+    shared = spread_over_sub(shared, bits)
+    own = call(
+        restrict_kernel,
+        "restrict",
+        jax.ShapeDtypeStruct((2 * count + 1, height, depth), F32),
+        scalars,
+        fine_residual,
+        fine_solution,
+        plane_of_slot,
+        scratch=[pltpu.VMEM((count, 2 * height, depth), F32)],
+    )
+    corners = call(
+        corner_kernel,
+        "corners",
+        jax.ShapeDtypeStruct((grids, 8, LANES), F32),
+        scalars,
+        fringe_counts,
+        coarse_diagonal,
+        *fringe,
+    )
+    every = spread_over_sub(own, bits)
+    scalars = scalars + (plane_of_slot,)
+    out, gain, mask = call(
+        partial_kernel,
+        "partial",
+        [
+            jax.ShapeDtypeStruct((grids * subs, 16, LANES), F32),
+            full,
+            jax.ShapeDtypeStruct((total, 1, height, depth), F32),
+        ],
+        scalars,
+        *shared,
+        plane_of_slot,
+        own,
+        corners,
+        scratch=[rows, stage, pltpu.VMEM((total, 2 * variables, height, depth), F32)],
+    )
+    arrived = lax.all_to_all(out, ("grid", "sub"), 0, 0, tiled=True)
+    restricted, residual, source = call(
+        assemble_kernel,
+        "assemble",
+        [full, full, full],
+        scalars,
+        *every,
+        coupling,
+        scratch=[pltpu.SMEM((subs, depth), F32), pltpu.SemaphoreType.DMA((subs,))],
+    )
+    return call(
+        finish_kernel,
+        "finish",
+        jax.ShapeDtypeStruct(fine_solution.shape, F32),
+        scalars,
+        *shared,
+        coupling,
+        plane_of_slot,
+        arrived,
+        restricted,
+        residual,
+        source,
+        gain,
+        mask,
+        fine_solution,
+        scratch=[
+            pltpu.VMEM((grids, 8, subs * slots), F32),
+            stage,
+            rows,
+            pltpu.VMEM((total + 2, variables, height, depth), F32),
+            pltpu.VMEM((count, 2 * height, depth), F32),
+        ],
+    )
+
+
 def solution(mesh):
     in_specs = (
         P("grid", "sub", None, None, None),
@@ -189,4 +727,6 @@
         P(),
     )
     out_specs = P("grid", "sub", None, None, None)
-    return jax.shard_map(shards, mesh=mesh, in_specs=in_specs, out_specs=out_specs, check_vma=False)
+    small = mesh.shape["sub"] == 4 and mesh.shape["grid"] * FRINGE == 64
+    body = fast_shards if small else shards
+    return jax.shard_map(body, mesh=mesh, in_specs=in_specs, out_specs=out_specs, check_vma=False)

time: 169 us -> 35.9 us (0.21)
  local copies, waits for them, and re-layouts: 59.7 us -> 4.48 us
  other arithmetic: 31.8 us -> 0 us
  blocking collectives: 26.4 us -> 0 us
  between operations: 15 us -> 0.09 us
  Pallas kernels: 0 us -> 12 us
  waiting for transfers between devices: 15.2 us -> 8.46 us
  starting transfers between devices: 15.6 us -> 10.5 us
  matrix products: 4.06 us -> 0 us
    reduce_sum x2 -> x0, other arithmetic: 23.4 us -> none  [restrict_planes(): return 0.125 * jnp.sum(split_cells, axis=(-3, -1))]
    gather x32 -> x0, local copies, waits for them, and re-layouts: 22.6 us -> none  [corner_values(): jnp.take_along_axis(flat_field, where_cells[..., None, :], axis=-1)]
    all_gather x2 -> x0, blocking collectives: 13.9 us -> none  [the longest x1 7.46 us: shards(): shard_rows = lax.all_gather(correction, 'sub', axis=0, tiled=True)]
    all_to_all x1 -> x0, blocking collectives: 12.5 us -> none  [shards(): lax.all_to_all(blend(corners, offsets), 'grid', split_axis=1, concat_axis...]
    pallas_call x0 -> x6, Pallas kernels: none -> 12 us  [call(): pl.pallas_call(functools.partial(kernel, sizes), out_shape=out_shape, in_...]
    unnamed x96 -> x23, local copies, waits for them, and re-layouts: 15.8 us -> 4.48 us
    all_gather x1 -> x0, waiting for transfers between devices: 8.93 us -> none  [shards(): lax.all_gather(contrib, 'sub', axis=0, tiled=True)]
    ppermute x6, starting transfers between devices: 10.1 us -> 4.25 us  [spread_over_sub(): held = held + [lax.ppermute(one, 'sub', pairs) for one in held]]
  transfers between devices with their start and end apart: 8 -> 7, of which waited for: 4 -> 3; matrix products, arithmetic and copies ran while one was open for 6% -> 0% of each run, Pallas kernels for 0% -> 18%
where the time goes in v2:
time: 35.9 us; the launch traced here: 35.5 us
  Pallas kernels  12 us (33%)
  starting transfers between devices  10.5 us (29%)
  waiting for transfers between devices  8.46 us (24%)
  local copies, waits for them, and re-layouts  4.48 us (12%)
    pallas_call x6, Pallas kernels, call(): pl.pallas_call(functools.partial(kernel, sizes), out_shape=out_shape, in_...  12 us
    all_to_all x1, waiting for transfers between devices, fast_shards(): arrived = lax.all_to_all(out, ('grid', 'sub'), 0, 0, tiled=True)  6.85 us
    all_to_all x1, starting transfers between devices, fast_shards(): arrived = lax.all_to_all(out, ('grid', 'sub'), 0, 0, tiled=True)  6.28 us
    unnamed x23, local copies, waits for them, and re-layouts  4.48 us
    ppermute x6, starting transfers between devices, spread_over_sub(): held = held + [lax.ppermute(one, 'sub', pairs) for one in held]  4.25 us
    ppermute x6, waiting for transfers between devices, spread_over_sub(): held = held + [lax.ppermute(one, 'sub', pairs) for one in held]  1.61 us
  transfers between devices with their start and end apart: 7, of which 3 were waited for; matrix products, arithmetic and copies ran while one was open for 0% of the time, Pallas kernels for 18%

profile of v2, /device:TPU:0, one launch (start us, length us, event | category | flops | bytes accessed | tf_op | source)
XLA Modules:
  0.0 35.5 jit_solution(11956913019930725724)
XLA Ops:
  0.0 0.7 %copy.10.offsets = f32[1,1,3,64]{3,2,1,0:T(4,128)S(1)} copy(f32[1,1,3,64]{3,1,2,0:T(1,128)} %param.15) | data formatting | bytes 1536 | tf_op args[6]
  0.7 0.9 %copy-done.3 = f32[1,4,5,8,128]{4,3,2,1,0:T(8,128)S(1)} copy-done((f32[1,4,5,8,128]{4,3,2,1,0:T(8,128)S(1)}, f32[1,4,5,8,128]{4,3,2,1,0:T(8,128)}, u32[]{:S(2)}) %copy-start.3) | copy-done | bytes 81944
  1.6 0.7 %copy-done.6 = s32[8,8]{1,0:T(8,128)S(1)} copy-done((s32[8,8]{1,0:T(8,128)S(1)}, s32[8,8]{1,0:T(8,128)}, u32[]{:S(2)}) %copy-start.6) | copy-done | bytes 280
  2.3 0.6 %pack.1.refs_0_ = f32[21,8,128]{2,1,0:T(8,128)S(1)} custom-call(s32[8,8]{1,0:T(8,128)S(1)} %copy-done.6, f32[1,4,5,8,128]{4,3,2,1,0:T(8,128)S(1)} %copy-done.3, s32[1,1,64]{2,1,0:T(1,128)S(1)} %copy-done.9, f32[1,1,3,64]{3,2,1,0:T(4,128)S(1)} %copy.10.offsets, s32[1,1,64]{2,1,0:T(1,128)S(1)} %copy-done.10), custom_call_target="tpu_custom_call" | custom-call | tf_op jit(solution)/shard_map/pack/pallas_call | solution.py:624
  2.9 3.0 %collective-permute-start = (f32[21,8,128]{2,1,0:T(8,128)S(1)}, f32[21,8,128]{2,1,0:T(8,128)S(1)}, u32[]{:S(2)}, u32[]{:S(2)}) collective-permute-start(f32[21,8,128]{2,1,0:T(8,128)S(1)} %pack.1.refs_0_), channel_id=1, source_target_pairs={{0,2},{1,3},{2,0},{3,1},{4,6},{5,7},{6,4},{7,5},{8,10},{9,11},{10,... | collective-permute-start | bytes 258056 | tf_op jit(solution)/shard_map/ppermute | solution.py:587
  6.0 1.1 %copy-done = f32[1,8,5,16,256]{4,3,2,1,0:T(8,128)S(1)} copy-done((f32[1,8,5,16,256]{4,3,2,1,0:T(8,128)S(1)}, f32[1,8,5,16,256]{4,3,2,1,0:T(8,128)}, u32[]{:S(2)}) %copy-start) | copy-done | bytes 655384
  7.1 1.1 %copy-done.2 = f32[1,8,5,16,256]{4,3,2,1,0:T(8,128)S(1)} copy-done((f32[1,8,5,16,256]{4,3,2,1,0:T(8,128)S(1)}, f32[1,8,5,16,256]{4,3,2,1,0:T(8,128)}, u32[]{:S(2)}) %copy-start.2) | copy-done | bytes 655384
  8.1 0.8 %restrict.1.refs_5_.refs_0_ = f32[81,8,128]{2,1,0:T(8,128)S(1)} custom-call(f32[1,8,5,16,256]{4,3,2,1,0:T(8,128)S(1)} %copy-done.2, f32[1,8,5,16,256]{4,3,2,1,0:T(8,128)S(1)} %copy-done, s32[1,8]{1,0:T(1,128)S(1)} %copy-done.8), custom_call_target="tpu_custom_call" | custom-call | tf_op jit(solution)/shard_map/restrict/pallas_call | solution.py:624
  8.9 0.1 collective-permute-start.3
  9.0 0.1 collective-permute-start.1
  9.1 0.0 collective-permute-done.refs_1_
  9.1 0.5 %collective-permute-start.2 = (f32[21,8,128]{2,1,0:T(8,128)S(1)}, f32[21,8,128]{2,1,0:T(8,128)S(1)}, u32[]{:S(2)}, u32[]{:S(2)}) collective-permute-start(f32[21,8,128]{2,1,0:T(8,128)S(1)} %collective-permute-done.refs_1_), channel_id=1, source_target_pairs={{0,1},{1,0},{2,3},{3,2},{4,5},{5,4},{6,7},{7,6},{8,9},{9,8},{10,11... | collective-permute-start | bytes 258056 | tf_op jit(solution)/shard_map/ppermute | solution.py:587
  9.6 1.2 %corners.1.refs_6_ = f32[8,8,128]{2,1,0:T(8,128)S(1)} custom-call(s32[8,8]{1,0:T(8,128)S(1)} %copy-done.7, f32[1,4,5,8,128]{4,3,2,1,0:T(8,128)S(1)} %copy-done.4, s32[1,1,64]{2,1,0:T(1,128)S(1)} %copy-done.9, f32[1,1,3,64]{3,2,1,0:T(4,128)S(1)} %copy.10.offsets, s32[1,1,64]{2,1,0:T(1,128)S(1)} %copy-done.10), custom_call_target="tpu_custom_call" | custom-call | tf_op jit(solution)/shard_map/corners/pallas_call | solution.py:624
  10.8 0.0 collective-permute-done.1.refs_2_
  10.8 2.9 %partial.1 = (f32[32,16,128]{2,1,0:T(8,128)}, f32[16,5,8,128]{3,2,1,0:T(8,128)S(1)}, f32[16,1,8,128]{3,2,1,0:T(8,128)S(1)}) custom-call(f32[21,8,128]{2,1,0:T(8,128)S(1)} %pack.1.refs_0_, f32[21,8,128]{2,1,0:T(8,128)S(1)} %collective-permute-done.refs_1_, f32[21,8,128]{2,1,0:T(8,128)S(1)} %collective-permute-done.1.refs_2_, ...), custom_call_target="tpu_custom_call" | custom-call | tf_op jit(solution)/shard_map/partial/pallas_call | solution.py:624
  13.7 6.3 %all-to-all-start = ((f32[32,16,128]{2,1,0:T(8,128)}), f32[32,16,128]{2,1,0:T(8,128)S(1)}, u32[]{:S(2)}, u32[]{:S(2)}) async-start(f32[32,16,128]{2,1,0:T(8,128)} %get-tuple-element.11), calls=%async_computation | async-start | bytes 524288 | tf_op jit(solution)/shard_map/all_to_all | solution.py:682
  20.0 0.0 copy-start.1
  20.0 0.3 collective-permute-start.4
  20.3 0.3 collective-permute-start.5
  20.6 1.1 %collective-permute-done.4.refs_2_ = f32[81,8,128]{2,1,0:T(8,128)S(1)} collective-permute-done((f32[81,8,128]{2,1,0:T(8,128)S(1)}, f32[81,8,128]{2,1,0:T(8,128)S(1)}, u32[]{:S(2)}, u32[]{:S(2)}) %collective-permute-start.4) | collective-permute-done | bytes 331808 | tf_op jit(solution)/shard_map/ppermute | solution.py:587
  21.7 0.5 %collective-permute-done.5.refs_3_ = f32[81,8,128]{2,1,0:T(8,128)S(1)} collective-permute-done((f32[81,8,128]{2,1,0:T(8,128)S(1)}, f32[81,8,128]{2,1,0:T(8,128)S(1)}, u32[]{:S(2)}, u32[]{:S(2)}) %collective-permute-start.5) | collective-permute-done | bytes 331808 | tf_op jit(solution)/shard_map/ppermute | solution.py:587
  22.2 1.5 %assemble.1 = (f32[16,5,8,128]{3,2,1,0:T(8,128)S(1)}, f32[16,5,8,128]{3,2,1,0:T(8,128)S(1)}, f32[16,5,8,128]{3,2,1,0:T(8,128)S(1)}) custom-call(f32[81,8,128]{2,1,0:T(8,128)S(1)} %restrict.1.refs_5_.refs_0_, f32[81,8,128]{2,1,0:T(8,128)S(1)} %collective-permute-done.3.refs_1_, f32[81,8,128]{2,1,0:T(8,128)S(1)} %collective-permute-done.4.refs_2_, ...), custom_call_target="tpu_custom_call" | custom-call | tf_op jit(solution)/shard_map/assemble/pallas_call | solution.py:624
  23.7 6.9 %all-to-all-done.refs_6_ = f32[32,16,128]{2,1,0:T(8,128)S(1)} async-done(((f32[32,16,128]{2,1,0:T(8,128)}), f32[32,16,128]{2,1,0:T(8,128)S(1)}, u32[]{:S(2)}, u32[]{:S(2)}) %all-to-all-start) | async-done | bytes 262176 | tf_op jit(solution)/shard_map/all_to_all | solution.py:682
  30.6 4.9 %finish.1 = f32[1,8,5,16,256]{4,3,2,1,0:T(8,128)} custom-call(f32[21,8,128]{2,1,0:T(8,128)S(1)} %pack.1.refs_0_, f32[21,8,128]{2,1,0:T(8,128)S(1)} %collective-permute-done.refs_1_, f32[21,8,128]{2,1,0:T(8,128)S(1)} %collective-permute-done.1.refs_2_, f32[21,8,128]{2,1,0:T(8,128)S(1)} %collective-permute-done.2.refs_3_, f32[5,5]{1,0:T(8,128)S(1)} %copy-done.5, ...), custom_call_target="tpu_custom_call" | custom-call | tf_op jit(solution)/shard_map/finish/pallas_call | solution.py:624
  (19 shorter events, 0.0 us)
Async XLA Ops:
  0.0 0.7 %copy-start.10 = (s32[1,1,64]{2,1,0:T(1,128)S(1)}, s32[1,1,64]{2,1,0:T(1,128)}, u32[]{:S(2)}) copy-start(s32[1,1,64]{2,1,0:T(1,128)} %receptors.3) | copy-start | bytes 772
  0.0 0.7 %copy-start.9 = (s32[1,1,64]{2,1,0:T(1,128)S(1)}, s32[1,1,64]{2,1,0:T(1,128)}, u32[]{:S(2)}) copy-start(s32[1,1,64]{2,1,0:T(1,128)} %donors.3) | copy-start | bytes 772
  0.7 0.9 %copy-start.3 = (f32[1,4,5,8,128]{4,3,2,1,0:T(8,128)S(1)}, f32[1,4,5,8,128]{4,3,2,1,0:T(8,128)}, u32[]{:S(2)}) copy-start(f32[1,4,5,8,128]{4,3,2,1,0:T(8,128)} %diagonal.3) | copy-start | bytes 245764
  1.6 0.7 %copy-start.6 = (s32[8,8]{1,0:T(8,128)S(1)}, s32[8,8]{1,0:T(8,128)}, u32[]{:S(2)}) copy-start(s32[8,8]{1,0:T(8,128)} %counts.3) | copy-start | bytes 772
  2.3 3.7 %copy-start.8 = (s32[1,8]{1,0:T(1,128)S(1)}, s32[1,8]{1,0:T(1,128)}, u32[]{:S(2)}) copy-start(s32[1,8]{1,0:T(1,128)} %refs_5_.1) | copy-start | bytes 100
  2.9 6.1 %collective-permute-start = (f32[21,8,128]{2,1,0:T(8,128)S(1)}, f32[21,8,128]{2,1,0:T(8,128)S(1)}, u32[]{:S(2)}, u32[]{:S(2)}) collective-permute-start(f32[21,8,128]{2,1,0:T(8,128)S(1)} %pack.1.refs_0_), channel_id=1, source_target_pairs={{0,2},{1,3},{2,0},{3,1},{4,6},{5,7},{6,4},{7,5},{8,10},{9,11},{10,... | collective-permute-start | bytes 258056 | tf_op jit(solution)/shard_map/ppermute | solution.py:587
  6.0 1.1 %copy-start = (f32[1,8,5,16,256]{4,3,2,1,0:T(8,128)S(1)}, f32[1,8,5,16,256]{4,3,2,1,0:T(8,128)}, u32[]{:S(2)}) copy-start(f32[1,8,5,16,256]{4,3,2,1,0:T(8,128)} %refs_12_.1) | copy-start | bytes 1966084
  7.0 1.1 %copy-start.2 = (f32[1,8,5,16,256]{4,3,2,1,0:T(8,128)S(1)}, f32[1,8,5,16,256]{4,3,2,1,0:T(8,128)}, u32[]{:S(2)}) copy-start(f32[1,8,5,16,256]{4,3,2,1,0:T(8,128)} %residual.1) | copy-start | bytes 1966084
  8.1 1.4 %copy-start.4 = (f32[1,4,5,8,128]{4,3,2,1,0:T(8,128)S(1)}, f32[1,4,5,8,128]{4,3,2,1,0:T(8,128)}, u32[]{:S(2)}) copy-start(f32[1,4,5,8,128]{4,3,2,1,0:T(8,128)} %diagonal.3) | copy-start | bytes 245764
  8.1 1.4 %copy-start.7 = (s32[8,8]{1,0:T(8,128)S(1)}, s32[8,8]{1,0:T(8,128)}, u32[]{:S(2)}) copy-start(s32[8,8]{1,0:T(8,128)} %counts.3) | copy-start | bytes 772
  8.9 11.4 %collective-permute-start.3 = (f32[81,8,128]{2,1,0:T(8,128)S(1)}, f32[81,8,128]{2,1,0:T(8,128)S(1)}, u32[]{:S(2)}, u32[]{:S(2)}) collective-permute-start(f32[81,8,128]{2,1,0:T(8,128)S(1)} %restrict.1.refs_5_.refs_0_), channel_id=1, source_target_pairs={{0,2},{1,3},{2,0},{3,1},{4,6},{5,7},{6,4},{7,5},{8,10},{9,11},{10,... | collective-permute-start | bytes 995336 | tf_op jit(solution)/shard_map/ppermute | solution.py:587
  9.0 1.8 %collective-permute-start.1 = (f32[21,8,128]{2,1,0:T(8,128)S(1)}, f32[21,8,128]{2,1,0:T(8,128)S(1)}, u32[]{:S(2)}, u32[]{:S(2)}) collective-permute-start(f32[21,8,128]{2,1,0:T(8,128)S(1)} %pack.1.refs_0_), channel_id=1, source_target_pairs={{0,1},{1,0},{2,3},{3,2},{4,5},{5,4},{6,7},{7,6},{8,9},{9,8},{10,11... | collective-permute-start | bytes 258056 | tf_op jit(solution)/shard_map/ppermute | solution.py:587
  9.1 1.7 %collective-permute-start.2 = (f32[21,8,128]{2,1,0:T(8,128)S(1)}, f32[21,8,128]{2,1,0:T(8,128)S(1)}, u32[]{:S(2)}, u32[]{:S(2)}) collective-permute-start(f32[21,8,128]{2,1,0:T(8,128)S(1)} %collective-permute-done.refs_1_), channel_id=1, source_target_pairs={{0,1},{1,0},{2,3},{3,2},{4,5},{5,4},{6,7},{7,6},{8,9},{9,8},{10,11... | collective-permute-start | bytes 258056 | tf_op jit(solution)/shard_map/ppermute | solution.py:587
  13.7 8.5 %copy-start.5 = (f32[5,5]{1,0:T(8,128)S(1)}, f32[5,5]{1,0:T(8,128)}, u32[]{:S(2)}) copy-start(f32[5,5]{1,0:T(8,128)} %refs_4_.5) | copy-start | bytes 304
  13.7 16.9 %all-to-all-start = ((f32[32,16,128]{2,1,0:T(8,128)}), f32[32,16,128]{2,1,0:T(8,128)S(1)}, u32[]{:S(2)}, u32[]{:S(2)}) async-start(f32[32,16,128]{2,1,0:T(8,128)} %get-tuple-element.11), calls=%async_computation | async-start | bytes 524288 | tf_op jit(solution)/shard_map/all_to_all | solution.py:682
  20.0 10.6 %copy-start.1 = (f32[1,8,5,16,256]{4,3,2,1,0:T(8,128)S(1)}, f32[1,8,5,16,256]{4,3,2,1,0:T(8,128)}, u32[]{:S(2)}) copy-start(f32[1,8,5,16,256]{4,3,2,1,0:T(8,128)} %refs_12_.1) | copy-start | bytes 1966084
  20.0 1.7 %collective-permute-start.4 = (f32[81,8,128]{2,1,0:T(8,128)S(1)}, f32[81,8,128]{2,1,0:T(8,128)S(1)}, u32[]{:S(2)}, u32[]{:S(2)}) collective-permute-start(f32[81,8,128]{2,1,0:T(8,128)S(1)} %restrict.1.refs_5_.refs_0_), channel_id=1, source_target_pairs={{0,1},{1,0},{2,3},{3,2},{4,5},{5,4},{6,7},{7,6},{8,9},{9,8},{10,11... | collective-permute-start | bytes 995336 | tf_op jit(solution)/shard_map/ppermute | solution.py:587
  20.3 1.9 %collective-permute-start.5 = (f32[81,8,128]{2,1,0:T(8,128)S(1)}, f32[81,8,128]{2,1,0:T(8,128)S(1)}, u32[]{:S(2)}, u32[]{:S(2)}) collective-permute-start(f32[81,8,128]{2,1,0:T(8,128)S(1)} %collective-permute-done.3.refs_1_), channel_id=1, source_target_pairs={{0,1},{1,0},{2,3},{3,2},{4,5},{5,4},{6,7},{7,6},{8,9},{9,8},{10,11... | collective-permute-start | bytes 995336 | tf_op jit(solution)/shard_map/ppermute | solution.py:587

commit v3 on v2

--- a/solution.py
+++ b/solution.py
@@ -185,25 +185,28 @@
 HIGHEST = lax.Precision.HIGHEST
 VMEM = pl.BlockSpec(memory_space=pltpu.VMEM)
 SMEM = pl.BlockSpec(memory_space=pltpu.SMEM)
+HBM = pl.BlockSpec(memory_space=pltpu.HBM)
 LANES = 128
-ROW = 256
-PLANE = 4096
-NOWHERE = -(1 << 20)
-
-
-def pieces(values):
-    high = values.astype(BF16).astype(F32)
-    middle = (values - high).astype(BF16).astype(F32)
-    low = (values - high - middle).astype(BF16).astype(F32)
-    return high, middle, low
+WET = 1 << 20
+
+
+def two_pieces(values):
+    high = values.astype(BF16)
+    return high, (values - high.astype(F32)).astype(BF16)
 
 
 def dot_exact(values, matrix, contract=(((1,), (0,)), ((), ()))):
-    total = None
-    for piece in reversed(pieces(values)):
-        term = lax.dot_general(piece.astype(BF16), matrix, contract, preferred_element_type=F32)
-        total = term if total is None else total + term
-    return total
+    high, low = two_pieces(values)
+    total = lax.dot_general(low, matrix, contract, preferred_element_type=F32)
+    return total + lax.dot_general(high, matrix, contract, preferred_element_type=F32)
+
+
+def dot_near(values, matrix):
+    high, low = two_pieces(values)
+    matrix_high, matrix_low = two_pieces(matrix)
+    total = jnp.dot(low, matrix_high, preferred_element_type=F32)
+    total = total + jnp.dot(high, matrix_low, preferred_element_type=F32)
+    return total + jnp.dot(high, matrix_high, preferred_element_type=F32)
 
 
 def iota(shape, dim):
@@ -248,55 +251,94 @@
     return mask.reshape(total, 1, height, depth), here, onehot
 
 
-def pack_kernel(sizes, counts, diagonal, donors, offsets, receptors, out):
+def start_copies(pairs, sems):
+    copies = [pltpu.make_async_copy(*pair, sems.at[i]) for i, pair in enumerate(pairs)]
+    for copy in copies:
+        copy.start()
+    return copies
+
+
+def pack_kernel(
+    sizes, counts, diagonal, donors, offsets, receptors, out, held, rows, cells, allowed, sems
+):
     planes, variables, height, depth = sizes["coarse"]
     slots = sizes["slots"]
     base = lax.axis_index("sub") * (planes * height * depth)
     grid_index = lax.axis_index("grid")
     count = planes * variables
-    out[0:count] = diagonal[0].reshape(count, height, depth)
-    cell = live_cells(counts, grid_index, sizes["grids"], receptors[0], base)
+    copies = start_copies(
+        [
+            (counts, allowed),
+            (receptors.at[0], cells.at[0]),
+            (donors.at[0], cells.at[1]),
+            (offsets.at[0], rows),
+            (diagonal.at[0], held),
+        ],
+        sems,
+    )
     out[count] = jnp.zeros((height, depth), F32)
-    out[count, 0:1, 0:slots] = (donors[0] + base).astype(F32)
-    out[count, 1:4, 0:slots] = offsets[0, 0]
+    for copy in copies:
+        copy.wait()
+    out[0:count] = OMEGA / (6.0 + held[...].reshape(count, height, depth))
+    cell = live_cells(allowed, grid_index, sizes["grids"], cells[0], base)
+    out[count, 0:1, 0:slots] = (cells[1] + base).astype(F32)
+    for k in range(3):
+        out[count, k + 1 : k + 2, 0:slots] = rows[k]
     out[count, 4:5, 0:slots] = cell.astype(F32)
 
 
-def restrict_kernel(sizes, residual, fine, ids, out, wide):
+def restrict_kernel(sizes, residual, fine, ids, first, second, out, held, wide, sems):
     planes, variables, height, depth = sizes["coarse"]
     blocks = sizes["blocks"]
-    count = blocks * variables
+    step = 8
+    copies = start_copies(
+        [
+            (source.at[0, q : q + step], held.at[k, q : q + step])
+            for k, source in enumerate((fine, residual))
+            for q in range(0, blocks, step)
+        ],
+        sems,
+    )
     pair = jnp.where(
         iota((2 * depth, depth), 0) // 2 == iota((2 * depth, depth), 1), 0.125, 0.0
     ).astype(BF16)
-    for at, source in ((0, fine), (count, residual)):
-        rows = source[0].reshape(count * 2 * height, 2 * depth)
-        wide[...] = dot_exact(rows, pair).reshape(count, 2 * height, depth)
-        out[at : at + count] = (
-            wide[:, pl.ds(0, height, stride=2), :] + wide[:, pl.ds(1, height, stride=2), :]
+    count = step * variables
+    out[2 * blocks * variables] = jnp.zeros((height, depth), F32)
+    out[2 * blocks * variables, 0:1, 0:blocks] = ids[...].astype(F32)
+    for i, copy in enumerate(copies):
+        k, q = divmod(i * step, blocks)
+        copy.wait()
+        rows = held[k, q : q + step].reshape(count * 2 * height, 2 * depth)
+        here = pl.ds(i * count, count)
+        wide[here] = dot_exact(rows, pair).reshape(count, 2 * height, depth)
+        out[here] = (
+            wide[here, pl.ds(0, height, stride=2), :] + wide[here, pl.ds(1, height, stride=2), :]
         )
-    out[2 * count] = jnp.zeros((height, depth), F32)
-    out[2 * count, 0:1, 0:blocks] = ids[...].astype(F32)
-
-
-def corner_kernel(sizes, counts, diagonal, donors, offsets, receptors, out):
+
+
+def corner_kernel(sizes, shared, out):
     planes, variables, height, depth = sizes["coarse"]
     slots, grids = sizes["slots"], sizes["grids"]
     sub_index = lax.axis_index("sub")
-    cell = live_cells(counts, lax.axis_index("grid"), grids, receptors[0], 0)
+    meta = shared[planes * variables, :, 0:slots]
+    base = sub_index * (planes * height * depth)
+    cell = meta[4:5].astype(jnp.int32)
+    cell = jnp.where(cell >= 0, cell - base, -1)
     mask, _, _ = receptor_mask(cell, planes, height, depth)
-    gain = OMEGA / (6.0 + diagonal[0])
-    fields = jnp.concatenate([gain, 1.0 - mask], axis=1)
-    twice = jnp.concatenate([donors[0], donors[0]], axis=1)
+    gain = shared[0 : planes * variables].reshape(planes, variables, height, depth)
+    fields = jnp.concatenate([gain, mask], axis=1)
+    donors = meta[0:1].astype(jnp.int32) - base
+    twice = jnp.concatenate([donors, donors], axis=1)
     step_z = iota(twice.shape, 1) // slots
     plane, row, column = split_cell(twice, height, depth)
     onehot = jnp.where(iota((depth, LANES), 0) == column + step_z, 1.0, 0.0).astype(BF16)
     count = planes * (variables + 1) * height
     at_column = dot_exact(fields.reshape(count, depth), onehot)
     at_column = at_column.reshape(planes, variables + 1, height, LANES)
-    both = jnp.concatenate([offsets[0, 0], offsets[0, 0]], axis=1)
+    both = jnp.concatenate([meta[1:4], meta[1:4]], axis=1)
     weight_z = jnp.where(step_z == 1, both[2:3], 1.0 - both[2:3])
     at_row = iota((height, LANES), 0)
+    empty = jnp.zeros((1, LANES), F32)
     tiles = []
     for step_x in (0, 1):
         weight_x = both[0:1] if step_x else 1.0 - both[0:1]
@@ -309,19 +351,14 @@
             here = jnp.where(at_row == row + step_y, 1.0, 0.0)
             found = jnp.sum(by_plane * here[None], axis=1)
             weight = weight_x * weight_y * weight_z
-            number = (
-                (plane + step_x + sub_index * planes) * PLANE
-                + (row + step_y) * ROW
-                + column
-                + step_z
-            ).astype(F32)
-            scaled = weight * found[:variables] * found[variables : variables + 1]
-            tiles.append(jnp.concatenate([weight, weight, scaled, number], axis=0))
+            wet = found[variables : variables + 1]
+            scaled = weight * (found[:variables] * (1.0 - wet) + wet)
+            number = twice + base + (step_x * height + step_y) * depth + step_z
+            number = number.astype(F32) + wet * float(WET)
+            tiles.append(jnp.concatenate([empty, empty, scaled, number], axis=0))
     lane = iota((8, LANES), 1)
     sublane = iota((8, LANES), 0)
-    target_plane, target_row, target_column = split_cell(cell, height, depth)
-    number = (target_plane + sub_index * planes) * PLANE + target_row * ROW + target_column
-    number = jnp.where(cell >= 0, number, NOWHERE).astype(F32)
+    number = meta[4:5]
     number = jnp.broadcast_to(jnp.concatenate([number, number], axis=1), (8, LANES))
     half = slots // 2
     moved = jnp.where(sublane == 2, pltpu.roll(number, half, 1), number)
@@ -332,8 +369,6 @@
         for c in range(8):
             shift = (64 + 8 * c - (c % 2) * 64 - 8 * h) % LANES
             tile = jnp.where(lane // 8 == 8 + c, pltpu.roll(tiles[c // 2], shift, 1), tile)
-        weight = pltpu.roll(jnp.broadcast_to(tile[0:1], (8, LANES)), 64, 1)
-        tile = jnp.where((sublane == 7) & (lane < 64), weight, tile)
         out[h] = jnp.where(targets, moved, tile)
 
 
@@ -349,12 +384,8 @@
     frac_x, frac_y, frac_z = rows[1:2, :], rows[2:3, :], rows[3:4, :]
     weight_z = hats((depth, count), 0, column, frac_z)
     weight_y = hats((height, count), 0, row, frac_y)
-    along_z = jnp.dot(
-        field.reshape(total * variables * height, depth),
-        weight_z,
-        precision=HIGHEST,
-        preferred_element_type=F32,
-    ).reshape(total, variables, height, count)
+    along_z = dot_near(field.reshape(total * variables * height, depth), weight_z)
+    along_z = along_z.reshape(total, variables, height, count)
     summed = None
     for p in range(total):
         weight_x = jnp.where(plane == p, 1.0 - frac_x, 0.0) + jnp.where(
@@ -377,8 +408,7 @@
     for i, part in enumerate(parts):
         owner = sub_index ^ sizes["order"][i]
         stage[owner] = part[count]
-        diagonal = part[0:count].reshape(planes, variables, height, depth)
-        gain[pl.ds(owner * planes, planes)] = OMEGA / (6.0 + diagonal)
+        gain[pl.ds(owner * planes, planes)] = part[0:count].reshape(sizes["coarse"])
     for j in range(subs):
         rows[:, j * slots : (j + 1) * slots] = stage[j, :, 0:slots]
     both[...] = jnp.zeros(both.shape, F32)
@@ -398,12 +428,9 @@
     swept = jnp.where(wet, 0.0, restricted + gain[...] * (residual - beside))
     values = interpolate(jnp.concatenate([restricted, swept], axis=1), rows)
     first, second = values[:variables], values[variables:]
-    top = jnp.concatenate(
-        [first[v : v + 1, k * LANES : (k + 1) * LANES] for v in range(4) for k in range(2)], axis=0
-    )
     empty = jnp.zeros((1, LANES), F32)
-    last = [first[4:5, k * LANES : (k + 1) * LANES] for k in range(2)]
-    low = jnp.concatenate(last + [second[:, 0:LANES], empty], axis=0)
+    top = jnp.concatenate([first[:, 0:LANES], first[0:3, LANES:]], axis=0)
+    low = jnp.concatenate([first[3:5, LANES:], second[:, 0:LANES], empty], axis=0)
     high = jnp.concatenate([empty, empty, second[:, LANES:], empty], axis=0)
     lane = iota((8, LANES), 1)
     sublane = iota((8, LANES), 0)
@@ -455,8 +482,29 @@
     return jnp.concatenate(outs, axis=1)
 
 
+def target_features(cell, height, depth):
+    plane, row, column = split_cell(jnp.maximum(cell, 0), height, depth)
+    square = plane * plane + row * row + column * column
+    square = jnp.where(cell >= 0, square, 1 << 15)
+    coarse = square // LANES * LANES
+    one = jnp.ones(cell.shape, jnp.int32)
+    rows = [plane, row, column, one, one, one, -coarse, 2 + coarse - square]
+    return jnp.concatenate([each.astype(F32) for each in rows], axis=0)
+
+
+def corner_features(number, height, depth):
+    wet = jnp.where(number >= WET, 1, 0)
+    plane, row, column = split_cell(number - WET * wet, height, depth)
+    square = plane * plane + row * row + column * column
+    coarse = square // LANES * LANES
+    one = jnp.ones(number.shape, jnp.int32)
+    rows = [2 * plane, 2 * row, 2 * column, -coarse, coarse - square, -wet, one, one]
+    return jnp.concatenate([each.astype(F32) for each in rows], axis=0)
+
+
 def fringe_values(sizes, arrived, landing):
-    subs, grids = sizes["subs"], sizes["grids"]
+    subs, grids, slots = sizes["subs"], sizes["grids"], sizes["slots"]
+    _, _, height, depth = sizes["coarse"]
     lane = iota((8, LANES), 1)
     sublane = iota((8, LANES), 0)
     group = lane % 64 // 8
@@ -467,11 +515,8 @@
         for s in range(1, subs):
             top = top + arrived[g * subs + s, 0:8]
             last = last + arrived[g * subs + s, 8:16]
-        halves = []
-        for k in range(2):
-            rows = [top[2 * v + k : 2 * v + k + 1] for v in range(4)] + [last[k : k + 1]]
-            halves.append(jnp.concatenate(rows + [jnp.zeros((3, LANES), F32)], axis=0))
-        firsts.append((halves, last))
+        right = jnp.where(sublane < 3, pltpu.roll(top, 3, 0), pltpu.roll(last, 3, 0))
+        firsts.append(((top, right), last))
     for g in range(grids):
         for k in range(2):
             sent = jnp.zeros((8, LANES), F32)
@@ -479,45 +524,78 @@
                 moved = pltpu.roll(firsts[other][0][k], (8 * other - 8 * g) % LANES, 1)
                 sent = jnp.where(group == other, moved, sent)
             landing[g, :, k * LANES : (k + 1) * LANES] = sent
-    targets, numbers, scales, weights = [], [], [], []
+    targets = [jnp.zeros((8, LANES), F32)] * 2
+    numbers = [jnp.zeros((8, LANES), F32)] * 2
+    scales = []
     for g in range(grids):
         tiles = [arrived[g * subs + s, 8:16] for s in range(subs)]
-        target, scale, weight = [], [], []
+        scale = []
         for k in range(2):
             one, two = tiles[2 * k], tiles[2 * k + 1]
             scale.append(jnp.where(lane < 64, pltpu.roll(one, 64, 1), two))
-            weight.append(jnp.where(lane < 64, one, pltpu.roll(two, 64, 1))[7:8])
-            left = jnp.where(lane < 32, pltpu.roll(one, 96, 1)[2:3], one[3:4])
-            right = jnp.where(lane < 96, pltpu.roll(two, 32, 1)[2:3], pltpu.roll(two, 64, 1)[3:4])
-            target.append(jnp.where(lane < 64, left, right)[0:1])
-        targets.append(jnp.concatenate(target, axis=1))
-        scales.append(jnp.concatenate(scale, axis=1))
-        weights.append(jnp.concatenate(weight, axis=1))
-    columns = jnp.concatenate(targets, axis=0).T
+            left = jnp.where(lane < 32, pltpu.roll(pltpu.roll(one, 96, 1), 1, 0), one)
+            right = pltpu.roll(two, 64, 1)
+            right = jnp.where(lane < 96, pltpu.roll(pltpu.roll(two, 32, 1), 1, 0), right)
+            target = jnp.where(lane < 64, left, right)
+            targets[k] = jnp.where(sublane == g, pltpu.roll(target, (g + 5) % 8, 0), targets[k])
+            number = pltpu.roll(scale[k], (g + 1) % 8, 0)
+            numbers[k] = jnp.where(sublane == g, number, numbers[k])
+        scales.append(scale)
+    targets = jnp.concatenate(targets, axis=1).astype(jnp.int32)
+    numbers = jnp.concatenate(numbers, axis=1).astype(jnp.int32)
+    theirs = target_features(targets, height, depth).T.astype(BF16)
+    ours = corner_features(numbers, height, depth)
+    which = iota(ours.shape, 0) % 8
+    mine = [jnp.where(which == g, ours, 0.0).astype(BF16) for g in range(grids)]
+    closeness = jnp.dot(theirs, jnp.concatenate(mine, axis=1), preferred_element_type=F32)
+    match = jnp.maximum(closeness.astype(BF16), 0.0)
+    lanes = subs * slots
     total = [jnp.zeros((8, LANES), F32), jnp.zeros((8, LANES), F32)]
     for g in range(grids):
-        apart = jnp.abs(columns[:, g : g + 1] - scales[g][7:8])
-        near = (apart == 1.0) | (apart == float(ROW)) | (apart == float(PLANE))
-        beside = jnp.where(near, 1.0, 0.0).astype(BF16)
-        equal = jnp.where(apart == 0.0, 1.0, 0.0).astype(BF16)
-        stacked = jnp.concatenate(pieces(landing[g]), axis=0).astype(BF16)
-        by_side = jnp.dot(stacked, beside, preferred_element_type=F32)
-        by_self = jnp.dot(stacked, equal, preferred_element_type=F32)
-        by_side = by_side[16:24] + by_side[8:16] + by_side[0:8]
-        by_self = by_self[16:24] + by_self[8:16] + by_self[0:8]
+        sent = landing[g]
+        high = sent.astype(BF16).astype(F32)
+        stacked = jnp.concatenate([high, sent - high], axis=0).astype(BF16)
+        near = jnp.dot(stacked, match[:, g * lanes : (g + 1) * lanes], preferred_element_type=F32)
+        near = near[0:8] + near[8:16]
+        known = pltpu.roll(firsts[g][1], 6, 0)
         for k in range(2):
             here = slice(k * LANES, (k + 1) * LANES)
-            scale = pltpu.roll(scales[g][:, here], 6, 0)
-            value = by_side[:, here] * scale + by_self[:, here] * weights[g][:, here]
+            scale = pltpu.roll(scales[g][k], 6, 0)
+            value = near[:, here] * scale
             for step in (32, 16, 8):
                 value = value + pltpu.roll(value, LANES - step, 1)
-            known = pltpu.roll(firsts[g][1], 6, 0)
+            value = pltpu.roll(value, 8 * g, 1)
             for s in range(2):
-                mine = (group == g) & (lane // 64 == s)
-                moved = pltpu.roll(value, 8 * g, 1)
                 base = pltpu.roll(known, (64 * s + 8 * g - 16 * k - 8 * s) % LANES, 1)
-                total[k] = jnp.where(mine, moved + base, total[k])
+                found = (group == g) & (lane // 64 == s)
+                total[k] = jnp.where(found, value + base, total[k])
     return landing[lax.axis_index("grid")], jnp.concatenate(total, axis=1)
+
+
+def spread(values, cell, total, height, depth):
+    count = cell.shape[1]
+    pairs = values.shape[0] // 2
+    plane, row, column = split_cell(cell, height, depth)
+    onehot = jnp.where(iota((depth, count), 0) == column, 1.0, 0.0).astype(BF16)
+    row_here = (iota((2 * height, count), 0) % height == row) & (cell >= 0)
+    tiles = []
+    for i in range(pairs):
+        twin = [jnp.broadcast_to(values[2 * i + k : 2 * i + k + 1], (height, count)) for k in (0, 1)]
+        tiles.append(two_pieces(jnp.concatenate(twin, axis=0)))
+    rows = [[], []]
+    for p in range(total):
+        here = jnp.where(row_here & (plane == p), 1.0, 0.0).astype(BF16)
+        for tile in tiles:
+            for k in (0, 1):
+                rows[k].append(tile[k] * here)
+    contract = (((1,), (1,)), ((), ()))
+    high, low = [
+        lax.dot_general(
+            jnp.concatenate(rows[k], axis=0), onehot, contract, preferred_element_type=F32
+        )
+        for k in (0, 1)
+    ]
+    return (high + low).reshape(total, 2 * pairs, height, depth)
 
 
 def finish_kernel(sizes, *refs):
@@ -526,7 +604,7 @@
     blocks = sizes["blocks"]
     parts = refs[:subs]
     coupling, ids, arrived, restricted, residual, source, gain, mask = refs[subs : subs + 8]
-    fine, out, landing, stage, rows, padded, tall = refs[subs + 8 :]
+    fine, out, landing, stage, rows, padded, tall, held, sems = refs[subs + 8 :]
     total = subs * planes
     slots = sizes["slots"]
     count = blocks * variables
@@ -537,15 +615,8 @@
         rows[:, j * slots : (j + 1) * slots] = stage[j, :, 0:slots]
     first, second = fringe_values(sizes, arrived, landing)
     cell = rows[4:5, :].astype(jnp.int32)
-    _, here, onehot = receptor_mask(cell, total, height, depth)
-    lanes = subs * slots
     values = jnp.concatenate([first[:variables], second[:variables]], axis=0)
-    stacked = here.reshape(total, 1, height, lanes) * values[None, :, None, :]
-    landed = dot_exact(
-        stacked.reshape(total * 2 * variables * height, lanes),
-        onehot,
-        (((1,), (1,)), ((), ())),
-    ).reshape(total, 2 * variables, height, depth)
+    landed = spread(values, cell, total, height, depth)
     wet = mask[...] > 0.5
     start = restricted[...]
     scale = gain[...]
@@ -560,6 +631,14 @@
     padded[total + 1 : total + 2] = jnp.zeros((1, variables, height, depth), F32)
     padded[1 : total + 1] = correction
     at_row = iota((variables, height, depth), 1)
+    coarse_at = iota((depth, 2 * depth), 0)
+    fine_at = iota((depth, 2 * depth), 1)
+    beside = fine_at // 2 - 1 + 2 * (fine_at % 2)
+    widen = jnp.where(
+        coarse_at == fine_at // 2, 0.75, jnp.where(coarse_at == beside, 0.25, 0.0)
+    ).astype(BF16)
+    copies = []
+    step = 2
     for q in range(blocks):
         number = ids[0, q]
         coarse = number // 2
@@ -569,14 +648,19 @@
         block = slice(q * variables, (q + 1) * variables)
         tall[block, pl.ds(0, height, stride=2), :] = 0.75 * along + 0.25 * below
         tall[block, pl.ds(1, height, stride=2), :] = 0.75 * along + 0.25 * above
-    coarse_at = iota((depth, 2 * depth), 0)
-    fine_at = iota((depth, 2 * depth), 1)
-    beside = fine_at // 2 - 1 + 2 * (fine_at % 2)
-    widen = jnp.where(
-        coarse_at == fine_at // 2, 0.75, jnp.where(coarse_at == beside, 0.25, 0.0)
-    ).astype(BF16)
-    prolonged = dot_exact(tall[...].reshape(count * 2 * height, depth), widen)
-    out[...] = fine[...] + prolonged.reshape(fine.shape)
+        if q % step == step - 1:
+            low = q + 1 - step
+            rows_in = tall[low * variables : (q + 1) * variables]
+            prolonged = dot_exact(rows_in.reshape(step * variables * 2 * height, depth), widen)
+            shape = (step, variables, 2 * height, 2 * depth)
+            held[low : q + 1] = fine[0, low : q + 1] + prolonged.reshape(shape)
+            copy = pltpu.make_async_copy(
+                held.at[low : q + 1], out.at[0, low : q + 1], sems.at[q // step]
+            )
+            copy.start()
+            copies.append(copy)
+    for copy in copies:
+        copy.wait()
 
 
 def spread_over_sub(block, order_bits):
@@ -619,51 +703,71 @@
     rows = pltpu.VMEM((8, subs * slots), F32)
     stage = pltpu.VMEM((subs, 8, depth), F32)
 
-    def call(kernel, name, out_shape, scalars, *operands, scratch=()):
-        specs = [SMEM if any(one is s for s in scalars) else VMEM for one in operands]
+    def call(kernel, name, out_shape, scalars, *operands, scratch=(), far=(), out_spec=VMEM, aliases={}):
+        specs = [
+            SMEM if any(one is s for s in scalars) else HBM if any(one is f for f in far) else VMEM
+            for one in operands
+        ]
+        operands = [
+            pltpu.with_memory_space_constraint(one, pltpu.HBM) if spec is HBM else one
+            for one, spec in zip(operands, specs)
+        ]
         return pl.pallas_call(
             functools.partial(kernel, sizes),
             out_shape=out_shape,
             in_specs=specs,
-            out_specs=jax.tree.map(lambda _: VMEM, out_shape),
+            out_specs=jax.tree.map(lambda _: out_spec, out_shape),
             scratch_shapes=list(scratch),
+            input_output_aliases=aliases,
             compiler_params=pltpu.CompilerParams(vmem_limit_bytes=48 * 1024 * 1024),
             name=name,
         )(*operands)
 
-    scalars = (fringe_counts, coupling)
-    fringe = (donor_cells, donor_offsets, receptor_cells)
+    scalars = (coupling, plane_of_slot)
+    offsets = donor_offsets.transpose(0, 2, 1, 3)
+    inputs = (fringe_counts, coarse_diagonal, donor_cells, offsets, receptor_cells)
     shared = call(
         pack_kernel,
         "pack",
         jax.ShapeDtypeStruct((planes * variables + 1, height, depth), F32),
         scalars,
-        fringe_counts,
-        coarse_diagonal,
-        *fringe,
-    )
+        *inputs,
+        far=inputs,
+        scratch=[
+            pltpu.VMEM(coarse, F32),
+            pltpu.VMEM(offsets.shape[1:], F32),
+            pltpu.VMEM((2, 1, slots), jnp.int32),
+            pltpu.SMEM(fringe_counts.shape, jnp.int32),
+            pltpu.SemaphoreType.DMA((5,)),
+        ],
+    )
+    mine = shared
     shared = spread_over_sub(shared, bits)
-    own = call(
-        restrict_kernel,
-        "restrict",
-        jax.ShapeDtypeStruct((2 * count + 1, height, depth), F32),
-        scalars,
-        fine_residual,
-        fine_solution,
-        plane_of_slot,
-        scratch=[pltpu.VMEM((count, 2 * height, depth), F32)],
-    )
     corners = call(
         corner_kernel,
         "corners",
         jax.ShapeDtypeStruct((grids, 8, LANES), F32),
         scalars,
-        fringe_counts,
-        coarse_diagonal,
-        *fringe,
+        mine,
+    )
+    own = call(
+        restrict_kernel,
+        "restrict",
+        jax.ShapeDtypeStruct((2 * count + 1, height, depth), F32),
+        (),
+        fine_residual,
+        fine_solution,
+        plane_of_slot,
+        corners,
+        shared[2],
+        far=(fine_residual, fine_solution),
+        scratch=[
+            pltpu.VMEM((2,) + fine_solution.shape[1:], F32),
+            pltpu.VMEM((2 * count, 2 * height, depth), F32),
+            pltpu.SemaphoreType.DMA((blocks,)),
+        ],
     )
     every = spread_over_sub(own, bits)
-    scalars = scalars + (plane_of_slot,)
     out, gain, mask = call(
         partial_kernel,
         "partial",
@@ -710,7 +814,10 @@
             rows,
             pltpu.VMEM((total + 2, variables, height, depth), F32),
             pltpu.VMEM((count, 2 * height, depth), F32),
+            pltpu.VMEM(fine_solution.shape[1:], F32),
+            pltpu.SemaphoreType.DMA((blocks // 2,)),
         ],
+        out_spec=HBM,
     )
 
 

time: 35.9 us -> 31.7 us (0.88)
  local copies, waits for them, and re-layouts: 4.48 us -> 0.02 us
  waiting for transfers between devices: 8.46 us -> 9.74 us
  Pallas kernels: 12 us -> 11.5 us
  starting transfers between devices: 10.5 us -> 10.1 us
    unnamed x23 -> x6, local copies, waits for them, and re-layouts: 4.48 us -> 0.02 us
    ppermute x6, waiting for transfers between devices: 1.61 us -> 2.88 us  [spread_over_sub(): held = held + [lax.ppermute(one, 'sub', pairs) for one in held]]
    all_to_all x1, starting transfers between devices: 6.28 us -> 5.67 us  [fast_shards(): arrived = lax.all_to_all(out, ('grid', 'sub'), 0, 0, tiled=True)]
    pallas_call x6, Pallas kernels: 12 us -> 11.5 us  [call(): pl.pallas_call(functools.partial(kernel, sizes), out_shape=out_shape, in_...]
  transfers between devices with their start and end apart: 7 -> 7, of which waited for: 3 -> 4; matrix products, arithmetic and copies ran while one was open for 0% -> 0% of each run, Pallas kernels for 18% -> 21%
where the time goes in v3:
time: 31.7 us; the launch traced here: 31.5 us
  Pallas kernels  11.5 us (36%)
  starting transfers between devices  10.1 us (32%)
  waiting for transfers between devices  9.74 us (31%)
    pallas_call x6, Pallas kernels, call(): pl.pallas_call(functools.partial(kernel, sizes), out_shape=out_shape, in_...  11.5 us
    all_to_all x1, waiting for transfers between devices, fast_shards(): arrived = lax.all_to_all(out, ('grid', 'sub'), 0, 0, tiled=True)  6.85 us
    all_to_all x1, starting transfers between devices, fast_shards(): arrived = lax.all_to_all(out, ('grid', 'sub'), 0, 0, tiled=True)  5.67 us
    ppermute x6, starting transfers between devices, spread_over_sub(): held = held + [lax.ppermute(one, 'sub', pairs) for one in held]  4.45 us
    ppermute x6, waiting for transfers between devices, spread_over_sub(): held = held + [lax.ppermute(one, 'sub', pairs) for one in held]  2.88 us
  transfers between devices with their start and end apart: 7, of which 4 were waited for; matrix products, arithmetic and copies ran while one was open for 0% of the time, Pallas kernels for 21%

profile of v3, /device:TPU:0, one launch (start us, length us, event | category | flops | bytes accessed | tf_op | source)
XLA Modules:
  0.0 31.5 jit_solution(3929818329758294016)
XLA Ops:
  0.0 1.0 %pack.1.shared.refs_0_ = f32[21,8,128]{2,1,0:T(8,128)S(1)} custom-call(s32[8,8]{1,0:T(8,128)} %counts.1, f32[1,4,5,8,128]{4,3,2,1,0:T(8,128)} %diagonal.1, s32[1,1,64]{2,1,0:T(1,128)} %donors.1, f32[1,3,1,64]{3,2,1,0:T(1,128)} %bitcast.1, s32[1,1,64]{2,1,0:T(1,128)} %receptors.1), custom_call_target="tpu_custom_call" | custom-call | tf_op jit(solution)/shard_map/pack/pallas_call | solution.py:715
  1.0 0.0 copy-start.2
  1.0 0.5 %collective-permute-start.1 = (f32[21,8,128]{2,1,0:T(8,128)S(1)}, f32[21,8,128]{2,1,0:T(8,128)S(1)}, u32[]{:S(2)}, u32[]{:S(2)}) collective-permute-start(f32[21,8,128]{2,1,0:T(8,128)S(1)} %pack.1.shared.refs_0_), channel_id=1, source_target_pairs={{0,1},{1,0},{2,3},{3,2},{4,5},{5,4},{6,7},{7,6},{8,9},{9,8},{10,11... | collective-permute-start | bytes 258056 | tf_op jit(solution)/shard_map/ppermute | solution.py:671
  1.5 2.6 %collective-permute-start = (f32[21,8,128]{2,1,0:T(8,128)S(1)}, f32[21,8,128]{2,1,0:T(8,128)S(1)}, u32[]{:S(2)}, u32[]{:S(2)}) collective-permute-start(f32[21,8,128]{2,1,0:T(8,128)S(1)} %pack.1.shared.refs_0_), channel_id=1, source_target_pairs={{0,2},{1,3},{2,0},{3,1},{4,6},{5,7},{6,4},{7,5},{8,10},{9,11},{10,... | collective-permute-start | bytes 258056 | tf_op jit(solution)/shard_map/ppermute | solution.py:671
  4.1 0.5 %corners.1.first.refs_6_ = f32[8,8,128]{2,1,0:T(8,128)S(1)} custom-call(f32[21,8,128]{2,1,0:T(8,128)S(1)} %pack.1.shared.refs_0_), custom_call_target="tpu_custom_call" | custom-call | tf_op jit(solution)/shard_map/corners/pallas_call | solution.py:715
  4.6 0.0 collective-permute-done.1.second.refs_2_
  4.6 0.0 copy-done.2
  4.6 2.3 %restrict.1.refs_5_.refs_0_ = f32[81,8,128]{2,1,0:T(8,128)S(1)} custom-call(f32[1,8,5,16,256]{4,3,2,1,0:T(8,128)} %residual.1, f32[1,8,5,16,256]{4,3,2,1,0:T(8,128)} %refs_12_.1, s32[1,8]{1,0:T(1,128)S(1)} %copy-done.2, f32[8,8,128]{2,1,0:T(8,128)S(1)} %corners.1.first.refs_6_, f32[21,8,128]{2,1,0:T(8,128)S(1)} %collective-permute-done.1.second.refs_2_), custom_call_target="tpu_custom_call" | custom-call | tf_op jit(solution)/shard_map/restrict/pallas_call | solution.py:715
  6.9 0.8 %collective-permute-start.3 = (f32[81,8,128]{2,1,0:T(8,128)S(1)}, f32[81,8,128]{2,1,0:T(8,128)S(1)}, u32[]{:S(2)}, u32[]{:S(2)}) collective-permute-start(f32[81,8,128]{2,1,0:T(8,128)S(1)} %restrict.1.refs_5_.refs_0_), channel_id=1, source_target_pairs={{0,2},{1,3},{2,0},{3,1},{4,6},{5,7},{6,4},{7,5},{8,10},{9,11},{10,... | collective-permute-start | bytes 995336 | tf_op jit(solution)/shard_map/ppermute | solution.py:671
  7.7 0.0 collective-permute-done.refs_1_
  7.7 0.0 collective-permute-start.2
  7.7 1.3 %collective-permute-done.2.refs_3_ = f32[21,8,128]{2,1,0:T(8,128)S(1)} collective-permute-done((f32[21,8,128]{2,1,0:T(8,128)S(1)}, f32[21,8,128]{2,1,0:T(8,128)S(1)}, u32[]{:S(2)}, u32[]{:S(2)}) %collective-permute-start.2) | collective-permute-done | bytes 86048 | tf_op jit(solution)/shard_map/ppermute | solution.py:671
  9.0 2.4 %partial.1 = (f32[32,16,128]{2,1,0:T(8,128)}, f32[16,5,8,128]{3,2,1,0:T(8,128)S(1)}, f32[16,1,8,128]{3,2,1,0:T(8,128)S(1)}) custom-call(f32[21,8,128]{2,1,0:T(8,128)S(1)} %pack.1.shared.refs_0_, f32[21,8,128]{2,1,0:T(8,128)S(1)} %collective-permute-done.refs_1_, f32[21,8,128]{2,1,0:T(8,128)S(1)} %collective-permute-done.1.second.refs_2_, ...), custom_call_target="tpu_custom_call" | custom-call | tf_op jit(solution)/shard_map/partial/pallas_call | solution.py:715
  11.4 5.7 %all-to-all-start = ((f32[32,16,128]{2,1,0:T(8,128)}), f32[32,16,128]{2,1,0:T(8,128)S(1)}, u32[]{:S(2)}, u32[]{:S(2)}) async-start(f32[32,16,128]{2,1,0:T(8,128)} %get-tuple-element.11), calls=%async_computation | async-start | bytes 524288 | tf_op jit(solution)/shard_map/all_to_all | solution.py:786
  17.0 0.0 copy-start
  17.1 0.3 %collective-permute-start.4 = (f32[81,8,128]{2,1,0:T(8,128)S(1)}, f32[81,8,128]{2,1,0:T(8,128)S(1)}, u32[]{:S(2)}, u32[]{:S(2)}) collective-permute-start(f32[81,8,128]{2,1,0:T(8,128)S(1)} %restrict.1.refs_5_.refs_0_), channel_id=1, source_target_pairs={{0,1},{1,0},{2,3},{3,2},{4,5},{5,4},{6,7},{7,6},{8,9},{9,8},{10,11... | collective-permute-start | bytes 995336 | tf_op jit(solution)/shard_map/ppermute | solution.py:671
  17.4 0.0 collective-permute-done.3.refs_1_
  17.4 0.3 collective-permute-start.5
  17.6 1.1 %collective-permute-done.4.refs_2_ = f32[81,8,128]{2,1,0:T(8,128)S(1)} collective-permute-done((f32[81,8,128]{2,1,0:T(8,128)S(1)}, f32[81,8,128]{2,1,0:T(8,128)S(1)}, u32[]{:S(2)}, u32[]{:S(2)}) %collective-permute-start.4) | collective-permute-done | bytes 331808 | tf_op jit(solution)/shard_map/ppermute | solution.py:671
  18.8 0.5 %collective-permute-done.5.refs_3_ = f32[81,8,128]{2,1,0:T(8,128)S(1)} collective-permute-done((f32[81,8,128]{2,1,0:T(8,128)S(1)}, f32[81,8,128]{2,1,0:T(8,128)S(1)}, u32[]{:S(2)}, u32[]{:S(2)}) %collective-permute-start.5) | collective-permute-done | bytes 331808 | tf_op jit(solution)/shard_map/ppermute | solution.py:671
  19.2 0.0 copy-done.1
  19.2 1.5 %assemble.1 = (f32[16,5,8,128]{3,2,1,0:T(8,128)S(1)}, f32[16,5,8,128]{3,2,1,0:T(8,128)S(1)}, f32[16,5,8,128]{3,2,1,0:T(8,128)S(1)}) custom-call(f32[81,8,128]{2,1,0:T(8,128)S(1)} %restrict.1.refs_5_.refs_0_, f32[81,8,128]{2,1,0:T(8,128)S(1)} %collective-permute-done.3.refs_1_, f32[81,8,128]{2,1,0:T(8,128)S(1)} %collective-permute-done.4.refs_2_, ...), custom_call_target="tpu_custom_call" | custom-call | tf_op jit(solution)/shard_map/assemble/pallas_call | solution.py:715
  20.8 6.9 %all-to-all-done.refs_6_ = f32[32,16,128]{2,1,0:T(8,128)S(1)} async-done(((f32[32,16,128]{2,1,0:T(8,128)}), f32[32,16,128]{2,1,0:T(8,128)S(1)}, u32[]{:S(2)}, u32[]{:S(2)}) %all-to-all-start) | async-done | bytes 262176 | tf_op jit(solution)/shard_map/all_to_all | solution.py:786
  27.6 3.8 %finish.1 = f32[1,8,5,16,256]{4,3,2,1,0:T(8,128)} custom-call(f32[21,8,128]{2,1,0:T(8,128)S(1)} %pack.1.shared.refs_0_, f32[21,8,128]{2,1,0:T(8,128)S(1)} %collective-permute-done.refs_1_, f32[21,8,128]{2,1,0:T(8,128)S(1)} %collective-permute-done.1.second.refs_2_, f32[21,8,128]{2,1,0:T(8,128)S(1)} %collective-permute-done.2.refs_3_, f32[5,5]{1,0:T(8,128)S(1)} %copy-done.1, ...), custom_call_target="tpu_custom_call" | custom-call | tf_op jit(solution)/shard_map/finish/pallas_call | solution.py:715
  (2 shorter events, 0.0 us)
Async XLA Ops:
  1.0 3.6 %copy-start.2 = (s32[1,8]{1,0:T(1,128)S(1)}, s32[1,8]{1,0:T(1,128)}, u32[]{:S(2)}) copy-start(s32[1,8]{1,0:T(1,128)} %refs_5_.1) | copy-start | bytes 100
  1.0 3.6 %collective-permute-start.1 = (f32[21,8,128]{2,1,0:T(8,128)S(1)}, f32[21,8,128]{2,1,0:T(8,128)S(1)}, u32[]{:S(2)}, u32[]{:S(2)}) collective-permute-start(f32[21,8,128]{2,1,0:T(8,128)S(1)} %pack.1.shared.refs_0_), channel_id=1, source_target_pairs={{0,1},{1,0},{2,3},{3,2},{4,5},{5,4},{6,7},{7,6},{8,9},{9,8},{10,11... | collective-permute-start | bytes 258056 | tf_op jit(solution)/shard_map/ppermute | solution.py:671
  1.5 6.1 %collective-permute-start = (f32[21,8,128]{2,1,0:T(8,128)S(1)}, f32[21,8,128]{2,1,0:T(8,128)S(1)}, u32[]{:S(2)}, u32[]{:S(2)}) collective-permute-start(f32[21,8,128]{2,1,0:T(8,128)S(1)} %pack.1.shared.refs_0_), channel_id=1, source_target_pairs={{0,2},{1,3},{2,0},{3,1},{4,6},{5,7},{6,4},{7,5},{8,10},{9,11},{10,... | collective-permute-start | bytes 258056 | tf_op jit(solution)/shard_map/ppermute | solution.py:671
  6.9 10.5 %collective-permute-start.3 = (f32[81,8,128]{2,1,0:T(8,128)S(1)}, f32[81,8,128]{2,1,0:T(8,128)S(1)}, u32[]{:S(2)}, u32[]{:S(2)}) collective-permute-start(f32[81,8,128]{2,1,0:T(8,128)S(1)} %restrict.1.refs_5_.refs_0_), channel_id=1, source_target_pairs={{0,2},{1,3},{2,0},{3,1},{4,6},{5,7},{6,4},{7,5},{8,10},{9,11},{10,... | collective-permute-start | bytes 995336 | tf_op jit(solution)/shard_map/ppermute | solution.py:671
  7.7 1.3 %collective-permute-start.2 = (f32[21,8,128]{2,1,0:T(8,128)S(1)}, f32[21,8,128]{2,1,0:T(8,128)S(1)}, u32[]{:S(2)}, u32[]{:S(2)}) collective-permute-start(f32[21,8,128]{2,1,0:T(8,128)S(1)} %collective-permute-done.refs_1_), channel_id=1, source_target_pairs={{0,1},{1,0},{2,3},{3,2},{4,5},{5,4},{6,7},{7,6},{8,9},{9,8},{10,11... | collective-permute-start | bytes 258056 | tf_op jit(solution)/shard_map/ppermute | solution.py:671
  11.4 7.9 %copy-start.1 = (f32[5,5]{1,0:T(8,128)S(1)}, f32[5,5]{1,0:T(8,128)}, u32[]{:S(2)}) copy-start(f32[5,5]{1,0:T(8,128)} %refs_4_.5) | copy-start | bytes 304
  11.4 16.3 %all-to-all-start = ((f32[32,16,128]{2,1,0:T(8,128)}), f32[32,16,128]{2,1,0:T(8,128)S(1)}, u32[]{:S(2)}, u32[]{:S(2)}) async-start(f32[32,16,128]{2,1,0:T(8,128)} %get-tuple-element.11), calls=%async_computation | async-start | bytes 524288 | tf_op jit(solution)/shard_map/all_to_all | solution.py:786
  17.0 10.6 %copy-start = (f32[1,8,5,16,256]{4,3,2,1,0:T(8,128)S(1)}, f32[1,8,5,16,256]{4,3,2,1,0:T(8,128)}, u32[]{:S(2)}) copy-start(f32[1,8,5,16,256]{4,3,2,1,0:T(8,128)} %refs_12_.1) | copy-start | bytes 1966084
  17.1 1.7 %collective-permute-start.4 = (f32[81,8,128]{2,1,0:T(8,128)S(1)}, f32[81,8,128]{2,1,0:T(8,128)S(1)}, u32[]{:S(2)}, u32[]{:S(2)}) collective-permute-start(f32[81,8,128]{2,1,0:T(8,128)S(1)} %restrict.1.refs_5_.refs_0_), channel_id=1, source_target_pairs={{0,1},{1,0},{2,3},{3,2},{4,5},{5,4},{6,7},{7,6},{8,9},{9,8},{10,11... | collective-permute-start | bytes 995336 | tf_op jit(solution)/shard_map/ppermute | solution.py:671
  17.4 1.9 %collective-permute-start.5 = (f32[81,8,128]{2,1,0:T(8,128)S(1)}, f32[81,8,128]{2,1,0:T(8,128)S(1)}, u32[]{:S(2)}, u32[]{:S(2)}) collective-permute-start(f32[81,8,128]{2,1,0:T(8,128)S(1)} %collective-permute-done.3.refs_1_), channel_id=1, source_target_pairs={{0,1},{1,0},{2,3},{3,2},{4,5},{5,4},{6,7},{7,6},{8,9},{9,8},{10,11... | collective-permute-start | bytes 995336 | tf_op jit(solution)/shard_map/ppermute | solution.py:671

commit v4 on v3

--- a/solution.py
+++ b/solution.py
@@ -187,7 +187,6 @@
 SMEM = pl.BlockSpec(memory_space=pltpu.SMEM)
 HBM = pl.BlockSpec(memory_space=pltpu.HBM)
 LANES = 128
-WET = 1 << 20
 
 
 def two_pieces(values):
@@ -319,9 +318,9 @@
 def corner_kernel(sizes, shared, out):
     planes, variables, height, depth = sizes["coarse"]
     slots, grids = sizes["slots"], sizes["grids"]
-    sub_index = lax.axis_index("sub")
+    grid_index = lax.axis_index("grid")
+    base = lax.axis_index("sub") * (planes * height * depth)
     meta = shared[planes * variables, :, 0:slots]
-    base = sub_index * (planes * height * depth)
     cell = meta[4:5].astype(jnp.int32)
     cell = jnp.where(cell >= 0, cell - base, -1)
     mask, _, _ = receptor_mask(cell, planes, height, depth)
@@ -338,7 +337,7 @@
     both = jnp.concatenate([meta[1:4], meta[1:4]], axis=1)
     weight_z = jnp.where(step_z == 1, both[2:3], 1.0 - both[2:3])
     at_row = iota((height, LANES), 0)
-    empty = jnp.zeros((1, LANES), F32)
+    empty = jnp.zeros((5, LANES), F32)
     tiles = []
     for step_x in (0, 1):
         weight_x = both[0:1] if step_x else 1.0 - both[0:1]
@@ -350,26 +349,27 @@
             weight_y = both[1:2] if step_y else 1.0 - both[1:2]
             here = jnp.where(at_row == row + step_y, 1.0, 0.0)
             found = jnp.sum(by_plane * here[None], axis=1)
-            weight = weight_x * weight_y * weight_z
             wet = found[variables : variables + 1]
-            scaled = weight * (found[:variables] * (1.0 - wet) + wet)
-            number = twice + base + (step_x * height + step_y) * depth + step_z
-            number = number.astype(F32) + wet * float(WET)
-            tiles.append(jnp.concatenate([empty, empty, scaled, number], axis=0))
+            scaled = weight_x * weight_y * weight_z * (found[:variables] * (1.0 - wet) + wet)
+            left = jnp.concatenate([empty, scaled[0:3]], axis=0)
+            right = jnp.concatenate([empty, scaled[3:5], empty[0:1]], axis=0)
+            tiles.append((left, right))
     lane = iota((8, LANES), 1)
     sublane = iota((8, LANES), 0)
-    number = meta[4:5]
-    number = jnp.broadcast_to(jnp.concatenate([number, number], axis=1), (8, LANES))
-    half = slots // 2
-    moved = jnp.where(sublane == 2, pltpu.roll(number, half, 1), number)
-    targets = (sublane == 2) | (sublane == 3)
-    targets = targets & (lane >= half) & (lane < slots)
+    cells = jnp.broadcast_to(jnp.concatenate([meta[4:5], meta[4:5]], axis=1), (8, LANES))
+    starts = jnp.broadcast_to(jnp.concatenate([meta[0:1], meta[0:1]], axis=1), (8, LANES))
+    starts = pltpu.roll(starts, 8 * grid_index, 1)
+    last = (sublane == 7) & (lane >= 64)
+    mine = last & (lane % 64 // 8 == grid_index)
     for h in range(grids):
         tile = jnp.zeros((8, LANES), F32)
         for c in range(8):
-            shift = (64 + 8 * c - (c % 2) * 64 - 8 * h) % LANES
-            tile = jnp.where(lane // 8 == 8 + c, pltpu.roll(tiles[c // 2], shift, 1), tile)
-        out[h] = jnp.where(targets, moved, tile)
+            for k in (0, 1):
+                shift = (64 * k + 8 * c - (c % 2) * 64 - 8 * h) % LANES
+                moved = pltpu.roll(tiles[c // 2][k], shift, 1)
+                tile = jnp.where(lane // 8 == 8 * k + c, moved, tile)
+        tile = jnp.where(last, cells, tile)
+        out[h] = jnp.where(mine, pltpu.roll(starts, (LANES - 8 * h) % LANES, 1), tile)
 
 
 def hats(shape, dim, start, frac):
@@ -400,75 +400,89 @@
     subs, grids, slots, blocks = sizes["subs"], sizes["grids"], sizes["slots"], sizes["blocks"]
     planes, variables, height, depth = sizes["coarse"]
     parts = refs[:subs]
-    ids, own, corners = refs[subs : subs + 3]
-    out, gain, mask_out, rows, stage, both = refs[subs + 3 :]
+    ids, own, mate, corners = refs[subs : subs + 4]
+    out, gain, mask_out, both, rows, stage, numbers, sem = refs[subs + 4 :]
     total = subs * planes
     sub_index = lax.axis_index("sub")
+    grid_index = lax.axis_index("grid")
     count = planes * variables
+    fine_count = blocks * variables
+    copy = pltpu.make_async_copy(mate.at[2 * fine_count, 0:1, :], numbers, sem)
+    copy.start()
     for i, part in enumerate(parts):
         owner = sub_index ^ sizes["order"][i]
         stage[owner] = part[count]
         gain[pl.ds(owner * planes, planes)] = part[0:count].reshape(sizes["coarse"])
     for j in range(subs):
         rows[:, j * slots : (j + 1) * slots] = stage[j, :, 0:slots]
-    both[...] = jnp.zeros(both.shape, F32)
-    fine_count = blocks * variables
-    for q in range(blocks):
-        coarse = ids[0, q] // 2
-        for k in range(2):
-            at = k * fine_count + q * variables
-            here = pl.ds(k * variables, variables)
-            both[pl.ds(coarse, 1), here] += own[at : at + variables][None]
     mask, _, _ = receptor_mask(rows[4:5, :].astype(jnp.int32), total, height, depth)
     mask_out[...] = mask
+    both[...] = jnp.zeros(both.shape, F32)
+    add_planes(sizes, own, ids, both)
+    copy.wait()
+    add_planes(sizes, mate, numbers, both)
     restricted = both[:, 0:variables]
     residual = both[:, variables:]
     wet = mask > 0.5
     beside = neighbour_sum(jnp.where(wet, restricted, 0.0))
     swept = jnp.where(wet, 0.0, restricted + gain[...] * (residual - beside))
-    values = interpolate(jnp.concatenate([restricted, swept], axis=1), rows)
-    first, second = values[:variables], values[variables:]
-    empty = jnp.zeros((1, LANES), F32)
-    top = jnp.concatenate([first[:, 0:LANES], first[0:3, LANES:]], axis=0)
-    low = jnp.concatenate([first[3:5, LANES:], second[:, 0:LANES], empty], axis=0)
-    high = jnp.concatenate([empty, empty, second[:, LANES:], empty], axis=0)
-    lane = iota((8, LANES), 1)
-    sublane = iota((8, LANES), 0)
-    values_at = (sublane >= 2) & (sublane < 7)
+    half = jnp.where(sub_index % 2 == 0, rows[:, 0:LANES], rows[:, LANES:])
+    values = interpolate(jnp.concatenate([restricted, swept], axis=1), half)
+    empty = jnp.zeros((3, LANES), F32)
+    first = jnp.concatenate([values[:variables], empty], axis=0)
+    second = jnp.concatenate([values[variables:], empty], axis=0)
+    second = pltpu.roll(second, 8 * grid_index, 1)
+    mine = iota((8, LANES), 1) % 64 // 8 == grid_index
+    top = iota((8, LANES), 0) < variables
     for h in range(grids):
-        tile = jnp.where(sublane < 2, low, corners[h])
+        tile = jnp.where(mine, pltpu.roll(second, (LANES - 8 * h) % LANES, 1), first)
+        tile = jnp.where(top, tile, corners[h])
         for s in range(subs):
-            source = low if s < 2 else high
-            moved = pltpu.roll(source, (8 * s - 8 * h - 64 * (s % 2)) % LANES, 1)
-            tile = jnp.where(values_at & (lane // 8 == s), moved, tile)
-        for s in range(subs):
-            out[h * subs + s, 0:8] = top
-            out[h * subs + s, 8:16] = tile
-
-
-def assemble_kernel(sizes, *refs):
-    subs, blocks = sizes["subs"], sizes["blocks"]
-    planes, variables, height, depth = sizes["coarse"]
-    parts = refs[:subs]
-    coupling, restricted, residual, source, numbers, sems = refs[subs:]
+            out[h * subs + s] = tile
+
+
+def add_planes(sizes, part, numbers, both):
+    variables = sizes["coarse"][1]
+    count = sizes["blocks"] * variables
+    for q in range(sizes["blocks"]):
+        coarse = pl.ds(numbers[0, q].astype(jnp.int32) // 2, 1)
+        for k in range(2):
+            at = k * count + q * variables
+            both[coarse, pl.ds(k * variables, variables)] += part[at : at + variables][None]
+
+
+def split_kernel(sizes, whole, *pieces):
+    at = 0
+    for piece in pieces:
+        piece[...] = whole[at : at + piece.shape[0]]
+        at = at + piece.shape[0]
+
+
+def assemble_kernel(sizes, known, across, *refs):
+    variables = sizes["coarse"][1]
+    blocks = sizes["blocks"]
     count = blocks * variables
-    copies = [
-        pltpu.make_async_copy(part.at[2 * count, 0:1, :], numbers.at[i : i + 1, :], sems.at[i])
-        for i, part in enumerate(parts)
-    ]
-    for copy in copies:
-        copy.start()
-    restricted[...] = jnp.zeros(restricted.shape, F32)
-    residual[...] = jnp.zeros(residual.shape, F32)
-    for copy in copies:
-        copy.wait()
-    for i, part in enumerate(parts):
-        for q in range(blocks):
-            coarse = pl.ds(numbers[i, q].astype(jnp.int32) // 2, 1)
-            at = q * variables
-            restricted[coarse] += part[at : at + variables][None]
-            residual[coarse] += part[count + at : count + at + variables][None]
-    source[...] = couple(coupling, restricted[...])
+    pieces = refs[:-5]
+    coupling, both, source, numbers, sems = refs[-5:]
+    width = pieces[0].shape[0] // variables
+    copies = start_copies(
+        [
+            (across.at[2 * count, 0:1, :], numbers.at[0]),
+            (pieces[-1].at[width * variables, 0:1, :], numbers.at[1]),
+        ],
+        sems,
+    )
+    both[...] = known[...]
+    copies[0].wait()
+    add_planes(sizes, across, numbers.at[0], both)
+    copies[1].wait()
+    for q in range(2 * blocks):
+        k, slot = divmod(q, blocks)
+        coarse = pl.ds(numbers[1, 0, slot].astype(jnp.int32) // 2, 1)
+        at = q % width * variables
+        part = pieces[q // width][at : at + variables]
+        both[coarse, pl.ds(k * variables, variables)] += part[None]
+    source[...] = couple(coupling, both[:, 0:variables])
 
 
 def couple(coupling, field):
@@ -492,13 +506,12 @@
     return jnp.concatenate([each.astype(F32) for each in rows], axis=0)
 
 
-def corner_features(number, height, depth):
-    wet = jnp.where(number >= WET, 1, 0)
-    plane, row, column = split_cell(number - WET * wet, height, depth)
+def corner_features(cell, height, depth):
+    plane, row, column = split_cell(cell, height, depth)
     square = plane * plane + row * row + column * column
     coarse = square // LANES * LANES
-    one = jnp.ones(number.shape, jnp.int32)
-    rows = [2 * plane, 2 * row, 2 * column, -coarse, coarse - square, -wet, one, one]
+    one = jnp.ones(cell.shape, jnp.int32)
+    rows = [2 * plane, 2 * row, 2 * column, -coarse, coarse - square, 0 * one, one, one]
     return jnp.concatenate([each.astype(F32) for each in rows], axis=0)
 
 
@@ -510,45 +523,53 @@
     group = lane % 64 // 8
     firsts = []
     for g in range(grids):
-        top = arrived[g * subs, 0:8]
-        last = arrived[g * subs, 8:16]
-        for s in range(1, subs):
-            top = top + arrived[g * subs + s, 0:8]
-            last = last + arrived[g * subs + s, 8:16]
-        right = jnp.where(sublane < 3, pltpu.roll(top, 3, 0), pltpu.roll(last, 3, 0))
-        firsts.append(((top, right), last))
+        halves = []
+        for k in range(2):
+            half = arrived[g * subs + k]
+            for s in range(k + 2, subs, 2):
+                half = half + arrived[g * subs + s]
+            halves.append(half)
+        firsts.append(halves)
     for g in range(grids):
         for k in range(2):
-            sent = jnp.zeros((8, LANES), F32)
+            sent = firsts[g][k]
             for other in range(grids):
-                moved = pltpu.roll(firsts[other][0][k], (8 * other - 8 * g) % LANES, 1)
-                sent = jnp.where(group == other, moved, sent)
+                if other != g:
+                    moved = pltpu.roll(firsts[other][k], (8 * other - 8 * g) % LANES, 1)
+                    sent = jnp.where(group == other, moved, sent)
             landing[g, :, k * LANES : (k + 1) * LANES] = sent
-    targets = [jnp.zeros((8, LANES), F32)] * 2
-    numbers = [jnp.zeros((8, LANES), F32)] * 2
+    cells = [jnp.zeros((8, LANES), F32)] * 2
     scales = []
     for g in range(grids):
-        tiles = [arrived[g * subs + s, 8:16] for s in range(subs)]
         scale = []
         for k in range(2):
-            one, two = tiles[2 * k], tiles[2 * k + 1]
-            scale.append(jnp.where(lane < 64, pltpu.roll(one, 64, 1), two))
-            left = jnp.where(lane < 32, pltpu.roll(pltpu.roll(one, 96, 1), 1, 0), one)
-            right = pltpu.roll(two, 64, 1)
-            right = jnp.where(lane < 96, pltpu.roll(pltpu.roll(two, 32, 1), 1, 0), right)
-            target = jnp.where(lane < 64, left, right)
-            targets[k] = jnp.where(sublane == g, pltpu.roll(target, (g + 5) % 8, 0), targets[k])
-            number = pltpu.roll(scale[k], (g + 1) % 8, 0)
-            numbers[k] = jnp.where(sublane == g, number, numbers[k])
+            one, two = arrived[g * subs + 2 * k], arrived[g * subs + 2 * k + 1]
+            low = jnp.where(lane < 64, one, pltpu.roll(two, 64, 1))
+            high = jnp.where(lane < 64, pltpu.roll(one, 64, 1), two)
+            scale.append(jnp.where(sublane < 3, pltpu.roll(low, 3, 0), pltpu.roll(high, 6, 0)))
+            cells[k] = jnp.where(sublane == g, pltpu.roll(high, (g + 1) % 8, 0), cells[k])
         scales.append(scale)
+    targets, corners = [], []
+    step = ((group // 4) * height + group // 2 % 2) * depth + group % 2
+    for k in range(2):
+        targets.append(jnp.where(group == sublane, -1.0, cells[k]))
+        starts = jnp.where(group == sublane, cells[k], 0.0)
+        parts = []
+        for half in (lane < 64, lane >= 64):
+            start = jnp.where(half, starts, 0.0)
+            for shift in (64, 32, 16, 8):
+                start = start + pltpu.roll(start, shift, 1)
+            parts.append(start)
+        corners.append(jnp.where(lane < 64, parts[0], parts[1]).astype(jnp.int32) + step)
     targets = jnp.concatenate(targets, axis=1).astype(jnp.int32)
-    numbers = jnp.concatenate(numbers, axis=1).astype(jnp.int32)
+    corners = jnp.concatenate(corners, axis=1)
     theirs = target_features(targets, height, depth).T.astype(BF16)
-    ours = corner_features(numbers, height, depth)
+    ours = corner_features(corners, height, depth)
     which = iota(ours.shape, 0) % 8
     mine = [jnp.where(which == g, ours, 0.0).astype(BF16) for g in range(grids)]
     closeness = jnp.dot(theirs, jnp.concatenate(mine, axis=1), preferred_element_type=F32)
-    match = jnp.maximum(closeness.astype(BF16), 0.0)
+    wet = jnp.maximum(jnp.max(closeness, axis=0, keepdims=True) - 1.0, 0.0)
+    match = jnp.maximum(closeness - wet, 0.0).astype(BF16)
     lanes = subs * slots
     total = [jnp.zeros((8, LANES), F32), jnp.zeros((8, LANES), F32)]
     for g in range(grids):
@@ -557,18 +578,12 @@
         stacked = jnp.concatenate([high, sent - high], axis=0).astype(BF16)
         near = jnp.dot(stacked, match[:, g * lanes : (g + 1) * lanes], preferred_element_type=F32)
         near = near[0:8] + near[8:16]
-        known = pltpu.roll(firsts[g][1], 6, 0)
         for k in range(2):
-            here = slice(k * LANES, (k + 1) * LANES)
-            scale = pltpu.roll(scales[g][k], 6, 0)
-            value = near[:, here] * scale
-            for step in (32, 16, 8):
-                value = value + pltpu.roll(value, LANES - step, 1)
-            value = pltpu.roll(value, 8 * g, 1)
-            for s in range(2):
-                base = pltpu.roll(known, (64 * s + 8 * g - 16 * k - 8 * s) % LANES, 1)
-                found = (group == g) & (lane // 64 == s)
-                total[k] = jnp.where(found, value + base, total[k])
+            value = near[:, k * LANES : (k + 1) * LANES] * scales[g][k]
+            for shift in (32, 16, 8):
+                value = value + pltpu.roll(value, LANES - shift, 1)
+            value = pltpu.roll(value, 8 * g, 1) + firsts[g][k]
+            total[k] = jnp.where(group == g, value, total[k])
     return landing[lax.axis_index("grid")], jnp.concatenate(total, axis=1)
 
 
@@ -602,12 +617,11 @@
     subs = sizes["subs"]
     planes, variables, height, depth = sizes["coarse"]
     blocks = sizes["blocks"]
+    slots = sizes["slots"]
     parts = refs[:subs]
-    coupling, ids, arrived, restricted, residual, source, gain, mask = refs[subs : subs + 8]
-    fine, out, landing, stage, rows, padded, tall, held, sems = refs[subs + 8 :]
+    coupling, ids, arrived, both, source, gain, mask, fine = refs[subs : subs + 8]
+    out, landing, stage, rows, padded, tall, held, sems = refs[subs + 8 :]
     total = subs * planes
-    slots = sizes["slots"]
-    count = blocks * variables
     sub_index = lax.axis_index("sub")
     for i, part in enumerate(parts):
         stage[sub_index ^ sizes["order"][i]] = part[planes * variables]
@@ -618,10 +632,10 @@
     values = jnp.concatenate([first[:variables], second[:variables]], axis=0)
     landed = spread(values, cell, total, height, depth)
     wet = mask[...] > 0.5
-    start = restricted[...]
+    start = both[:, 0:variables]
+    rest = both[:, variables:]
     scale = gain[...]
-    rest = residual[...]
-    change = jnp.where(wet, landed[:, :variables] - start, 0.0)
+    change = jnp.where(wet, landed[:, 0:variables] - start, 0.0)
     update = scale * (rest + neighbour_sum(change))
     change = jnp.where(wet, landed[:, variables:] - start, update)
     apart = source[...] - couple(coupling, start + change)
@@ -759,7 +773,7 @@
         fine_solution,
         plane_of_slot,
         corners,
-        shared[2],
+        shared[order.index(1)],
         far=(fine_residual, fine_solution),
         scratch=[
             pltpu.VMEM((2,) + fine_solution.shape[1:], F32),
@@ -767,31 +781,54 @@
             pltpu.SemaphoreType.DMA((blocks,)),
         ],
     )
-    every = spread_over_sub(own, bits)
-    out, gain, mask = call(
+    own, shared[1] = lax.optimization_barrier((own, shared[1]))
+    cores = [(i, i ^ 1) for i in range(subs)]
+    mate = lax.ppermute(own, "sub", cores)
+    across = lax.ppermute(own, "sub", [(i, i ^ 2) for i in range(subs)])
+    out, gain, mask, both = call(
         partial_kernel,
         "partial",
         [
-            jax.ShapeDtypeStruct((grids * subs, 16, LANES), F32),
+            jax.ShapeDtypeStruct((grids * subs, 8, LANES), F32),
             full,
             jax.ShapeDtypeStruct((total, 1, height, depth), F32),
+            jax.ShapeDtypeStruct((total, 2 * variables, height, depth), F32),
         ],
         scalars,
         *shared,
         plane_of_slot,
         own,
+        mate,
         corners,
-        scratch=[rows, stage, pltpu.VMEM((total, 2 * variables, height, depth), F32)],
+        scratch=[
+            rows,
+            stage,
+            pltpu.SMEM((1, depth), F32),
+            pltpu.SemaphoreType.DMA,
+        ],
     )
     arrived = lax.all_to_all(out, ("grid", "sub"), 0, 0, tiled=True)
-    restricted, residual, source = call(
+    width = blocks // 2 * variables
+    sizes_of = [width, width, width, 2 * count + 1 - 3 * width]
+    pieces = call(
+        split_kernel,
+        "split",
+        [jax.ShapeDtypeStruct((each, height, depth), F32) for each in sizes_of],
+        (),
+        across,
+    )
+    pieces = [lax.ppermute(piece, "sub", cores) for piece in pieces]
+    both, source = call(
         assemble_kernel,
         "assemble",
-        [full, full, full],
+        [jax.ShapeDtypeStruct(both.shape, F32), full],
         scalars,
-        *every,
+        both,
+        across,
+        *pieces,
         coupling,
-        scratch=[pltpu.SMEM((subs, depth), F32), pltpu.SemaphoreType.DMA((subs,))],
+        aliases={0: 0},
+        scratch=[pltpu.SMEM((2, 1, depth), F32), pltpu.SemaphoreType.DMA((2,))],
     )
     return call(
         finish_kernel,
@@ -802,8 +839,7 @@
         coupling,
         plane_of_slot,
         arrived,
-        restricted,
-        residual,
+        both,
         source,
         gain,
         mask,

time: 31.7 us -> 30.5 us (0.962)
  waiting for transfers between devices: 9.74 us -> 6.98 us
  starting transfers between devices: 10.1 us -> 11.1 us
  Pallas kernels: 11.5 us -> 12 us
    ppermute x0 -> x6, starting transfers between devices: none -> 2.85 us  [the longest x1 1.76 us: fast_shards(): across = lax.ppermute(own, 'sub', [(i, i ^ 2) for i in range(subs)])]
    all_to_all x1, waiting for transfers between devices: 6.85 us -> 4.61 us  [fast_shards(): arrived = lax.all_to_all(out, ('grid', 'sub'), 0, 0, tiled=True)]
    ppermute x6 -> x3, waiting for transfers between devices: 2.88 us -> 1.35 us  [spread_over_sub(): held = held + [lax.ppermute(one, 'sub', pairs) for one in held]]
    ppermute x6 -> x3, starting transfers between devices: 4.45 us -> 3.34 us  [spread_over_sub(): held = held + [lax.ppermute(one, 'sub', pairs) for one in held]]
    ppermute x0 -> x6, waiting for transfers between devices: none -> 1.03 us  [the longest x4 1.02 us: fast_shards(): pieces = [lax.ppermute(piece, 'sub', cores) for piece in pieces]]
    all_to_all x1, starting transfers between devices: 5.67 us -> 4.9 us  [fast_shards(): arrived = lax.all_to_all(out, ('grid', 'sub'), 0, 0, tiled=True)]
    pallas_call x6 -> x7, Pallas kernels: 11.5 us -> 12 us  [call(): pl.pallas_call(functools.partial(kernel, sizes), out_shape=out_shape, in_...]
  transfers between devices with their start and end apart: 7 -> 10, of which waited for: 4 -> 6; matrix products, arithmetic and copies ran while one was open for 0% -> 0% of each run, Pallas kernels for 21% -> 23%
where the time goes in v4:
time: 30.5 us; the launch traced here: 30.2 us
  Pallas kernels  12 us (39%)
  starting transfers between devices  11.1 us (36%)
  waiting for transfers between devices  6.98 us (23%)
    pallas_call x7, Pallas kernels, call(): pl.pallas_call(functools.partial(kernel, sizes), out_shape=out_shape, in_...  12 us
    all_to_all x1, starting transfers between devices, fast_shards(): arrived = lax.all_to_all(out, ('grid', 'sub'), 0, 0, tiled=True)  4.9 us
    all_to_all x1, waiting for transfers between devices, fast_shards(): arrived = lax.all_to_all(out, ('grid', 'sub'), 0, 0, tiled=True)  4.61 us
    ppermute x3, starting transfers between devices, spread_over_sub(): held = held + [lax.ppermute(one, 'sub', pairs) for one in held]  3.34 us
    ppermute x1, starting transfers between devices, fast_shards(): across = lax.ppermute(own, 'sub', [(i, i ^ 2) for i in range(subs)])  1.76 us
    ppermute x3, waiting for transfers between devices, spread_over_sub(): held = held + [lax.ppermute(one, 'sub', pairs) for one in held]  1.35 us
    ppermute x4, starting transfers between devices, fast_shards(): pieces = [lax.ppermute(piece, 'sub', cores) for piece in pieces]  1.09 us
    ppermute x4, waiting for transfers between devices, fast_shards(): pieces = [lax.ppermute(piece, 'sub', cores) for piece in pieces]  1.02 us
  transfers between devices with their start and end apart: 10, of which 6 were waited for; matrix products, arithmetic and copies ran while one was open for 0% of the time, Pallas kernels for 23%

profile of v4, /device:TPU:0, one launch (start us, length us, event | category | flops | bytes accessed | tf_op | source)
XLA Modules:
  0.0 30.2 jit_solution(8776348260363435622)
XLA Ops:
  0.0 1.0 %pack.1.shared.refs_0_ = f32[21,8,128]{2,1,0:T(8,128)S(1)} custom-call(s32[8,8]{1,0:T(8,128)} %counts.1, f32[1,4,5,8,128]{4,3,2,1,0:T(8,128)} %diagonal.1, s32[1,1,64]{2,1,0:T(1,128)} %donors.1, f32[1,3,1,64]{3,2,1,0:T(1,128)} %bitcast.1, s32[1,1,64]{2,1,0:T(1,128)} %receptors.1), custom_call_target="tpu_custom_call" | custom-call | tf_op jit(solution)/shard_map/pack/pallas_call | solution.py:729
  1.0 0.0 copy-start.2
  1.0 0.5 %collective-permute-start = (f32[21,8,128]{2,1,0:T(8,128)S(1)}, f32[21,8,128]{2,1,0:T(8,128)S(1)}, u32[]{:S(2)}, u32[]{:S(2)}) collective-permute-start(f32[21,8,128]{2,1,0:T(8,128)S(1)} %pack.1.shared.refs_0_), channel_id=1, source_target_pairs={{0,1},{1,0},{2,3},{3,2},{4,5},{5,4},{6,7},{7,6},{8,9},{9,8},{10,11... | collective-permute-start | bytes 258056 | tf_op jit(solution)/shard_map/ppermute | solution.py:685
  1.5 2.6 %collective-permute-start.1 = (f32[21,8,128]{2,1,0:T(8,128)S(1)}, f32[21,8,128]{2,1,0:T(8,128)S(1)}, u32[]{:S(2)}, u32[]{:S(2)}) collective-permute-start(f32[21,8,128]{2,1,0:T(8,128)S(1)} %pack.1.shared.refs_0_), channel_id=1, source_target_pairs={{0,2},{1,3},{2,0},{3,1},{4,6},{5,7},{6,4},{7,5},{8,10},{9,11},{10,... | collective-permute-start | bytes 258056 | tf_op jit(solution)/shard_map/ppermute | solution.py:685
  4.1 0.5 %corners.1.first.refs_7_ = f32[8,8,128]{2,1,0:T(8,128)S(1)} custom-call(f32[21,8,128]{2,1,0:T(8,128)S(1)} %pack.1.shared.refs_0_), custom_call_target="tpu_custom_call" | custom-call | tf_op jit(solution)/shard_map/corners/pallas_call | solution.py:729
  4.7 0.0 collective-permute-done.second.refs_2_
  4.7 2.3 %restrict.1.refs_5_ = f32[81,8,128]{2,1,0:T(8,128)S(1)} custom-call(f32[1,8,5,16,256]{4,3,2,1,0:T(8,128)} %residual.1, f32[1,8,5,16,256]{4,3,2,1,0:T(8,128)} %refs_11_.1, s32[1,8]{1,0:T(1,128)S(1)} %copy-done.2, f32[8,8,128]{2,1,0:T(8,128)S(1)} %corners.1.first.refs_7_, f32[21,8,128]{2,1,0:T(8,128)S(1)} %collective-permute-done.second.refs_2_), custom_call_target="tpu_custom_call" | custom-call | tf_op jit(solution)/shard_map/restrict/pallas_call | solution.py:729
  7.0 0.3 collective-permute-done.1.refs_1_
  7.3 1.8 %collective-permute-start.4 = (f32[81,8,128]{2,1,0:T(8,128)S(1)}, f32[81,8,128]{2,1,0:T(8,128)S(1)}, u32[]{:S(2)}, u32[]{:S(2)}) collective-permute-start(f32[81,8,128]{2,1,0:T(8,128)S(1)} %restrict.1.refs_5_), channel_id=1, source_target_pairs={{0,2},{1,3},{2,0},{3,1},{4,6},{5,7},{6,4},{7,5},{8,10},{9,11},{10,... | collective-permute-start | bytes 995336 | tf_op jit(solution)/shard_map/ppermute | solution.py:787
  9.0 0.2 collective-permute-start.2
  9.2 1.1 %collective-permute-done.2.refs_3_ = f32[21,8,128]{2,1,0:T(8,128)S(1)} collective-permute-done((f32[21,8,128]{2,1,0:T(8,128)S(1)}, f32[21,8,128]{2,1,0:T(8,128)S(1)}, u32[]{:S(2)}, u32[]{:S(2)}) %collective-permute-start.2) | collective-permute-done | bytes 86048 | tf_op jit(solution)/shard_map/ppermute | solution.py:685
  10.3 2.7 %partial.1 = (f32[32,8,128]{2,1,0:T(8,128)}, f32[16,5,8,128]{3,2,1,0:T(8,128)S(1)}, f32[16,1,8,128]{3,2,1,0:T(8,128)S(1)}, f32[16,10,8,128]{3,2,1,0:T(8,128)S(1)}) custom-call(f32[21,8,128]{2,1,0:T(8,128)S(1)} %pack.1.shared.refs_0_, f32[21,8,128]{2,1,0:T(8,128)S(1)} %collective-permute-done.1.refs_1_, ...), custom_call_target="tpu_custom_call" | custom-call | tf_op jit(solution)/shard_map/partial/pallas_call | solution.py:729
  13.0 4.9 %all-to-all-start = ((f32[32,8,128]{2,1,0:T(8,128)}), f32[32,8,128]{2,1,0:T(8,128)S(1)}, u32[]{:S(2)}, u32[]{:S(2)}) async-start(f32[32,8,128]{2,1,0:T(8,128)} %get-tuple-element.19), calls=%async_computation | async-start | bytes 262144 | tf_op jit(solution)/shard_map/all_to_all | solution.py:810
  18.0 0.0 copy-start.1
  18.0 0.3 %collective-permute-start.8 = (f32[21,8,128]{2,1,0:T(8,128)S(1)}, f32[21,8,128]{2,1,0:T(8,128)S(1)}, u32[]{:S(2)}, u32[]{:S(2)}) collective-permute-start(f32[21,8,128]{2,1,0:T(8,128)S(1)} %get-tuple-element.24), channel_id=1, source_target_pairs={{0,1},{1,0},{2,3},{3,2},{4,5},{5,4},{6,7},{7,6},{8,9},{9,8},{10,11... | collective-permute-start | bytes 258056 | tf_op jit(solution)/shard_map/ppermute | solution.py:820
  18.3 0.3 collective-permute-start.5
  18.6 0.3 collective-permute-start.6
  18.8 0.3 collective-permute-start.7
  19.1 0.5 %collective-permute-done.5.refs_0_ = f32[20,8,128]{2,1,0:T(8,128)S(1)} collective-permute-done((f32[20,8,128]{2,1,0:T(8,128)S(1)}, f32[20,8,128]{2,1,0:T(8,128)S(1)}, u32[]{:S(2)}, u32[]{:S(2)}) %collective-permute-start.5) | collective-permute-done | bytes 81952 | tf_op jit(solution)/shard_map/ppermute | solution.py:820
  19.6 0.3 collective-permute-done.6.refs_1_
  19.8 0.3 collective-permute-done.7.refs_2_
  20.1 1.4 %assemble.1 = (f32[16,10,8,128]{3,2,1,0:T(8,128)S(1)}, f32[16,5,8,128]{3,2,1,0:T(8,128)S(1)}) custom-call(f32[16,10,8,128]{3,2,1,0:T(8,128)S(1)} %get-tuple-element.20.known, f32[81,8,128]{2,1,0:T(8,128)S(1)} %collective-permute-done.4.whole.across, f32[20,8,128]{2,1,0:T(8,128)S(1)} %collective-permute-done.5.refs_0_, ...), custom_call_target="tpu_custom_call", output_to_operand_aliasing={{0}: (0, {})} | custom-call | tf_op jit(solution)/shard_map/assemble/pallas_call | solution.py:729
  21.6 4.6 %all-to-all-done.refs_6_ = f32[32,8,128]{2,1,0:T(8,128)S(1)} async-done(((f32[32,8,128]{2,1,0:T(8,128)}), f32[32,8,128]{2,1,0:T(8,128)S(1)}, u32[]{:S(2)}, u32[]{:S(2)}) %all-to-all-start) | async-done | bytes 131104 | tf_op jit(solution)/shard_map/all_to_all | solution.py:810
  26.2 4.1 %finish.1 = f32[1,8,5,16,256]{4,3,2,1,0:T(8,128)} custom-call(f32[21,8,128]{2,1,0:T(8,128)S(1)} %pack.1.shared.refs_0_, f32[21,8,128]{2,1,0:T(8,128)S(1)} %collective-permute-done.1.refs_1_, f32[21,8,128]{2,1,0:T(8,128)S(1)} %collective-permute-done.second.refs_2_, f32[21,8,128]{2,1,0:T(8,128)S(1)} %collective-permute-done.2.refs_3_, f32[5,5]{1,0:T(8,128)S(1)} %copy-done.1, ...), custom_call_target="tpu_custom_call" | custom-call | tf_op jit(solution)/shard_map/finish/pallas_call | solution.py:729
  (9 shorter events, 0.0 us)
Async XLA Ops:
  1.0 3.7 %copy-start.2 = (s32[1,8]{1,0:T(1,128)S(1)}, s32[1,8]{1,0:T(1,128)}, u32[]{:S(2)}) copy-start(s32[1,8]{1,0:T(1,128)} %refs_5_.1) | copy-start | bytes 100
  1.0 3.7 %collective-permute-start = (f32[21,8,128]{2,1,0:T(8,128)S(1)}, f32[21,8,128]{2,1,0:T(8,128)S(1)}, u32[]{:S(2)}, u32[]{:S(2)}) collective-permute-start(f32[21,8,128]{2,1,0:T(8,128)S(1)} %pack.1.shared.refs_0_), channel_id=1, source_target_pairs={{0,1},{1,0},{2,3},{3,2},{4,5},{5,4},{6,7},{7,6},{8,9},{9,8},{10,11... | collective-permute-start | bytes 258056 | tf_op jit(solution)/shard_map/ppermute | solution.py:685
  1.5 5.7 %collective-permute-start.1 = (f32[21,8,128]{2,1,0:T(8,128)S(1)}, f32[21,8,128]{2,1,0:T(8,128)S(1)}, u32[]{:S(2)}, u32[]{:S(2)}) collective-permute-start(f32[21,8,128]{2,1,0:T(8,128)S(1)} %pack.1.shared.refs_0_), channel_id=1, source_target_pairs={{0,2},{1,3},{2,0},{3,1},{4,6},{5,7},{6,4},{7,5},{8,10},{9,11},{10,... | collective-permute-start | bytes 258056 | tf_op jit(solution)/shard_map/ppermute | solution.py:685
  7.3 3.0 %collective-permute-start.3 = (f32[81,8,128]{2,1,0:T(8,128)S(1)}, f32[81,8,128]{2,1,0:T(8,128)S(1)}, u32[]{:S(2)}, u32[]{:S(2)}) collective-permute-start(f32[81,8,128]{2,1,0:T(8,128)S(1)} %restrict.1.refs_5_), channel_id=1, source_target_pairs={{0,1},{1,0},{2,3},{3,2},{4,5},{5,4},{6,7},{7,6},{8,9},{9,8},{10,11... | collective-permute-start | bytes 995336 | tf_op jit(solution)/shard_map/ppermute | solution.py:786
  7.3 10.7 %collective-permute-start.4 = (f32[81,8,128]{2,1,0:T(8,128)S(1)}, f32[81,8,128]{2,1,0:T(8,128)S(1)}, u32[]{:S(2)}, u32[]{:S(2)}) collective-permute-start(f32[81,8,128]{2,1,0:T(8,128)S(1)} %restrict.1.refs_5_), channel_id=1, source_target_pairs={{0,2},{1,3},{2,0},{3,1},{4,6},{5,7},{6,4},{7,5},{8,10},{9,11},{10,... | collective-permute-start | bytes 995336 | tf_op jit(solution)/shard_map/ppermute | solution.py:787
  9.0 1.3 %collective-permute-start.2 = (f32[21,8,128]{2,1,0:T(8,128)S(1)}, f32[21,8,128]{2,1,0:T(8,128)S(1)}, u32[]{:S(2)}, u32[]{:S(2)}) collective-permute-start(f32[21,8,128]{2,1,0:T(8,128)S(1)} %collective-permute-done.1.refs_1_), channel_id=1, source_target_pairs={{0,1},{1,0},{2,3},{3,2},{4,5},{5,4},{6,7},{7,6},{8,9},{9,8},{10,11... | collective-permute-start | bytes 258056 | tf_op jit(solution)/shard_map/ppermute | solution.py:685
  13.0 13.1 %all-to-all-start = ((f32[32,8,128]{2,1,0:T(8,128)}), f32[32,8,128]{2,1,0:T(8,128)S(1)}, u32[]{:S(2)}, u32[]{:S(2)}) async-start(f32[32,8,128]{2,1,0:T(8,128)} %get-tuple-element.19), calls=%async_computation | async-start | bytes 262144 | tf_op jit(solution)/shard_map/all_to_all | solution.py:810
  18.0 2.1 %copy-start.1 = (f32[5,5]{1,0:T(8,128)S(1)}, f32[5,5]{1,0:T(8,128)}, u32[]{:S(2)}) copy-start(f32[5,5]{1,0:T(8,128)} %refs_4_.5) | copy-start | bytes 304
  18.0 2.1 %collective-permute-start.8 = (f32[21,8,128]{2,1,0:T(8,128)S(1)}, f32[21,8,128]{2,1,0:T(8,128)S(1)}, u32[]{:S(2)}, u32[]{:S(2)}) collective-permute-start(f32[21,8,128]{2,1,0:T(8,128)S(1)} %get-tuple-element.24), channel_id=1, source_target_pairs={{0,1},{1,0},{2,3},{3,2},{4,5},{5,4},{6,7},{7,6},{8,9},{9,8},{10,11... | collective-permute-start | bytes 258056 | tf_op jit(solution)/shard_map/ppermute | solution.py:820
  18.3 1.3 %collective-permute-start.5 = (f32[20,8,128]{2,1,0:T(8,128)S(1)}, f32[20,8,128]{2,1,0:T(8,128)S(1)}, u32[]{:S(2)}, u32[]{:S(2)}) collective-permute-start(f32[20,8,128]{2,1,0:T(8,128)S(1)} %get-tuple-element.21), channel_id=1, source_target_pairs={{0,1},{1,0},{2,3},{3,2},{4,5},{5,4},{6,7},{7,6},{8,9},{9,8},{10,11... | collective-permute-start | bytes 245768 | tf_op jit(solution)/shard_map/ppermute | solution.py:820
  18.6 1.3 %collective-permute-start.6 = (f32[20,8,128]{2,1,0:T(8,128)S(1)}, f32[20,8,128]{2,1,0:T(8,128)S(1)}, u32[]{:S(2)}, u32[]{:S(2)}) collective-permute-start(f32[20,8,128]{2,1,0:T(8,128)S(1)} %get-tuple-element.22), channel_id=1, source_target_pairs={{0,1},{1,0},{2,3},{3,2},{4,5},{5,4},{6,7},{7,6},{8,9},{9,8},{10,11... | collective-permute-start | bytes 245768 | tf_op jit(solution)/shard_map/ppermute | solution.py:820
  18.8 1.3 %collective-permute-start.7 = (f32[20,8,128]{2,1,0:T(8,128)S(1)}, f32[20,8,128]{2,1,0:T(8,128)S(1)}, u32[]{:S(2)}, u32[]{:S(2)}) collective-permute-start(f32[20,8,128]{2,1,0:T(8,128)S(1)} %get-tuple-element.23), channel_id=1, source_target_pairs={{0,1},{1,0},{2,3},{3,2},{4,5},{5,4},{6,7},{7,6},{8,9},{9,8},{10,11... | collective-permute-start | bytes 245768 | tf_op jit(solution)/shard_map/ppermute | solution.py:820
  20.1 6.1 %copy-start = (f32[1,8,5,16,256]{4,3,2,1,0:T(8,128)S(1)}, f32[1,8,5,16,256]{4,3,2,1,0:T(8,128)}, u32[]{:S(2)}) copy-start(f32[1,8,5,16,256]{4,3,2,1,0:T(8,128)} %refs_11_.1) | copy-start | bytes 1966084

commit v5 on v4

--- a/solution.py
+++ b/solution.py
@@ -184,7 +184,6 @@
 F32 = jnp.float32
 HIGHEST = lax.Precision.HIGHEST
 VMEM = pl.BlockSpec(memory_space=pltpu.VMEM)
-SMEM = pl.BlockSpec(memory_space=pltpu.SMEM)
 HBM = pl.BlockSpec(memory_space=pltpu.HBM)
 LANES = 128
 
@@ -258,7 +257,7 @@
 
 
 def pack_kernel(
-    sizes, counts, diagonal, donors, offsets, receptors, out, held, rows, cells, allowed, sems
+    sizes, counts, ids, diagonal, donors, offsets, receptors, out, meta, held, rows, cells, planes_of, allowed, sems
 ):
     planes, variables, height, depth = sizes["coarse"]
     slots = sizes["slots"]
@@ -271,6 +270,7 @@
             (receptors.at[0], cells.at[0]),
             (donors.at[0], cells.at[1]),
             (offsets.at[0], rows),
+            (ids, planes_of),
             (diagonal.at[0], held),
         ],
         sems,
@@ -284,38 +284,11 @@
     for k in range(3):
         out[count, k + 1 : k + 2, 0:slots] = rows[k]
     out[count, 4:5, 0:slots] = cell.astype(F32)
-
-
-def restrict_kernel(sizes, residual, fine, ids, first, second, out, held, wide, sems):
-    planes, variables, height, depth = sizes["coarse"]
-    blocks = sizes["blocks"]
-    step = 8
-    copies = start_copies(
-        [
-            (source.at[0, q : q + step], held.at[k, q : q + step])
-            for k, source in enumerate((fine, residual))
-            for q in range(0, blocks, step)
-        ],
-        sems,
-    )
-    pair = jnp.where(
-        iota((2 * depth, depth), 0) // 2 == iota((2 * depth, depth), 1), 0.125, 0.0
-    ).astype(BF16)
-    count = step * variables
-    out[2 * blocks * variables] = jnp.zeros((height, depth), F32)
-    out[2 * blocks * variables, 0:1, 0:blocks] = ids[...].astype(F32)
-    for i, copy in enumerate(copies):
-        k, q = divmod(i * step, blocks)
-        copy.wait()
-        rows = held[k, q : q + step].reshape(count * 2 * height, 2 * depth)
-        here = pl.ds(i * count, count)
-        wide[here] = dot_exact(rows, pair).reshape(count, 2 * height, depth)
-        out[here] = (
-            wide[here, pl.ds(0, height, stride=2), :] + wide[here, pl.ds(1, height, stride=2), :]
-        )
-
-
-def corner_kernel(sizes, shared, out):
+    out[count, 5:6, 0 : sizes["blocks"]] = planes_of[...].astype(F32)
+    meta[0] = out[count]
+
+
+def find_corners(sizes, shared, out):
     planes, variables, height, depth = sizes["coarse"]
     slots, grids = sizes["slots"], sizes["grids"]
     grid_index = lax.axis_index("grid")
@@ -372,22 +345,55 @@
         out[h] = jnp.where(mine, pltpu.roll(starts, (LANES - 8 * h) % LANES, 1), tile)
 
 
+def restrict_kernel(sizes, residual, fine, shared, out, corners, held, wide, sems):
+    planes, variables, height, depth = sizes["coarse"]
+    blocks = sizes["blocks"]
+    step = 8
+    copies = start_copies(
+        [
+            (source.at[0, q : q + step], held.at[k, q : q + step])
+            for k, source in enumerate((fine, residual))
+            for q in range(0, blocks, step)
+        ],
+        sems,
+    )
+    find_corners(sizes, shared, corners)
+    pair = jnp.where(
+        iota((2 * depth, depth), 0) // 2 == iota((2 * depth, depth), 1), 0.125, 0.0
+    ).astype(BF16)
+    count = step * variables
+    for i, copy in enumerate(copies):
+        k, q = divmod(i * step, blocks)
+        copy.wait()
+        rows = held[k, q : q + step].reshape(count * 2 * height, 2 * depth)
+        here = pl.ds(i * count, count)
+        wide[here] = dot_exact(rows, pair).reshape(count, 2 * height, depth)
+        out[here] = (
+            wide[here, pl.ds(0, height, stride=2), :] + wide[here, pl.ds(1, height, stride=2), :]
+        )
+
+
 def hats(shape, dim, start, frac):
     at = iota(shape, dim)
     return jnp.where(at == start, 1.0 - frac, 0.0) + jnp.where(at == start + 1, frac, 0.0)
 
 
-def interpolate(field, rows):
-    total, variables, height, depth = field.shape
+def interpolate(fields, rows, base):
+    planes, variables, height, depth = fields[0].shape
     count = rows.shape[1]
-    plane, row, column = split_cell(rows[0:1, :].astype(jnp.int32), height, depth)
+    cell = rows[0:1, :].astype(jnp.int32) - base
+    plane, row, column = split_cell(cell, height, depth)
     frac_x, frac_y, frac_z = rows[1:2, :], rows[2:3, :], rows[3:4, :]
     weight_z = hats((depth, count), 0, column, frac_z)
     weight_y = hats((height, count), 0, row, frac_y)
-    along_z = dot_near(field.reshape(total * variables * height, depth), weight_z)
-    along_z = along_z.reshape(total, variables, height, count)
+    lower = iota((depth, count), 1) < count // 2
+    weight_z = jnp.concatenate(
+        [jnp.where(lower, weight_z, 0.0), jnp.where(lower, 0.0, weight_z)], axis=0
+    )
+    both = jnp.concatenate([each.reshape(-1, depth) for each in fields], axis=1)
+    along_z = dot_near(both, weight_z).reshape(planes, variables, height, count)
     summed = None
-    for p in range(total):
+    for p in range(planes):
         weight_x = jnp.where(plane == p, 1.0 - frac_x, 0.0) + jnp.where(
             plane + 1 == p, frac_x, 0.0
         )
@@ -396,38 +402,51 @@
     return jnp.sum(summed, axis=1)
 
 
+def gather_rows(sizes, known, stage, rows):
+    slots = sizes["slots"]
+    for part, bit in zip(known, (0, 2, 1, 3)):
+        stage[lax.axis_index("sub") ^ bit] = part[part.shape[0] - 1]
+    for j, s in enumerate((0, 2, 1, 3)):
+        rows[:, j * slots : (j + 1) * slots] = stage[s, :, 0:slots]
+
+
 def partial_kernel(sizes, *refs):
     subs, grids, slots, blocks = sizes["subs"], sizes["grids"], sizes["slots"], sizes["blocks"]
     planes, variables, height, depth = sizes["coarse"]
-    parts = refs[:subs]
-    ids, own, mate, corners = refs[subs : subs + 4]
-    out, gain, mask_out, both, rows, stage, numbers, sem = refs[subs + 4 :]
+    known = refs[:subs]
+    own, mate, corners = refs[subs:-8]
+    out, mask_out, both, rows, stage, pair, padded, wet = refs[-8:]
     total = subs * planes
     sub_index = lax.axis_index("sub")
     grid_index = lax.axis_index("grid")
     count = planes * variables
-    fine_count = blocks * variables
-    copy = pltpu.make_async_copy(mate.at[2 * fine_count, 0:1, :], numbers, sem)
-    copy.start()
-    for i, part in enumerate(parts):
-        owner = sub_index ^ sizes["order"][i]
-        stage[owner] = part[count]
-        gain[pl.ds(owner * planes, planes)] = part[0:count].reshape(sizes["coarse"])
-    for j in range(subs):
-        rows[:, j * slots : (j + 1) * slots] = stage[j, :, 0:slots]
+    gather_rows(sizes, known, stage, rows)
+    pair[sub_index // 2] = known[0][...]
+    pair[1 - sub_index // 2] = known[1][...]
     mask, _, _ = receptor_mask(rows[4:5, :].astype(jnp.int32), total, height, depth)
     mask_out[...] = mask
-    both[...] = jnp.zeros(both.shape, F32)
-    add_planes(sizes, own, ids, both)
-    copy.wait()
-    add_planes(sizes, mate, numbers, both)
-    restricted = both[:, 0:variables]
-    residual = both[:, variables:]
-    wet = mask > 0.5
-    beside = neighbour_sum(jnp.where(wet, restricted, 0.0))
-    swept = jnp.where(wet, 0.0, restricted + gain[...] * (residual - beside))
-    half = jnp.where(sub_index % 2 == 0, rows[:, 0:LANES], rows[:, LANES:])
-    values = interpolate(jnp.concatenate([restricted, swept], axis=1), half)
+    wet[1 : total + 1] = mask
+    padded[...] = jnp.zeros(padded.shape, F32)
+    inner = padded.at[1 : total + 1]
+    add_planes(sizes, [own], plane_numbers(known[0][count], blocks), inner)
+    add_planes(sizes, [mate], plane_numbers(known[2][0], blocks), inner)
+    both[...] = padded[1 : total + 1]
+    core = sub_index % 2
+    fields = []
+    for k in range(2):
+        start = (core + 2 * k) * planes
+        here = padded[pl.ds(start, planes + 2)]
+        dry = wet[pl.ds(start, planes + 2)] < 0.5
+        drowned = jnp.where(dry, 0.0, here[:, 0:variables])
+        beside = neighbour_sum(drowned)[1 : planes + 1]
+        restricted, residual = here[1 : planes + 1, :variables], here[1 : planes + 1, variables:]
+        gain = pair[k, 0:count].reshape(sizes["coarse"])
+        swept = jnp.where(dry[1 : planes + 1], restricted + gain * (residual - beside), 0.0)
+        fields.append(jnp.concatenate([restricted, swept], axis=1))
+    half = jnp.concatenate([pair[0, count, :, 0:slots], pair[1, count, :, 0:slots]], axis=1)
+    lane = iota((1, LANES), 1)
+    base = (core + 2 * (lane // slots)) * (planes * height * depth)
+    values = interpolate(fields, half, base)
     empty = jnp.zeros((3, LANES), F32)
     first = jnp.concatenate([values[:variables], empty], axis=0)
     second = jnp.concatenate([values[variables:], empty], axis=0)
@@ -441,14 +460,22 @@
             out[h * subs + s] = tile
 
 
-def add_planes(sizes, part, numbers, both):
-    variables = sizes["coarse"][1]
-    count = sizes["blocks"] * variables
-    for q in range(sizes["blocks"]):
-        coarse = pl.ds(numbers[0, q].astype(jnp.int32) // 2, 1)
+def plane_numbers(meta, blocks):
+    row = meta[5:6, :]
+    lane = iota(row.shape, 1)
+    return [jnp.sum(jnp.where(lane == q, row, 0.0)).astype(jnp.int32) for q in range(blocks)]
+
+
+def add_planes(sizes, pieces, numbers, both):
+    variables, blocks = sizes["coarse"][1], sizes["blocks"]
+    width = pieces[0].shape[0] // variables
+    for q in range(blocks):
+        coarse = pl.ds(numbers[q] // 2, 1)
         for k in range(2):
-            at = k * count + q * variables
-            both[coarse, pl.ds(k * variables, variables)] += part[at : at + variables][None]
+            i = k * blocks + q
+            at = i % width * variables
+            part = pieces[i // width][at : at + variables]
+            both[coarse, pl.ds(k * variables, variables)] += part[None]
 
 
 def split_kernel(sizes, whole, *pieces):
@@ -458,30 +485,20 @@
         at = at + piece.shape[0]
 
 
-def assemble_kernel(sizes, known, across, *refs):
+def assemble_kernel(sizes, known, across, shared, partner, beside, last, *refs):
     variables = sizes["coarse"][1]
+    pieces = refs[:-4]
+    coupling, both, source, gain = refs[-4:]
+    planes = sizes["coarse"][0]
+    for part, bit in ((shared, 0), (partner, 2), (beside, 1), (last, 3)):
+        owner = lax.axis_index("sub") ^ bit
+        here = part[0 : planes * variables].reshape(sizes["coarse"])
+        gain[pl.ds(owner * planes, planes)] = here
+    count = planes * variables
     blocks = sizes["blocks"]
-    count = blocks * variables
-    pieces = refs[:-5]
-    coupling, both, source, numbers, sems = refs[-5:]
-    width = pieces[0].shape[0] // variables
-    copies = start_copies(
-        [
-            (across.at[2 * count, 0:1, :], numbers.at[0]),
-            (pieces[-1].at[width * variables, 0:1, :], numbers.at[1]),
-        ],
-        sems,
-    )
     both[...] = known[...]
-    copies[0].wait()
-    add_planes(sizes, across, numbers.at[0], both)
-    copies[1].wait()
-    for q in range(2 * blocks):
-        k, slot = divmod(q, blocks)
-        coarse = pl.ds(numbers[1, 0, slot].astype(jnp.int32) // 2, 1)
-        at = q % width * variables
-        part = pieces[q // width][at : at + variables]
-        both[coarse, pl.ds(k * variables, variables)] += part[None]
+    add_planes(sizes, [across], plane_numbers(partner[count], blocks), both)
+    add_planes(sizes, pieces, plane_numbers(last[count], blocks), both)
     source[...] = couple(coupling, both[:, 0:variables])
 
 
@@ -489,9 +506,10 @@
     variables = field.shape[1]
     outs = []
     for v in range(variables):
-        summed = coupling[v, 0] * field[:, 0]
-        for x in range(1, variables):
-            summed = summed + coupling[v, x] * field[:, x]
+        summed = None
+        for x in range(variables):
+            term = coupling[v : v + 1, x : x + 1][None] * field[:, x]
+            summed = term if summed is None else summed + term
         outs.append(jnp.tanh(summed)[:, None])
     return jnp.concatenate(outs, axis=1)
 
@@ -543,7 +561,7 @@
     for g in range(grids):
         scale = []
         for k in range(2):
-            one, two = arrived[g * subs + 2 * k], arrived[g * subs + 2 * k + 1]
+            one, two = arrived[g * subs + k], arrived[g * subs + k + 2]
             low = jnp.where(lane < 64, one, pltpu.roll(two, 64, 1))
             high = jnp.where(lane < 64, pltpu.roll(one, 64, 1), two)
             scale.append(jnp.where(sublane < 3, pltpu.roll(low, 3, 0), pltpu.roll(high, 6, 0)))
@@ -617,16 +635,11 @@
     subs = sizes["subs"]
     planes, variables, height, depth = sizes["coarse"]
     blocks = sizes["blocks"]
-    slots = sizes["slots"]
     parts = refs[:subs]
-    coupling, ids, arrived, both, source, gain, mask, fine = refs[subs : subs + 8]
-    out, landing, stage, rows, padded, tall, held, sems = refs[subs + 8 :]
+    coupling, arrived, both, source, gain, mask, fine = refs[subs : subs + 7]
+    out, landing, stage, rows, padded, tall, held, sems = refs[subs + 7 :]
     total = subs * planes
-    sub_index = lax.axis_index("sub")
-    for i, part in enumerate(parts):
-        stage[sub_index ^ sizes["order"][i]] = part[planes * variables]
-    for j in range(subs):
-        rows[:, j * slots : (j + 1) * slots] = stage[j, :, 0:slots]
+    gather_rows(sizes, parts, stage, rows)
     first, second = fringe_values(sizes, arrived, landing)
     cell = rows[4:5, :].astype(jnp.int32)
     values = jnp.concatenate([first[:variables], second[:variables]], axis=0)
@@ -653,8 +666,8 @@
     ).astype(BF16)
     copies = []
     step = 2
-    for q in range(blocks):
-        number = ids[0, q]
+    numbers = plane_numbers(parts[0][planes * variables], blocks)
+    for q, number in enumerate(numbers):
         coarse = number // 2
         along = 0.75 * padded[coarse + 1] + 0.25 * padded[coarse + 2 * (number % 2)]
         below = jnp.where(at_row > 0, pltpu.roll(along, 1, 1), 0.0)
@@ -677,15 +690,6 @@
         copy.wait()
 
 
-def spread_over_sub(block, order_bits):
-    held = [block]
-    count = lax.axis_size("sub")
-    for bit in order_bits:
-        pairs = [(i, i ^ bit) for i in range(count)]
-        held = held + [lax.ppermute(one, "sub", pairs) for one in held]
-    return held
-
-
 def fast_shards(
     fine_residual,
     fine_solution,
@@ -703,13 +707,7 @@
     planes, variables, height, depth = coarse
     blocks = plane_of_slot.shape[1]
     slots = donor_cells.shape[-1]
-    bits = [1 << k for k in reversed(range(subs.bit_length() - 1))]
-    order = [0]
-    for bit in bits:
-        order = order + [one ^ bit for one in order]
-    sizes = dict(
-        coarse=coarse, blocks=blocks, slots=slots, grids=grids, subs=subs, order=tuple(order)
-    )
+    sizes = dict(coarse=coarse, blocks=blocks, slots=slots, grids=grids, subs=subs)
     count = blocks * variables
     total = subs * planes
     whole = (total, variables, height, depth)
@@ -717,11 +715,8 @@
     rows = pltpu.VMEM((8, subs * slots), F32)
     stage = pltpu.VMEM((subs, 8, depth), F32)
 
-    def call(kernel, name, out_shape, scalars, *operands, scratch=(), far=(), out_spec=VMEM, aliases={}):
-        specs = [
-            SMEM if any(one is s for s in scalars) else HBM if any(one is f for f in far) else VMEM
-            for one in operands
-        ]
+    def call(kernel, name, out_shape, *operands, scratch=(), far=(), out_spec=VMEM, aliases={}):
+        specs = [HBM if any(one is each for each in far) else VMEM for one in operands]
         operands = [
             pltpu.with_memory_space_constraint(one, pltpu.HBM) if spec is HBM else one
             for one, spec in zip(operands, specs)
@@ -737,43 +732,39 @@
             name=name,
         )(*operands)
 
-    scalars = (coupling, plane_of_slot)
     offsets = donor_offsets.transpose(0, 2, 1, 3)
-    inputs = (fringe_counts, coarse_diagonal, donor_cells, offsets, receptor_cells)
-    shared = call(
+    inputs = (fringe_counts, plane_of_slot, coarse_diagonal, donor_cells, offsets, receptor_cells)
+    shared, meta = call(
         pack_kernel,
         "pack",
-        jax.ShapeDtypeStruct((planes * variables + 1, height, depth), F32),
-        scalars,
+        [
+            jax.ShapeDtypeStruct((planes * variables + 1, height, depth), F32),
+            jax.ShapeDtypeStruct((1, height, depth), F32),
+        ],
         *inputs,
         far=inputs,
         scratch=[
             pltpu.VMEM(coarse, F32),
             pltpu.VMEM(offsets.shape[1:], F32),
             pltpu.VMEM((2, 1, slots), jnp.int32),
+            pltpu.VMEM(plane_of_slot.shape, jnp.int32),
             pltpu.SMEM(fringe_counts.shape, jnp.int32),
-            pltpu.SemaphoreType.DMA((5,)),
+            pltpu.SemaphoreType.DMA((6,)),
         ],
     )
-    mine = shared
-    shared = spread_over_sub(shared, bits)
-    corners = call(
-        corner_kernel,
-        "corners",
-        jax.ShapeDtypeStruct((grids, 8, LANES), F32),
-        scalars,
-        mine,
-    )
-    own = call(
+    swap = {bit: [(i, i ^ bit) for i in range(subs)] for bit in (1, 2)}
+    partner = lax.ppermute(shared, "sub", swap[2])
+    beside = lax.ppermute(meta, "sub", swap[1])
+    own, corners = call(
         restrict_kernel,
         "restrict",
-        jax.ShapeDtypeStruct((2 * count + 1, height, depth), F32),
-        (),
+        [
+            jax.ShapeDtypeStruct((2 * count, height, depth), F32),
+            jax.ShapeDtypeStruct((grids, 8, LANES), F32),
+        ],
         fine_residual,
         fine_solution,
-        plane_of_slot,
-        corners,
-        shared[order.index(1)],
+        shared,
         far=(fine_residual, fine_solution),
         scratch=[
             pltpu.VMEM((2,) + fine_solution.shape[1:], F32),
@@ -781,63 +772,55 @@
             pltpu.SemaphoreType.DMA((blocks,)),
         ],
     )
-    own, shared[1] = lax.optimization_barrier((own, shared[1]))
-    cores = [(i, i ^ 1) for i in range(subs)]
-    mate = lax.ppermute(own, "sub", cores)
-    across = lax.ppermute(own, "sub", [(i, i ^ 2) for i in range(subs)])
-    out, gain, mask, both = call(
+    own, partner, beside = lax.optimization_barrier((own, partner, beside))
+    mate = lax.ppermute(own, "sub", swap[1])
+    known = (shared, partner, beside, lax.ppermute(partner, "sub", swap[1]))
+    across = lax.ppermute(own, "sub", swap[2])
+    out, mask, both = call(
         partial_kernel,
         "partial",
         [
             jax.ShapeDtypeStruct((grids * subs, 8, LANES), F32),
-            full,
             jax.ShapeDtypeStruct((total, 1, height, depth), F32),
             jax.ShapeDtypeStruct((total, 2 * variables, height, depth), F32),
         ],
-        scalars,
-        *shared,
-        plane_of_slot,
+        *known,
         own,
         mate,
         corners,
         scratch=[
             rows,
             stage,
-            pltpu.SMEM((1, depth), F32),
-            pltpu.SemaphoreType.DMA,
+            pltpu.VMEM((2, planes * variables + 1, height, depth), F32),
+            pltpu.VMEM((total + 2, 2 * variables, height, depth), F32),
+            pltpu.VMEM((total + 2, 1, height, depth), F32),
         ],
     )
     arrived = lax.all_to_all(out, ("grid", "sub"), 0, 0, tiled=True)
-    width = blocks // 2 * variables
-    sizes_of = [width, width, width, 2 * count + 1 - 3 * width]
-    pieces = call(
-        split_kernel,
-        "split",
-        [jax.ShapeDtypeStruct((each, height, depth), F32) for each in sizes_of],
-        (),
-        across,
-    )
-    pieces = [lax.ppermute(piece, "sub", cores) for piece in pieces]
-    both, source = call(
+    piece = jax.ShapeDtypeStruct((blocks // 2 * variables, height, depth), F32)
+    pieces = call(split_kernel, "split", [piece] * 4, across)
+    pieces = [lax.ppermute(each, "sub", swap[1]) for each in pieces]
+    beside_gain = lax.ppermute(shared, "sub", swap[1])
+    both, source, gain = call(
         assemble_kernel,
         "assemble",
-        [jax.ShapeDtypeStruct(both.shape, F32), full],
-        scalars,
+        [jax.ShapeDtypeStruct(both.shape, F32), full, full],
         both,
         across,
+        shared,
+        partner,
+        beside_gain,
+        known[3],
         *pieces,
         coupling,
         aliases={0: 0},
-        scratch=[pltpu.SMEM((2, 1, depth), F32), pltpu.SemaphoreType.DMA((2,))],
     )
     return call(
         finish_kernel,
         "finish",
         jax.ShapeDtypeStruct(fine_solution.shape, F32),
-        scalars,
-        *shared,
+        *known,
         coupling,
-        plane_of_slot,
         arrived,
         both,
         source,

time: 30.5 us -> 28.5 us (0.934)
  Pallas kernels: 12 us -> 9.17 us
  starting transfers between devices: 11.1 us -> 11.6 us
  waiting for transfers between devices: 6.98 us -> 7.43 us
    pallas_call x7 -> x6, Pallas kernels: 12 us -> 9.17 us  [call(): pl.pallas_call(functools.partial(kernel, sizes), out_shape=out_shape, in_...]
    all_to_all x1, waiting for transfers between devices: 4.61 us -> 5.22 us  [fast_shards(): arrived = lax.all_to_all(out, ('grid', 'sub'), 0, 0, tiled=True)]
    ppermute x9 -> x10, starting transfers between devices: 6.18 us -> 6.39 us  [the longest x1 3.03 us: fast_shards(): partner = lax.ppermute(shared, 'sub', swap[2])]
    ppermute x9 -> x10, waiting for transfers between devices: 2.37 us -> 2.21 us  [the longest x1 1.06 us: fast_shards(): known = (shared, partner, beside, lax.ppermute(partner, 'sub', swap[1]))]
  transfers between devices with their start and end apart: 10 -> 11, of which waited for: 6 -> 7; matrix products, arithmetic and copies ran while one was open for 0% -> 0% of each run, Pallas kernels for 23% -> 16%
where the time goes in v5:
time: 28.5 us; the launch traced here: 28.3 us
  starting transfers between devices  11.6 us (41%)
  Pallas kernels  9.17 us (32%)
  waiting for transfers between devices  7.43 us (26%)
    pallas_call x6, Pallas kernels, call(): pl.pallas_call(functools.partial(kernel, sizes), out_shape=out_shape, in_...  9.17 us
    all_to_all x1, waiting for transfers between devices, fast_shards(): arrived = lax.all_to_all(out, ('grid', 'sub'), 0, 0, tiled=True)  5.22 us
    all_to_all x1, starting transfers between devices, fast_shards(): arrived = lax.all_to_all(out, ('grid', 'sub'), 0, 0, tiled=True)  5.2 us
    ppermute x1, starting transfers between devices, fast_shards(): partner = lax.ppermute(shared, 'sub', swap[2])  3.03 us
    ppermute x1, starting transfers between devices, fast_shards(): across = lax.ppermute(own, 'sub', swap[2])  1.16 us
    ppermute x4, starting transfers between devices, fast_shards(): pieces = [lax.ppermute(each, 'sub', swap[1]) for each in pieces]  1.09 us
    ppermute x1, waiting for transfers between devices, fast_shards(): known = (shared, partner, beside, lax.ppermute(partner, 'sub', swap[1]))  1.06 us
    ppermute x4, waiting for transfers between devices, fast_shards(): pieces = [lax.ppermute(each, 'sub', swap[1]) for each in pieces]  0.92 us
  transfers between devices with their start and end apart: 11, of which 7 were waited for; matrix products, arithmetic and copies ran while one was open for 0% of the time, Pallas kernels for 16%

profile of v5, /device:TPU:0, one launch (start us, length us, event | category | flops | bytes accessed | tf_op | source)
XLA Modules:
  0.0 28.3 jit_solution(16652530112998280549)
XLA Ops:
  0.0 1.0 %pack.1 = (f32[21,8,128]{2,1,0:T(8,128)S(1)}, f32[1,8,128]{2,1,0:T(8,128)S(1)}) custom-call(s32[8,8]{1,0:T(8,128)} %counts.1, s32[1,8]{1,0:T(1,128)} %ids.1, f32[1,4,5,8,128]{4,3,2,1,0:T(8,128)} %diagonal.1, s32[1,1,64]{2,1,0:T(1,128)} %donors.1, f32[1,3,1,64]{3,2,1,0:T(1,128)} %bitcast.1, s32[1,1,64]{2,1,0:T(1,128)} %receptors.1), custom_call_target="tpu_custom_call" | custom-call | tf_op jit(solution)/shard_map/pack/pallas_call | solution.py:724
  1.0 3.0 %collective-permute-start = (f32[21,8,128]{2,1,0:T(8,128)S(1)}, f32[21,8,128]{2,1,0:T(8,128)S(1)}, u32[]{:S(2)}, u32[]{:S(2)}) collective-permute-start(f32[21,8,128]{2,1,0:T(8,128)S(1)} %get-tuple-element.22.shared.refs_0_), channel_id=1, source_target_pairs={{0,2},{1,3},{2,0},{3,1},{4,6},{5,7},{6,4},{7,5},{8,10},{9,11},{10,... | collective-permute-start | bytes 258056 | tf_op jit(solution)/shard_map/ppermute | solution.py:756
  4.1 2.7 %restrict.1 = (f32[80,8,128]{2,1,0:T(8,128)S(1)}, f32[8,8,128]{2,1,0:T(8,128)S(1)}) custom-call(f32[1,8,5,16,256]{4,3,2,1,0:T(8,128)} %residual.1, f32[1,8,5,16,256]{4,3,2,1,0:T(8,128)} %refs_10_.1, f32[21,8,128]{2,1,0:T(8,128)S(1)} %get-tuple-element.22.shared.refs_0_), custom_call_target="tpu_custom_call" | custom-call | tf_op jit(solution)/shard_map/restrict/pallas_call | solution.py:724
  6.8 0.0 collective-permute-done.1.refs_2_
  6.8 0.6 %collective-permute-start.3 = (f32[80,8,128]{2,1,0:T(8,128)S(1)}, f32[80,8,128]{2,1,0:T(8,128)S(1)}, u32[]{:S(2)}, u32[]{:S(2)}) collective-permute-start(f32[80,8,128]{2,1,0:T(8,128)S(1)} %get-tuple-element.27.refs_4_), channel_id=1, source_target_pairs={{0,1},{1,0},{2,3},{3,2},{4,5},{5,4},{6,7},{7,6},{8,9},{9,8},{10,11... | collective-permute-start | bytes 983048 | tf_op jit(solution)/shard_map/ppermute | solution.py:776
  7.4 1.2 %collective-permute-start.4 = (f32[80,8,128]{2,1,0:T(8,128)S(1)}, f32[80,8,128]{2,1,0:T(8,128)S(1)}, u32[]{:S(2)}, u32[]{:S(2)}) collective-permute-start(f32[80,8,128]{2,1,0:T(8,128)S(1)} %get-tuple-element.27.refs_4_), channel_id=1, source_target_pairs={{0,2},{1,3},{2,0},{3,1},{4,6},{5,7},{6,4},{7,5},{8,10},{9,11},{10,... | collective-permute-start | bytes 983048 | tf_op jit(solution)/shard_map/ppermute | solution.py:778
  8.6 0.2 collective-permute-start.2
  8.8 1.1 %collective-permute-done.2.refs_3_.last = f32[21,8,128]{2,1,0:T(8,128)S(1)} collective-permute-done((f32[21,8,128]{2,1,0:T(8,128)S(1)}, f32[21,8,128]{2,1,0:T(8,128)S(1)}, u32[]{:S(2)}, u32[]{:S(2)}) %collective-permute-start.2) | collective-permute-done | bytes 86048 | tf_op jit(solution)/shard_map/ppermute | solution.py:777
  9.8 1.5 %partial.1 = (f32[32,8,128]{2,1,0:T(8,128)}, f32[16,1,8,128]{3,2,1,0:T(8,128)S(1)}, f32[16,10,8,128]{3,2,1,0:T(8,128)S(1)}) custom-call(f32[21,8,128]{2,1,0:T(8,128)S(1)} %get-tuple-element.22.shared.refs_0_, f32[21,8,128]{2,1,0:T(8,128)S(1)} %collective-permute-done.refs_1_.partner, f32[1,8,128]{2,1,0:T(8,128)S(1)} %collective-permute-done.1.refs_2_, ...), custom_call_target="tpu_custom_call" | custom-call | tf_op jit(solution)/shard_map/partial/pallas_call | solution.py:724
  11.3 5.2 %all-to-all-start = ((f32[32,8,128]{2,1,0:T(8,128)}), f32[32,8,128]{2,1,0:T(8,128)S(1)}, u32[]{:S(2)}, u32[]{:S(2)}) async-start(f32[32,8,128]{2,1,0:T(8,128)} %get-tuple-element.29), calls=%async_computation | async-start | bytes 262144 | tf_op jit(solution)/shard_map/all_to_all | solution.py:799
  16.6 0.3 %collective-permute-start.5 = (f32[21,8,128]{2,1,0:T(8,128)S(1)}, f32[21,8,128]{2,1,0:T(8,128)S(1)}, u32[]{:S(2)}, u32[]{:S(2)}) collective-permute-start(f32[21,8,128]{2,1,0:T(8,128)S(1)} %get-tuple-element.22.shared.refs_0_), channel_id=1, source_target_pairs={{0,1},{1,0},{2,3},{3,2},{4,5},{5,4},{6,7},{7,6},{8,9},{9,8},{10,11... | collective-permute-start | bytes 258056 | tf_op jit(solution)/shard_map/ppermute | solution.py:803
  16.9 0.2 collective-permute-done.4.whole.across
  17.1 0.0 copy-start.1
  17.1 0.1 collective-permute-start.6
  17.2 0.5 %collective-permute-start.7 = (f32[20,8,128]{2,1,0:T(8,128)S(1)}, f32[20,8,128]{2,1,0:T(8,128)S(1)}, u32[]{:S(2)}, u32[]{:S(2)}) collective-permute-start(f32[20,8,128]{2,1,0:T(8,128)S(1)} %get-tuple-element.32), channel_id=1, source_target_pairs={{0,1},{1,0},{2,3},{3,2},{4,5},{5,4},{6,7},{7,6},{8,9},{9,8},{10,11... | collective-permute-start | bytes 245768 | tf_op jit(solution)/shard_map/ppermute | solution.py:802
  17.7 0.1 collective-permute-start.8
  17.8 0.4 %collective-permute-start.9 = (f32[20,8,128]{2,1,0:T(8,128)S(1)}, f32[20,8,128]{2,1,0:T(8,128)S(1)}, u32[]{:S(2)}, u32[]{:S(2)}) collective-permute-start(f32[20,8,128]{2,1,0:T(8,128)S(1)} %get-tuple-element.34), channel_id=1, source_target_pairs={{0,1},{1,0},{2,3},{3,2},{4,5},{5,4},{6,7},{7,6},{8,9},{9,8},{10,11... | collective-permute-start | bytes 245768 | tf_op jit(solution)/shard_map/ppermute | solution.py:802
  18.2 0.3 collective-permute-done.6.refs_0_
  18.5 0.2 collective-permute-done.7.refs_1_
  18.6 0.4 %collective-permute-done.8.refs_2_ = f32[20,8,128]{2,1,0:T(8,128)S(1)} collective-permute-done((f32[20,8,128]{2,1,0:T(8,128)S(1)}, f32[20,8,128]{2,1,0:T(8,128)S(1)}, u32[]{:S(2)}, u32[]{:S(2)}) %collective-permute-start.8) | collective-permute-done | bytes 81952 | tf_op jit(solution)/shard_map/ppermute | solution.py:802
  19.0 0.2 collective-permute-done.9.refs_3_
  19.1 0.4 %assemble.1 = (f32[16,10,8,128]{3,2,1,0:T(8,128)S(1)}, f32[16,5,8,128]{3,2,1,0:T(8,128)S(1)}, f32[16,5,8,128]{3,2,1,0:T(8,128)S(1)}) custom-call(f32[16,10,8,128]{3,2,1,0:T(8,128)S(1)} %get-tuple-element.30.known, f32[80,8,128]{2,1,0:T(8,128)S(1)} %collective-permute-done.4.whole.across, ...), custom_call_target="tpu_custom_call", output_to_operand_aliasing={{0}: (0, {})} | custom-call | tf_op jit(solution)/shard_map/assemble/pallas_call | solution.py:724
  19.6 5.2 %all-to-all-done.refs_5_ = f32[32,8,128]{2,1,0:T(8,128)S(1)} async-done(((f32[32,8,128]{2,1,0:T(8,128)}), f32[32,8,128]{2,1,0:T(8,128)S(1)}, u32[]{:S(2)}, u32[]{:S(2)}) %all-to-all-start) | async-done | bytes 131104 | tf_op jit(solution)/shard_map/all_to_all | solution.py:799
  24.8 3.5 %finish.1 = f32[1,8,5,16,256]{4,3,2,1,0:T(8,128)} custom-call(f32[21,8,128]{2,1,0:T(8,128)S(1)} %get-tuple-element.22.shared.refs_0_, f32[21,8,128]{2,1,0:T(8,128)S(1)} %collective-permute-done.refs_1_.partner, f32[1,8,128]{2,1,0:T(8,128)S(1)} %collective-permute-done.1.refs_2_, f32[21,8,128]{2,1,0:T(8,128)S(1)} %collective-permute-done.2.refs_3_.last, ...), custom_call_target="tpu_custom_call" | custom-call | tf_op jit(solution)/shard_map/finish/pallas_call | solution.py:724
  (8 shorter events, 0.0 us)
Async XLA Ops:
  1.0 5.8 %collective-permute-start = (f32[21,8,128]{2,1,0:T(8,128)S(1)}, f32[21,8,128]{2,1,0:T(8,128)S(1)}, u32[]{:S(2)}, u32[]{:S(2)}) collective-permute-start(f32[21,8,128]{2,1,0:T(8,128)S(1)} %get-tuple-element.22.shared.refs_0_), channel_id=1, source_target_pairs={{0,2},{1,3},{2,0},{3,1},{4,6},{5,7},{6,4},{7,5},{8,10},{9,11},{10,... | collective-permute-start | bytes 258056 | tf_op jit(solution)/shard_map/ppermute | solution.py:756
  4.1 2.7 %collective-permute-start.1 = (f32[1,8,128]{2,1,0:T(8,128)S(1)}, f32[1,8,128]{2,1,0:T(8,128)S(1)}, u32[]{:S(2)}, u32[]{:S(2)}) collective-permute-start(f32[1,8,128]{2,1,0:T(8,128)S(1)} %get-tuple-element.24), channel_id=1, source_target_pairs={{0,1},{1,0},{2,3},{3,2},{4,5},{5,4},{6,7},{7,6},{8,9},{9,8},{10,11... | collective-permute-start | bytes 12296 | tf_op jit(solution)/shard_map/ppermute | solution.py:757
  6.8 3.0 %collective-permute-start.3 = (f32[80,8,128]{2,1,0:T(8,128)S(1)}, f32[80,8,128]{2,1,0:T(8,128)S(1)}, u32[]{:S(2)}, u32[]{:S(2)}) collective-permute-start(f32[80,8,128]{2,1,0:T(8,128)S(1)} %get-tuple-element.27.refs_4_), channel_id=1, source_target_pairs={{0,1},{1,0},{2,3},{3,2},{4,5},{5,4},{6,7},{7,6},{8,9},{9,8},{10,11... | collective-permute-start | bytes 983048 | tf_op jit(solution)/shard_map/ppermute | solution.py:776
  7.4 9.7 %collective-permute-start.4 = (f32[80,8,128]{2,1,0:T(8,128)S(1)}, f32[80,8,128]{2,1,0:T(8,128)S(1)}, u32[]{:S(2)}, u32[]{:S(2)}) collective-permute-start(f32[80,8,128]{2,1,0:T(8,128)S(1)} %get-tuple-element.27.refs_4_), channel_id=1, source_target_pairs={{0,2},{1,3},{2,0},{3,1},{4,6},{5,7},{6,4},{7,5},{8,10},{9,11},{10,... | collective-permute-start | bytes 983048 | tf_op jit(solution)/shard_map/ppermute | solution.py:778
  8.6 1.3 %collective-permute-start.2 = (f32[21,8,128]{2,1,0:T(8,128)S(1)}, f32[21,8,128]{2,1,0:T(8,128)S(1)}, u32[]{:S(2)}, u32[]{:S(2)}) collective-permute-start(f32[21,8,128]{2,1,0:T(8,128)S(1)} %collective-permute-done.refs_1_.partner), channel_id=1, source_target_pairs={{0,1},{1,0},{2,3},{3,2},{4,5},{5,4},{6,7},{7,6},{8,9},{9,8},{10,11... | collective-permute-start | bytes 258056 | tf_op jit(solution)/shard_map/ppermute | solution.py:777
  11.3 13.4 %all-to-all-start = ((f32[32,8,128]{2,1,0:T(8,128)}), f32[32,8,128]{2,1,0:T(8,128)S(1)}, u32[]{:S(2)}, u32[]{:S(2)}) async-start(f32[32,8,128]{2,1,0:T(8,128)} %get-tuple-element.29), calls=%async_computation | async-start | bytes 262144 | tf_op jit(solution)/shard_map/all_to_all | solution.py:799
  16.6 1.7 %collective-permute-start.5 = (f32[21,8,128]{2,1,0:T(8,128)S(1)}, f32[21,8,128]{2,1,0:T(8,128)S(1)}, u32[]{:S(2)}, u32[]{:S(2)}) collective-permute-start(f32[21,8,128]{2,1,0:T(8,128)S(1)} %get-tuple-element.22.shared.refs_0_), channel_id=1, source_target_pairs={{0,1},{1,0},{2,3},{3,2},{4,5},{5,4},{6,7},{7,6},{8,9},{9,8},{10,11... | collective-permute-start | bytes 258056 | tf_op jit(solution)/shard_map/ppermute | solution.py:803
  17.1 2.0 %copy-start.1 = (f32[5,5]{1,0:T(8,128)S(1)}, f32[5,5]{1,0:T(8,128)}, u32[]{:S(2)}) copy-start(f32[5,5]{1,0:T(8,128)} %refs_4_.3) | copy-start | bytes 304
  17.1 1.3 %collective-permute-start.6 = (f32[20,8,128]{2,1,0:T(8,128)S(1)}, f32[20,8,128]{2,1,0:T(8,128)S(1)}, u32[]{:S(2)}, u32[]{:S(2)}) collective-permute-start(f32[20,8,128]{2,1,0:T(8,128)S(1)} %get-tuple-element.31), channel_id=1, source_target_pairs={{0,1},{1,0},{2,3},{3,2},{4,5},{5,4},{6,7},{7,6},{8,9},{9,8},{10,11... | collective-permute-start | bytes 245768 | tf_op jit(solution)/shard_map/ppermute | solution.py:802
  17.2 1.4 %collective-permute-start.7 = (f32[20,8,128]{2,1,0:T(8,128)S(1)}, f32[20,8,128]{2,1,0:T(8,128)S(1)}, u32[]{:S(2)}, u32[]{:S(2)}) collective-permute-start(f32[20,8,128]{2,1,0:T(8,128)S(1)} %get-tuple-element.32), channel_id=1, source_target_pairs={{0,1},{1,0},{2,3},{3,2},{4,5},{5,4},{6,7},{7,6},{8,9},{9,8},{10,11... | collective-permute-start | bytes 245768 | tf_op jit(solution)/shard_map/ppermute | solution.py:802
  17.7 1.3 %collective-permute-start.8 = (f32[20,8,128]{2,1,0:T(8,128)S(1)}, f32[20,8,128]{2,1,0:T(8,128)S(1)}, u32[]{:S(2)}, u32[]{:S(2)}) collective-permute-start(f32[20,8,128]{2,1,0:T(8,128)S(1)} %get-tuple-element.33), channel_id=1, source_target_pairs={{0,1},{1,0},{2,3},{3,2},{4,5},{5,4},{6,7},{7,6},{8,9},{9,8},{10,11... | collective-permute-start | bytes 245768 | tf_op jit(solution)/shard_map/ppermute | solution.py:802
  17.8 1.4 %collective-permute-start.9 = (f32[20,8,128]{2,1,0:T(8,128)S(1)}, f32[20,8,128]{2,1,0:T(8,128)S(1)}, u32[]{:S(2)}, u32[]{:S(2)}) collective-permute-start(f32[20,8,128]{2,1,0:T(8,128)S(1)} %get-tuple-element.34), channel_id=1, source_target_pairs={{0,1},{1,0},{2,3},{3,2},{4,5},{5,4},{6,7},{7,6},{8,9},{9,8},{10,11... | collective-permute-start | bytes 245768 | tf_op jit(solution)/shard_map/ppermute | solution.py:802
  19.1 5.6 %copy-start = (f32[1,8,5,16,256]{4,3,2,1,0:T(8,128)S(1)}, f32[1,8,5,16,256]{4,3,2,1,0:T(8,128)}, u32[]{:S(2)}) copy-start(f32[1,8,5,16,256]{4,3,2,1,0:T(8,128)} %refs_10_.1) | copy-start | bytes 1966084

commit v6 on v5

--- a/solution.py
+++ b/solution.py
@@ -257,7 +257,7 @@
 
 
 def pack_kernel(
-    sizes, counts, ids, diagonal, donors, offsets, receptors, out, meta, held, rows, cells, planes_of, allowed, sems
+    sizes, counts, ids, diagonal, donors, offsets, receptors, out, held, rows, cells, planes_of, allowed, sems
 ):
     planes, variables, height, depth = sizes["coarse"]
     slots = sizes["slots"]
@@ -285,7 +285,6 @@
         out[count, k + 1 : k + 2, 0:slots] = rows[k]
     out[count, 4:5, 0:slots] = cell.astype(F32)
     out[count, 5:6, 0 : sizes["blocks"]] = planes_of[...].astype(F32)
-    meta[0] = out[count]
 
 
 def find_corners(sizes, shared, out):
@@ -413,8 +412,9 @@
 def partial_kernel(sizes, *refs):
     subs, grids, slots, blocks = sizes["subs"], sizes["grids"], sizes["slots"], sizes["blocks"]
     planes, variables, height, depth = sizes["coarse"]
-    known = refs[:subs]
-    own, mate, corners = refs[subs:-8]
+    *known, own, corners = refs[:-8]
+    joined = known[2]
+    known = four_blocks(sizes, known)
     out, mask_out, both, rows, stage, pair, padded, wet = refs[-8:]
     total = subs * planes
     sub_index = lax.axis_index("sub")
@@ -429,7 +429,7 @@
     padded[...] = jnp.zeros(padded.shape, F32)
     inner = padded.at[1 : total + 1]
     add_planes(sizes, [own], plane_numbers(known[0][count], blocks), inner)
-    add_planes(sizes, [mate], plane_numbers(known[2][0], blocks), inner)
+    add_planes(sizes, [joined], plane_numbers(known[2][count], blocks), inner)
     both[...] = padded[1 : total + 1]
     core = sub_index % 2
     fields = []
@@ -468,7 +468,7 @@
 
 def add_planes(sizes, pieces, numbers, both):
     variables, blocks = sizes["coarse"][1], sizes["blocks"]
-    width = pieces[0].shape[0] // variables
+    width = min(pieces[0].shape[0] // variables, 2 * blocks)
     for q in range(blocks):
         coarse = pl.ds(numbers[q] // 2, 1)
         for k in range(2):
@@ -478,6 +478,19 @@
             both[coarse, pl.ds(k * variables, variables)] += part[None]
 
 
+def join_kernel(sizes, *refs):
+    at = 0
+    for part in refs[:-1]:
+        refs[-1][at : at + part.shape[0]] = part[...]
+        at = at + part.shape[0]
+
+
+def four_blocks(sizes, known):
+    shared, partner, joined, last = known
+    size = shared.shape[0]
+    return shared, partner, joined.at[joined.shape[0] - size :], last
+
+
 def split_kernel(sizes, whole, *pieces):
     at = 0
     for piece in pieces:
@@ -485,20 +498,22 @@
         at = at + piece.shape[0]
 
 
-def assemble_kernel(sizes, known, across, shared, partner, beside, last, *refs):
+def assemble_kernel(sizes, before, across, shared, partner, joined, last, *refs):
     variables = sizes["coarse"][1]
     pieces = refs[:-4]
     coupling, both, source, gain = refs[-4:]
     planes = sizes["coarse"][0]
-    for part, bit in ((shared, 0), (partner, 2), (beside, 1), (last, 3)):
+    known = four_blocks(sizes, (shared, partner, joined, last))
+    for part, bit in zip(known, (0, 2, 1, 3)):
         owner = lax.axis_index("sub") ^ bit
-        here = part[0 : planes * variables].reshape(sizes["coarse"])
+        end = part.shape[0] - 1
+        here = part[end - planes * variables : end].reshape(sizes["coarse"])
         gain[pl.ds(owner * planes, planes)] = here
     count = planes * variables
     blocks = sizes["blocks"]
-    both[...] = known[...]
+    both[...] = before[...]
     add_planes(sizes, [across], plane_numbers(partner[count], blocks), both)
-    add_planes(sizes, pieces, plane_numbers(last[count], blocks), both)
+    add_planes(sizes, pieces, plane_numbers(known[3][count], blocks), both)
     source[...] = couple(coupling, both[:, 0:variables])
 
 
@@ -586,10 +601,15 @@
     which = iota(ours.shape, 0) % 8
     mine = [jnp.where(which == g, ours, 0.0).astype(BF16) for g in range(grids)]
     closeness = jnp.dot(theirs, jnp.concatenate(mine, axis=1), preferred_element_type=F32)
-    wet = jnp.maximum(jnp.max(closeness, axis=0, keepdims=True) - 1.0, 0.0)
-    match = jnp.maximum(closeness - wet, 0.0).astype(BF16)
+    closeness = closeness.astype(BF16)
+    most = closeness
+    while most.shape[0] > 16:
+        half = most.shape[0] // 2
+        most = jnp.maximum(most[:half], most[half:])
+    wet = jnp.max(most.astype(F32), axis=0, keepdims=True) - 1.0
+    match = jnp.maximum(closeness - jnp.maximum(wet, 0.0).astype(BF16), 0.0)
     lanes = subs * slots
-    total = [jnp.zeros((8, LANES), F32), jnp.zeros((8, LANES), F32)]
+    values = [[], []]
     for g in range(grids):
         sent = landing[g]
         high = sent.astype(BF16).astype(F32)
@@ -597,11 +617,25 @@
         near = jnp.dot(stacked, match[:, g * lanes : (g + 1) * lanes], preferred_element_type=F32)
         near = near[0:8] + near[8:16]
         for k in range(2):
-            value = near[:, k * LANES : (k + 1) * LANES] * scales[g][k]
-            for shift in (32, 16, 8):
-                value = value + pltpu.roll(value, LANES - shift, 1)
-            value = pltpu.roll(value, 8 * g, 1) + firsts[g][k]
-            total[k] = jnp.where(group == g, value, total[k])
+            values[k].append(near[:, k * LANES : (k + 1) * LANES] * scales[g][k])
+    total = []
+    for k in range(2):
+        parts = values[k]
+        for bit in (4, 2, 1):
+            width = 8 * bit
+            lower = lane // width % 2 == 0
+            parts = [
+                jnp.where(
+                    lower,
+                    one + pltpu.roll(one, LANES - width, 1),
+                    two + pltpu.roll(two, width, 1),
+                )
+                for one, two in zip(parts[:bit], parts[bit:])
+            ]
+        known = firsts[0][k]
+        for g in range(1, grids):
+            known = jnp.where(group == g, firsts[g][k], known)
+        total.append(parts[0] + known)
     return landing[lax.axis_index("grid")], jnp.concatenate(total, axis=1)
 
 
@@ -635,9 +669,9 @@
     subs = sizes["subs"]
     planes, variables, height, depth = sizes["coarse"]
     blocks = sizes["blocks"]
-    parts = refs[:subs]
-    coupling, arrived, both, source, gain, mask, fine = refs[subs : subs + 7]
-    out, landing, stage, rows, padded, tall, held, sems = refs[subs + 7 :]
+    parts = four_blocks(sizes, refs[:4])
+    coupling, arrived, both, source, gain, mask, fine = refs[4:11]
+    out, landing, stage, rows, padded, tall, held, sems = refs[11:]
     total = subs * planes
     gather_rows(sizes, parts, stage, rows)
     first, second = fringe_values(sizes, arrived, landing)
@@ -715,7 +749,7 @@
     rows = pltpu.VMEM((8, subs * slots), F32)
     stage = pltpu.VMEM((subs, 8, depth), F32)
 
-    def call(kernel, name, out_shape, *operands, scratch=(), far=(), out_spec=VMEM, aliases={}):
+    def call(kernel, name, out_shape, *operands, scratch=(), far=(), out_spec=VMEM, aliases={}, cost=None):
         specs = [HBM if any(one is each for each in far) else VMEM for one in operands]
         operands = [
             pltpu.with_memory_space_constraint(one, pltpu.HBM) if spec is HBM else one
@@ -728,19 +762,17 @@
             out_specs=jax.tree.map(lambda _: out_spec, out_shape),
             scratch_shapes=list(scratch),
             input_output_aliases=aliases,
+            cost_estimate=cost,
             compiler_params=pltpu.CompilerParams(vmem_limit_bytes=48 * 1024 * 1024),
             name=name,
         )(*operands)
 
     offsets = donor_offsets.transpose(0, 2, 1, 3)
     inputs = (fringe_counts, plane_of_slot, coarse_diagonal, donor_cells, offsets, receptor_cells)
-    shared, meta = call(
+    shared = call(
         pack_kernel,
         "pack",
-        [
-            jax.ShapeDtypeStruct((planes * variables + 1, height, depth), F32),
-            jax.ShapeDtypeStruct((1, height, depth), F32),
-        ],
+        jax.ShapeDtypeStruct((planes * variables + 1, height, depth), F32),
         *inputs,
         far=inputs,
         scratch=[
@@ -754,7 +786,6 @@
     )
     swap = {bit: [(i, i ^ bit) for i in range(subs)] for bit in (1, 2)}
     partner = lax.ppermute(shared, "sub", swap[2])
-    beside = lax.ppermute(meta, "sub", swap[1])
     own, corners = call(
         restrict_kernel,
         "restrict",
@@ -772,9 +803,16 @@
             pltpu.SemaphoreType.DMA((blocks,)),
         ],
     )
-    own, partner, beside = lax.optimization_barrier((own, partner, beside))
-    mate = lax.ppermute(own, "sub", swap[1])
-    known = (shared, partner, beside, lax.ppermute(partner, "sub", swap[1]))
+    size = own.shape[0] + shared.shape[0]
+    joined = call(
+        join_kernel, "join", jax.ShapeDtypeStruct((size, height, depth), F32), own, shared
+    )
+    joined = lax.ppermute(joined, "sub", swap[1])
+    own, partner = lax.optimization_barrier((own, partner))
+    partner = call(
+        join_kernel, "pass", jax.ShapeDtypeStruct(partner.shape, F32), partner, cost=pl.CostEstimate(flops=20_000_000_000, transcendentals=0, bytes_accessed=100_000_000)
+    )
+    known = (shared, partner, joined, lax.ppermute(partner, "sub", swap[1]))
     across = lax.ppermute(own, "sub", swap[2])
     out, mask, both = call(
         partial_kernel,
@@ -786,8 +824,8 @@
         ],
         *known,
         own,
-        mate,
         corners,
+        cost=pl.CostEstimate(flops=20_000_000_000, transcendentals=0, bytes_accessed=100_000_000),
         scratch=[
             rows,
             stage,
@@ -800,17 +838,13 @@
     piece = jax.ShapeDtypeStruct((blocks // 2 * variables, height, depth), F32)
     pieces = call(split_kernel, "split", [piece] * 4, across)
     pieces = [lax.ppermute(each, "sub", swap[1]) for each in pieces]
-    beside_gain = lax.ppermute(shared, "sub", swap[1])
     both, source, gain = call(
         assemble_kernel,
         "assemble",
         [jax.ShapeDtypeStruct(both.shape, F32), full, full],
         both,
         across,
-        shared,
-        partner,
-        beside_gain,
-        known[3],
+        *known,
         *pieces,
         coupling,
         aliases={0: 0},

time: 28.5 us -> 27.5 us (0.965)
  waiting for transfers between devices: 7.43 us -> 6.76 us
    ppermute x1, waiting for transfers between devices: 0.22 us -> 1.44 us  [fast_shards(): across = lax.ppermute(own, 'sub', swap[2])]
    ppermute x4 -> x2, waiting for transfers between devices: 1.06 us -> 0.08 us  [the longest x1 0.08 us: fast_shards(): known = (shared, partner, joined, lax.ppermute(partner, 'sub', swap[1]))]
    all_to_all x1, waiting for transfers between devices: 5.22 us -> 4.32 us  [fast_shards(): arrived = lax.all_to_all(out, ('grid', 'sub'), 0, 0, tiled=True)]
    ppermute x4 -> x2, starting transfers between devices: 1.12 us -> 0.62 us  [the longest x1 0.55 us: fast_shards(): known = (shared, partner, joined, lax.ppermute(partner, 'sub', swap[1]))]
    pallas_call x6 -> x8, Pallas kernels: 9.17 us -> 9.05 us  [call(): pl.pallas_call(functools.partial(kernel, sizes), out_shape=out_shape, in_...]
  transfers between devices with their start and end apart: 11 -> 9, of which waited for: 7 -> 7; matrix products, arithmetic and copies ran while one was open for 0% -> 0% of each run, Pallas kernels for 16% -> 17%
where the time goes in v6:
time: 27.5 us; the launch traced here: 27.3 us
  starting transfers between devices  11.4 us (41%)
  Pallas kernels  9.05 us (33%)
  waiting for transfers between devices  6.76 us (25%)
    pallas_call x8, Pallas kernels, call(): pl.pallas_call(functools.partial(kernel, sizes), out_shape=out_shape, in_...  9.05 us
    all_to_all x1, starting transfers between devices, fast_shards(): arrived = lax.all_to_all(out, ('grid', 'sub'), 0, 0, tiled=True)  5.46 us
    all_to_all x1, waiting for transfers between devices, fast_shards(): arrived = lax.all_to_all(out, ('grid', 'sub'), 0, 0, tiled=True)  4.32 us
    ppermute x1, starting transfers between devices, fast_shards(): partner = lax.ppermute(shared, 'sub', swap[2])  3.03 us
    ppermute x1, waiting for transfers between devices, fast_shards(): across = lax.ppermute(own, 'sub', swap[2])  1.44 us
    ppermute x1, starting transfers between devices, fast_shards(): across = lax.ppermute(own, 'sub', swap[2])  1.21 us
    ppermute x4, starting transfers between devices, fast_shards(): pieces = [lax.ppermute(each, 'sub', swap[1]) for each in pieces]  1.08 us
    ppermute x4, waiting for transfers between devices, fast_shards(): pieces = [lax.ppermute(each, 'sub', swap[1]) for each in pieces]  0.92 us
  transfers between devices with their start and end apart: 9, of which 7 were waited for; matrix products, arithmetic and copies ran while one was open for 0% of the time, Pallas kernels for 17%

profile of v6, /device:TPU:0, one launch (start us, length us, event | category | flops | bytes accessed | tf_op | source)
XLA Modules:
  0.0 27.3 jit_solution(7506885006381846387)
XLA Ops:
  0.0 1.0 %pack.1.shared.refs_1_.refs_0_ = f32[21,8,128]{2,1,0:T(8,128)S(1)} custom-call(s32[8,8]{1,0:T(8,128)} %counts.1, s32[1,8]{1,0:T(1,128)} %ids.1, f32[1,4,5,8,128]{4,3,2,1,0:T(8,128)} %diagonal.1, s32[1,1,64]{2,1,0:T(1,128)} %donors.1, f32[1,3,1,64]{3,2,1,0:T(1,128)} %bitcast.1, s32[1,1,64]{2,1,0:T(1,128)} %receptors.1), custom_call_target="tpu_custom_call" | custom-call | tf_op jit(solution)/shard_map/pack/pallas_call | solution.py:758
  1.0 3.0 %collective-permute-start = (f32[21,8,128]{2,1,0:T(8,128)S(1)}, f32[21,8,128]{2,1,0:T(8,128)S(1)}, u32[]{:S(2)}, u32[]{:S(2)}) collective-permute-start(f32[21,8,128]{2,1,0:T(8,128)S(1)} %pack.1.shared.refs_1_.refs_0_), channel_id=1, source_target_pairs={{0,2},{1,3},{2,0},{3,1},{4,6},{5,7},{6,4},{7,5},{8,10},{9,11},{10,... | collective-permute-start | bytes 258056 | tf_op jit(solution)/shard_map/ppermute | solution.py:788
  4.1 2.7 %restrict.1 = (f32[80,8,128]{2,1,0:T(8,128)S(1)}, f32[8,8,128]{2,1,0:T(8,128)S(1)}) custom-call(f32[1,8,5,16,256]{4,3,2,1,0:T(8,128)} %residual.1, f32[1,8,5,16,256]{4,3,2,1,0:T(8,128)} %refs_10_.1, f32[21,8,128]{2,1,0:T(8,128)S(1)} %pack.1.shared.refs_1_.refs_0_), custom_call_target="tpu_custom_call" | custom-call | tf_op jit(solution)/shard_map/restrict/pallas_call | solution.py:758
  6.8 0.1 collective-permute-start.1
  6.9 0.0 collective-permute-done.refs_0_
  6.9 0.5 %collective-permute-start.2 = (f32[21,8,128]{2,1,0:T(8,128)S(1)}, f32[21,8,128]{2,1,0:T(8,128)S(1)}, u32[]{:S(2)}, u32[]{:S(2)}) collective-permute-start(f32[21,8,128]{2,1,0:T(8,128)S(1)} %pass.1.refs_1_.partner), channel_id=1, source_target_pairs={{0,1},{1,0},{2,3},{3,2},{4,5},{5,4},{6,7},{7,6},{8,9},{9,8},{10,11... | collective-permute-start | bytes 258056 | tf_op jit(solution)/shard_map/ppermute | solution.py:815
  7.5 1.2 %collective-permute-start.3 = (f32[80,8,128]{2,1,0:T(8,128)S(1)}, f32[80,8,128]{2,1,0:T(8,128)S(1)}, u32[]{:S(2)}, u32[]{:S(2)}) collective-permute-start(f32[80,8,128]{2,1,0:T(8,128)S(1)} %get-tuple-element.21.refs_0_.refs_4_), channel_id=1, source_target_pairs={{0,2},{1,3},{2,0},{3,1},{4,6},{5,7},{6,4},{7,5},{8,10},{9,11},{10,... | collective-permute-start | bytes 983048 | tf_op jit(solution)/shard_map/ppermute | solution.py:816
  8.7 0.1 collective-permute-done.2.refs_3_.last
  8.8 0.0 collective-permute-done.1.refs_2_.joined
  8.8 1.5 %partial.1 = (f32[32,8,128]{2,1,0:T(8,128)}, f32[16,1,8,128]{3,2,1,0:T(8,128)S(1)}, f32[16,10,8,128]{3,2,1,0:T(8,128)S(1)}) custom-call(f32[21,8,128]{2,1,0:T(8,128)S(1)} %pack.1.shared.refs_1_.refs_0_, f32[21,8,128]{2,1,0:T(8,128)S(1)} %pass.1.refs_1_.partner, f32[101,8,128]{2,1,0:T(8,128)S(1)} %collective-permute-done.1.refs_2_.joined, ...), custom_call_target="tpu_custom_call" | custom-call | flops 20000000000 | bytes 100000000 | tf_op jit(solution)/shard_map/partial/pallas_call | solution.py:758
  10.3 5.5 %all-to-all-start = ((f32[32,8,128]{2,1,0:T(8,128)}), f32[32,8,128]{2,1,0:T(8,128)S(1)}, u32[]{:S(2)}, u32[]{:S(2)}) async-start(f32[32,8,128]{2,1,0:T(8,128)} %get-tuple-element.23), calls=%async_computation | async-start | bytes 262144 | tf_op jit(solution)/shard_map/all_to_all | solution.py:837
  15.7 1.4 %collective-permute-done.3.whole.across = f32[80,8,128]{2,1,0:T(8,128)S(1)} collective-permute-done((f32[80,8,128]{2,1,0:T(8,128)S(1)}, f32[80,8,128]{2,1,0:T(8,128)S(1)}, u32[]{:S(2)}, u32[]{:S(2)}) %collective-permute-start.3) | collective-permute-done | bytes 327712 | tf_op jit(solution)/shard_map/ppermute | solution.py:816
  17.2 0.0 copy-start.1
  17.2 0.1 collective-permute-start.4
  17.3 0.5 %collective-permute-start.5 = (f32[20,8,128]{2,1,0:T(8,128)S(1)}, f32[20,8,128]{2,1,0:T(8,128)S(1)}, u32[]{:S(2)}, u32[]{:S(2)}) collective-permute-start(f32[20,8,128]{2,1,0:T(8,128)S(1)} %get-tuple-element.26), channel_id=1, source_target_pairs={{0,1},{1,0},{2,3},{3,2},{4,5},{5,4},{6,7},{7,6},{8,9},{9,8},{10,11... | collective-permute-start | bytes 245768 | tf_op jit(solution)/shard_map/ppermute | solution.py:840
  17.8 0.1 collective-permute-start.6
  17.9 0.4 %collective-permute-start.7 = (f32[20,8,128]{2,1,0:T(8,128)S(1)}, f32[20,8,128]{2,1,0:T(8,128)S(1)}, u32[]{:S(2)}, u32[]{:S(2)}) collective-permute-start(f32[20,8,128]{2,1,0:T(8,128)S(1)} %get-tuple-element.28), channel_id=1, source_target_pairs={{0,1},{1,0},{2,3},{3,2},{4,5},{5,4},{6,7},{7,6},{8,9},{9,8},{10,11... | collective-permute-start | bytes 245768 | tf_op jit(solution)/shard_map/ppermute | solution.py:840
  18.3 0.3 collective-permute-done.4.refs_0_
  18.6 0.2 collective-permute-done.5.refs_1_
  18.7 0.4 %collective-permute-done.6.refs_2_ = f32[20,8,128]{2,1,0:T(8,128)S(1)} collective-permute-done((f32[20,8,128]{2,1,0:T(8,128)S(1)}, f32[20,8,128]{2,1,0:T(8,128)S(1)}, u32[]{:S(2)}, u32[]{:S(2)}) %collective-permute-start.6) | collective-permute-done | bytes 81952 | tf_op jit(solution)/shard_map/ppermute | solution.py:840
  19.1 0.2 collective-permute-done.7.refs_3_
  19.2 0.4 %assemble.1 = (f32[16,10,8,128]{3,2,1,0:T(8,128)S(1)}, f32[16,5,8,128]{3,2,1,0:T(8,128)S(1)}, f32[16,5,8,128]{3,2,1,0:T(8,128)S(1)}) custom-call(f32[16,10,8,128]{3,2,1,0:T(8,128)S(1)} %get-tuple-element.24.before, f32[80,8,128]{2,1,0:T(8,128)S(1)} %collective-permute-done.3.whole.across, ...), custom_call_target="tpu_custom_call", output_to_operand_aliasing={{0}: (0, {})} | custom-call | tf_op jit(solution)/shard_map/assemble/pallas_call | solution.py:758
  19.7 4.3 %all-to-all-done.refs_5_ = f32[32,8,128]{2,1,0:T(8,128)S(1)} async-done(((f32[32,8,128]{2,1,0:T(8,128)}), f32[32,8,128]{2,1,0:T(8,128)S(1)}, u32[]{:S(2)}, u32[]{:S(2)}) %all-to-all-start) | async-done | bytes 131104 | tf_op jit(solution)/shard_map/all_to_all | solution.py:837
  24.0 3.3 %finish.1 = f32[1,8,5,16,256]{4,3,2,1,0:T(8,128)} custom-call(f32[21,8,128]{2,1,0:T(8,128)S(1)} %pack.1.shared.refs_1_.refs_0_, f32[21,8,128]{2,1,0:T(8,128)S(1)} %pass.1.refs_1_.partner, f32[101,8,128]{2,1,0:T(8,128)S(1)} %collective-permute-done.1.refs_2_.joined, f32[21,8,128]{2,1,0:T(8,128)S(1)} %collective-permute-done.2.refs_3_.last, ...), custom_call_target="tpu_custom_call" | custom-call | tf_op jit(solution)/shard_map/finish/pallas_call | solution.py:758
  (6 shorter events, 0.1 us)
Async XLA Ops:
  1.0 5.9 %collective-permute-start = (f32[21,8,128]{2,1,0:T(8,128)S(1)}, f32[21,8,128]{2,1,0:T(8,128)S(1)}, u32[]{:S(2)}, u32[]{:S(2)}) collective-permute-start(f32[21,8,128]{2,1,0:T(8,128)S(1)} %pack.1.shared.refs_1_.refs_0_), channel_id=1, source_target_pairs={{0,2},{1,3},{2,0},{3,1},{4,6},{5,7},{6,4},{7,5},{8,10},{9,11},{10,... | collective-permute-start | bytes 258056 | tf_op jit(solution)/shard_map/ppermute | solution.py:788
  6.8 1.9 %collective-permute-start.1 = (f32[101,8,128]{2,1,0:T(8,128)S(1)}, f32[101,8,128]{2,1,0:T(8,128)S(1)}, u32[]{:S(2)}, u32[]{:S(2)}) collective-permute-start(f32[101,8,128]{2,1,0:T(8,128)S(1)} %join.1), channel_id=1, source_target_pairs={{0,1},{1,0},{2,3},{3,2},{4,5},{5,4},{6,7},{7,6},{8,9},{9,8},{10,11... | collective-permute-start | bytes 1241096 | tf_op jit(solution)/shard_map/ppermute | solution.py:810
  6.9 1.8 %collective-permute-start.2 = (f32[21,8,128]{2,1,0:T(8,128)S(1)}, f32[21,8,128]{2,1,0:T(8,128)S(1)}, u32[]{:S(2)}, u32[]{:S(2)}) collective-permute-start(f32[21,8,128]{2,1,0:T(8,128)S(1)} %pass.1.refs_1_.partner), channel_id=1, source_target_pairs={{0,1},{1,0},{2,3},{3,2},{4,5},{5,4},{6,7},{7,6},{8,9},{9,8},{10,11... | collective-permute-start | bytes 258056 | tf_op jit(solution)/shard_map/ppermute | solution.py:815
  7.5 9.7 %collective-permute-start.3 = (f32[80,8,128]{2,1,0:T(8,128)S(1)}, f32[80,8,128]{2,1,0:T(8,128)S(1)}, u32[]{:S(2)}, u32[]{:S(2)}) collective-permute-start(f32[80,8,128]{2,1,0:T(8,128)S(1)} %get-tuple-element.21.refs_0_.refs_4_), channel_id=1, source_target_pairs={{0,2},{1,3},{2,0},{3,1},{4,6},{5,7},{6,4},{7,5},{8,10},{9,11},{10,... | collective-permute-start | bytes 983048 | tf_op jit(solution)/shard_map/ppermute | solution.py:816
  10.3 13.7 %all-to-all-start = ((f32[32,8,128]{2,1,0:T(8,128)}), f32[32,8,128]{2,1,0:T(8,128)S(1)}, u32[]{:S(2)}, u32[]{:S(2)}) async-start(f32[32,8,128]{2,1,0:T(8,128)} %get-tuple-element.23), calls=%async_computation | async-start | bytes 262144 | tf_op jit(solution)/shard_map/all_to_all | solution.py:837
  17.2 2.0 %copy-start.1 = (f32[5,5]{1,0:T(8,128)S(1)}, f32[5,5]{1,0:T(8,128)}, u32[]{:S(2)}) copy-start(f32[5,5]{1,0:T(8,128)} %refs_4_.3) | copy-start | bytes 304
  17.2 1.3 %collective-permute-start.4 = (f32[20,8,128]{2,1,0:T(8,128)S(1)}, f32[20,8,128]{2,1,0:T(8,128)S(1)}, u32[]{:S(2)}, u32[]{:S(2)}) collective-permute-start(f32[20,8,128]{2,1,0:T(8,128)S(1)} %get-tuple-element.25), channel_id=1, source_target_pairs={{0,1},{1,0},{2,3},{3,2},{4,5},{5,4},{6,7},{7,6},{8,9},{9,8},{10,11... | collective-permute-start | bytes 245768 | tf_op jit(solution)/shard_map/ppermute | solution.py:840
  17.3 1.4 %collective-permute-start.5 = (f32[20,8,128]{2,1,0:T(8,128)S(1)}, f32[20,8,128]{2,1,0:T(8,128)S(1)}, u32[]{:S(2)}, u32[]{:S(2)}) collective-permute-start(f32[20,8,128]{2,1,0:T(8,128)S(1)} %get-tuple-element.26), channel_id=1, source_target_pairs={{0,1},{1,0},{2,3},{3,2},{4,5},{5,4},{6,7},{7,6},{8,9},{9,8},{10,11... | collective-permute-start | bytes 245768 | tf_op jit(solution)/shard_map/ppermute | solution.py:840
  17.8 1.3 %collective-permute-start.6 = (f32[20,8,128]{2,1,0:T(8,128)S(1)}, f32[20,8,128]{2,1,0:T(8,128)S(1)}, u32[]{:S(2)}, u32[]{:S(2)}) collective-permute-start(f32[20,8,128]{2,1,0:T(8,128)S(1)} %get-tuple-element.27), channel_id=1, source_target_pairs={{0,1},{1,0},{2,3},{3,2},{4,5},{5,4},{6,7},{7,6},{8,9},{9,8},{10,11... | collective-permute-start | bytes 245768 | tf_op jit(solution)/shard_map/ppermute | solution.py:840
  17.9 1.4 %collective-permute-start.7 = (f32[20,8,128]{2,1,0:T(8,128)S(1)}, f32[20,8,128]{2,1,0:T(8,128)S(1)}, u32[]{:S(2)}, u32[]{:S(2)}) collective-permute-start(f32[20,8,128]{2,1,0:T(8,128)S(1)} %get-tuple-element.28), channel_id=1, source_target_pairs={{0,1},{1,0},{2,3},{3,2},{4,5},{5,4},{6,7},{7,6},{8,9},{9,8},{10,11... | collective-permute-start | bytes 245768 | tf_op jit(solution)/shard_map/ppermute | solution.py:840
  19.2 4.7 %copy-start = (f32[1,8,5,16,256]{4,3,2,1,0:T(8,128)S(1)}, f32[1,8,5,16,256]{4,3,2,1,0:T(8,128)}, u32[]{:S(2)}) copy-start(f32[1,8,5,16,256]{4,3,2,1,0:T(8,128)} %refs_10_.1) | copy-start | bytes 1966084

commit v7 on v6

--- a/solution.py
+++ b/solution.py
@@ -193,18 +193,21 @@
     return high, (values - high.astype(F32)).astype(BF16)
 
 
-def dot_exact(values, matrix, contract=(((1,), (0,)), ((), ()))):
-    high, low = two_pieces(values)
-    total = lax.dot_general(low, matrix, contract, preferred_element_type=F32)
-    return total + lax.dot_general(high, matrix, contract, preferred_element_type=F32)
+def dot_exact(values, matrix):
+    parts = jnp.concatenate(two_pieces(values), axis=1)
+    return jnp.dot(
+        parts, jnp.concatenate([matrix, matrix], axis=0), preferred_element_type=F32
+    )
 
 
 def dot_near(values, matrix):
     high, low = two_pieces(values)
     matrix_high, matrix_low = two_pieces(matrix)
-    total = jnp.dot(low, matrix_high, preferred_element_type=F32)
-    total = total + jnp.dot(high, matrix_low, preferred_element_type=F32)
-    return total + jnp.dot(high, matrix_high, preferred_element_type=F32)
+    return jnp.dot(
+        jnp.concatenate([high, low, high], axis=1),
+        jnp.concatenate([matrix_high, matrix_high, matrix_low], axis=0),
+        preferred_element_type=F32,
+    )
 
 
 def iota(shape, dim):
@@ -344,14 +347,14 @@
         out[h] = jnp.where(mine, pltpu.roll(starts, (LANES - 8 * h) % LANES, 1), tile)
 
 
-def restrict_kernel(sizes, residual, fine, shared, out, corners, held, wide, sems):
+def restrict_kernel(sizes, residual, fine, shared, out, corners, fine_here, held, wide, sems):
     planes, variables, height, depth = sizes["coarse"]
     blocks = sizes["blocks"]
     step = 8
     copies = start_copies(
         [
-            (source.at[0, q : q + step], held.at[k, q : q + step])
-            for k, source in enumerate((fine, residual))
+            (source.at[0, q : q + step], target.at[q : q + step])
+            for source, target in ((fine, fine_here), (residual, held))
             for q in range(0, blocks, step)
         ],
         sems,
@@ -364,7 +367,7 @@
     for i, copy in enumerate(copies):
         k, q = divmod(i * step, blocks)
         copy.wait()
-        rows = held[k, q : q + step].reshape(count * 2 * height, 2 * depth)
+        rows = (fine_here, held)[k][q : q + step].reshape(count * 2 * height, 2 * depth)
         here = pl.ds(i * count, count)
         wide[here] = dot_exact(rows, pair).reshape(count, 2 * height, depth)
         out[here] = (
@@ -655,14 +658,14 @@
         for tile in tiles:
             for k in (0, 1):
                 rows[k].append(tile[k] * here)
-    contract = (((1,), (1,)), ((), ()))
-    high, low = [
-        lax.dot_general(
-            jnp.concatenate(rows[k], axis=0), onehot, contract, preferred_element_type=F32
-        )
-        for k in (0, 1)
-    ]
-    return (high + low).reshape(total, 2 * pairs, height, depth)
+    values = jnp.concatenate([jnp.concatenate(each, axis=0) for each in rows], axis=1)
+    field = lax.dot_general(
+        values,
+        jnp.concatenate([onehot, onehot], axis=1),
+        (((1,), (1,)), ((), ())),
+        preferred_element_type=F32,
+    )
+    return field.reshape(total, 2 * pairs, height, depth)
 
 
 def finish_kernel(sizes, *refs):
@@ -714,7 +717,7 @@
             rows_in = tall[low * variables : (q + 1) * variables]
             prolonged = dot_exact(rows_in.reshape(step * variables * 2 * height, depth), widen)
             shape = (step, variables, 2 * height, 2 * depth)
-            held[low : q + 1] = fine[0, low : q + 1] + prolonged.reshape(shape)
+            held[low : q + 1] = fine[low : q + 1] + prolonged.reshape(shape)
             copy = pltpu.make_async_copy(
                 held.at[low : q + 1], out.at[0, low : q + 1], sems.at[q // step]
             )
@@ -786,19 +789,20 @@
     )
     swap = {bit: [(i, i ^ bit) for i in range(subs)] for bit in (1, 2)}
     partner = lax.ppermute(shared, "sub", swap[2])
-    own, corners = call(
+    own, corners, fine_here = call(
         restrict_kernel,
         "restrict",
         [
             jax.ShapeDtypeStruct((2 * count, height, depth), F32),
             jax.ShapeDtypeStruct((grids, 8, LANES), F32),
+            jax.ShapeDtypeStruct(fine_solution.shape[1:], F32),
         ],
         fine_residual,
         fine_solution,
         shared,
         far=(fine_residual, fine_solution),
         scratch=[
-            pltpu.VMEM((2,) + fine_solution.shape[1:], F32),
+            pltpu.VMEM(fine_solution.shape[1:], F32),
             pltpu.VMEM((2 * count, 2 * height, depth), F32),
             pltpu.SemaphoreType.DMA((blocks,)),
         ],
@@ -860,7 +864,7 @@
         source,
         gain,
         mask,
-        fine_solution,
+        fine_here,
         scratch=[
             pltpu.VMEM((grids, 8, subs * slots), F32),
             stage,

time: 27.5 us -> 27.4 us (level)
  Pallas kernels: 9.05 us -> 8.4 us
  starting transfers between devices: 11.4 us -> 11.8 us
    pallas_call x8, Pallas kernels: 9.05 us -> 8.4 us  [call(): pl.pallas_call(functools.partial(kernel, sizes), out_shape=out_shape, in_...]
    ppermute x1, starting transfers between devices: 1.21 us -> 1.66 us  [fast_shards(): across = lax.ppermute(own, 'sub', swap[2])]
  transfers between devices with their start and end apart: 9 -> 9, of which waited for: 7 -> 7; matrix products, arithmetic and copies ran while one was open for 0% -> 0% of each run, Pallas kernels for 17% -> 16%
where the time goes in v7:
time: 27.4 us; the launch traced here: 27.1 us
  starting transfers between devices  11.8 us (43%)
  Pallas kernels  8.4 us (31%)
  waiting for transfers between devices  6.82 us (25%)
    pallas_call x8, Pallas kernels, call(): pl.pallas_call(functools.partial(kernel, sizes), out_shape=out_shape, in_...  8.4 us
    all_to_all x1, starting transfers between devices, fast_shards(): arrived = lax.all_to_all(out, ('grid', 'sub'), 0, 0, tiled=True)  5.53 us
    all_to_all x1, waiting for transfers between devices, fast_shards(): arrived = lax.all_to_all(out, ('grid', 'sub'), 0, 0, tiled=True)  4.5 us
    ppermute x1, starting transfers between devices, fast_shards(): partner = lax.ppermute(shared, 'sub', swap[2])  3.03 us
    ppermute x1, starting transfers between devices, fast_shards(): across = lax.ppermute(own, 'sub', swap[2])  1.66 us
    ppermute x1, waiting for transfers between devices, fast_shards(): across = lax.ppermute(own, 'sub', swap[2])  1.26 us
    ppermute x4, starting transfers between devices, fast_shards(): pieces = [lax.ppermute(each, 'sub', swap[1]) for each in pieces]  1.08 us
    ppermute x4, waiting for transfers between devices, fast_shards(): pieces = [lax.ppermute(each, 'sub', swap[1]) for each in pieces]  0.92 us
  transfers between devices with their start and end apart: 9, of which 7 were waited for; matrix products, arithmetic and copies ran while one was open for 0% of the time, Pallas kernels for 16%

profile of v7, /device:TPU:0, one launch (start us, length us, event | category | flops | bytes accessed | tf_op | source)
XLA Modules:
  0.0 27.1 jit_solution(408847557365634309)
XLA Ops:
  0.0 1.0 %pack.1.shared.refs_1_.refs_0_ = f32[21,8,128]{2,1,0:T(8,128)S(1)} custom-call(s32[8,8]{1,0:T(8,128)} %counts.1, s32[1,8]{1,0:T(1,128)} %ids.1, f32[1,4,5,8,128]{4,3,2,1,0:T(8,128)} %diagonal.1, s32[1,1,64]{2,1,0:T(1,128)} %donors.1, f32[1,3,1,64]{3,2,1,0:T(1,128)} %bitcast.1, s32[1,1,64]{2,1,0:T(1,128)} %receptors.1), custom_call_target="tpu_custom_call" | custom-call | tf_op jit(solution)/shard_map/pack/pallas_call | solution.py:761
  1.0 3.0 %collective-permute-start = (f32[21,8,128]{2,1,0:T(8,128)S(1)}, f32[21,8,128]{2,1,0:T(8,128)S(1)}, u32[]{:S(2)}, u32[]{:S(2)}) collective-permute-start(f32[21,8,128]{2,1,0:T(8,128)S(1)} %pack.1.shared.refs_1_.refs_0_), channel_id=1, source_target_pairs={{0,2},{1,3},{2,0},{3,1},{4,6},{5,7},{6,4},{7,5},{8,10},{9,11},{10,... | collective-permute-start | bytes 258056 | tf_op jit(solution)/shard_map/ppermute | solution.py:791
  4.1 2.3 %restrict.1 = (f32[80,8,128]{2,1,0:T(8,128)S(1)}, f32[8,8,128]{2,1,0:T(8,128)S(1)}, f32[8,5,16,256]{3,2,1,0:T(8,128)S(1)}) custom-call(f32[1,8,5,16,256]{4,3,2,1,0:T(8,128)} %residual.1, f32[1,8,5,16,256]{4,3,2,1,0:T(8,128)} %fine.1, f32[21,8,128]{2,1,0:T(8,128)S(1)} %pack.1.shared.refs_1_.refs_0_), custom_call_target="tpu_custom_call" | custom-call | tf_op jit(solution)/shard_map/restrict/pallas_call | solution.py:761
  6.4 0.1 collective-permute-start.1
  6.5 0.1 collective-permute-done.refs_0_
  6.6 0.4 %collective-permute-start.2 = (f32[21,8,128]{2,1,0:T(8,128)S(1)}, f32[21,8,128]{2,1,0:T(8,128)S(1)}, u32[]{:S(2)}, u32[]{:S(2)}) collective-permute-start(f32[21,8,128]{2,1,0:T(8,128)S(1)} %pass.1.refs_1_.partner), channel_id=1, source_target_pairs={{0,1},{1,0},{2,3},{3,2},{4,5},{5,4},{6,7},{7,6},{8,9},{9,8},{10,11... | collective-permute-start | bytes 258056 | tf_op jit(solution)/shard_map/ppermute | solution.py:819
  7.0 1.7 %collective-permute-start.3 = (f32[80,8,128]{2,1,0:T(8,128)S(1)}, f32[80,8,128]{2,1,0:T(8,128)S(1)}, u32[]{:S(2)}, u32[]{:S(2)}) collective-permute-start(f32[80,8,128]{2,1,0:T(8,128)S(1)} %get-tuple-element.22.refs_0_.refs_4_), channel_id=1, source_target_pairs={{0,2},{1,3},{2,0},{3,1},{4,6},{5,7},{6,4},{7,5},{8,10},{9,11},{10,... | collective-permute-start | bytes 983048 | tf_op jit(solution)/shard_map/ppermute | solution.py:820
  8.7 0.0 collective-permute-done.2.refs_3_.last
  8.7 0.0 collective-permute-done.1.refs_2_.joined
  8.7 1.5 %partial.1 = (f32[32,8,128]{2,1,0:T(8,128)}, f32[16,1,8,128]{3,2,1,0:T(8,128)S(1)}, f32[16,10,8,128]{3,2,1,0:T(8,128)S(1)}) custom-call(f32[21,8,128]{2,1,0:T(8,128)S(1)} %pack.1.shared.refs_1_.refs_0_, f32[21,8,128]{2,1,0:T(8,128)S(1)} %pass.1.refs_1_.partner, f32[101,8,128]{2,1,0:T(8,128)S(1)} %collective-permute-done.1.refs_2_.joined, ...), custom_call_target="tpu_custom_call" | custom-call | flops 20000000000 | bytes 100000000 | tf_op jit(solution)/shard_map/partial/pallas_call | solution.py:761
  10.2 5.5 %all-to-all-start = ((f32[32,8,128]{2,1,0:T(8,128)}), f32[32,8,128]{2,1,0:T(8,128)S(1)}, u32[]{:S(2)}, u32[]{:S(2)}) async-start(f32[32,8,128]{2,1,0:T(8,128)} %get-tuple-element.24), calls=%async_computation | async-start | bytes 262144 | tf_op jit(solution)/shard_map/all_to_all | solution.py:841
  15.7 1.3 %collective-permute-done.3.whole.across = f32[80,8,128]{2,1,0:T(8,128)S(1)} collective-permute-done((f32[80,8,128]{2,1,0:T(8,128)S(1)}, f32[80,8,128]{2,1,0:T(8,128)S(1)}, u32[]{:S(2)}, u32[]{:S(2)}) %collective-permute-start.3) | collective-permute-done | bytes 327712 | tf_op jit(solution)/shard_map/ppermute | solution.py:820
  17.0 0.0 copy-start
  17.0 0.1 collective-permute-start.4
  17.1 0.5 %collective-permute-start.5 = (f32[20,8,128]{2,1,0:T(8,128)S(1)}, f32[20,8,128]{2,1,0:T(8,128)S(1)}, u32[]{:S(2)}, u32[]{:S(2)}) collective-permute-start(f32[20,8,128]{2,1,0:T(8,128)S(1)} %get-tuple-element.27), channel_id=1, source_target_pairs={{0,1},{1,0},{2,3},{3,2},{4,5},{5,4},{6,7},{7,6},{8,9},{9,8},{10,11... | collective-permute-start | bytes 245768 | tf_op jit(solution)/shard_map/ppermute | solution.py:844
  17.6 0.1 collective-permute-start.6
  17.7 0.4 %collective-permute-start.7 = (f32[20,8,128]{2,1,0:T(8,128)S(1)}, f32[20,8,128]{2,1,0:T(8,128)S(1)}, u32[]{:S(2)}, u32[]{:S(2)}) collective-permute-start(f32[20,8,128]{2,1,0:T(8,128)S(1)} %get-tuple-element.29), channel_id=1, source_target_pairs={{0,1},{1,0},{2,3},{3,2},{4,5},{5,4},{6,7},{7,6},{8,9},{9,8},{10,11... | collective-permute-start | bytes 245768 | tf_op jit(solution)/shard_map/ppermute | solution.py:844
  18.1 0.3 collective-permute-done.4.refs_0_
  18.4 0.2 collective-permute-done.5.refs_1_
  18.5 0.4 %collective-permute-done.6.refs_2_ = f32[20,8,128]{2,1,0:T(8,128)S(1)} collective-permute-done((f32[20,8,128]{2,1,0:T(8,128)S(1)}, f32[20,8,128]{2,1,0:T(8,128)S(1)}, u32[]{:S(2)}, u32[]{:S(2)}) %collective-permute-start.6) | collective-permute-done | bytes 81952 | tf_op jit(solution)/shard_map/ppermute | solution.py:844
  18.9 0.2 collective-permute-done.7.refs_3_
  19.1 0.4 %assemble.1 = (f32[16,10,8,128]{3,2,1,0:T(8,128)S(1)}, f32[16,5,8,128]{3,2,1,0:T(8,128)S(1)}, f32[16,5,8,128]{3,2,1,0:T(8,128)S(1)}) custom-call(f32[16,10,8,128]{3,2,1,0:T(8,128)S(1)} %get-tuple-element.25.before, f32[80,8,128]{2,1,0:T(8,128)S(1)} %collective-permute-done.3.whole.across, ...), custom_call_target="tpu_custom_call", output_to_operand_aliasing={{0}: (0, {})} | custom-call | tf_op jit(solution)/shard_map/assemble/pallas_call | solution.py:761
  19.5 4.5 %all-to-all-done.refs_5_ = f32[32,8,128]{2,1,0:T(8,128)S(1)} async-done(((f32[32,8,128]{2,1,0:T(8,128)}), f32[32,8,128]{2,1,0:T(8,128)S(1)}, u32[]{:S(2)}, u32[]{:S(2)}) %all-to-all-start) | async-done | bytes 131104 | tf_op jit(solution)/shard_map/all_to_all | solution.py:841
  24.0 3.1 %finish.1 = f32[1,8,5,16,256]{4,3,2,1,0:T(8,128)} custom-call(f32[21,8,128]{2,1,0:T(8,128)S(1)} %pack.1.shared.refs_1_.refs_0_, f32[21,8,128]{2,1,0:T(8,128)S(1)} %pass.1.refs_1_.partner, f32[101,8,128]{2,1,0:T(8,128)S(1)} %collective-permute-done.1.refs_2_.joined, f32[21,8,128]{2,1,0:T(8,128)S(1)} %collective-permute-done.2.refs_3_.last, ...), custom_call_target="tpu_custom_call" | custom-call | tf_op jit(solution)/shard_map/finish/pallas_call | solution.py:761
  (4 shorter events, 0.1 us)
Async XLA Ops:
  1.0 5.6 %collective-permute-start = (f32[21,8,128]{2,1,0:T(8,128)S(1)}, f32[21,8,128]{2,1,0:T(8,128)S(1)}, u32[]{:S(2)}, u32[]{:S(2)}) collective-permute-start(f32[21,8,128]{2,1,0:T(8,128)S(1)} %pack.1.shared.refs_1_.refs_0_), channel_id=1, source_target_pairs={{0,2},{1,3},{2,0},{3,1},{4,6},{5,7},{6,4},{7,5},{8,10},{9,11},{10,... | collective-permute-start | bytes 258056 | tf_op jit(solution)/shard_map/ppermute | solution.py:791
  6.4 2.3 %collective-permute-start.1 = (f32[101,8,128]{2,1,0:T(8,128)S(1)}, f32[101,8,128]{2,1,0:T(8,128)S(1)}, u32[]{:S(2)}, u32[]{:S(2)}) collective-permute-start(f32[101,8,128]{2,1,0:T(8,128)S(1)} %join.1), channel_id=1, source_target_pairs={{0,1},{1,0},{2,3},{3,2},{4,5},{5,4},{6,7},{7,6},{8,9},{9,8},{10,11... | collective-permute-start | bytes 1241096 | tf_op jit(solution)/shard_map/ppermute | solution.py:814
  6.6 2.1 %collective-permute-start.2 = (f32[21,8,128]{2,1,0:T(8,128)S(1)}, f32[21,8,128]{2,1,0:T(8,128)S(1)}, u32[]{:S(2)}, u32[]{:S(2)}) collective-permute-start(f32[21,8,128]{2,1,0:T(8,128)S(1)} %pass.1.refs_1_.partner), channel_id=1, source_target_pairs={{0,1},{1,0},{2,3},{3,2},{4,5},{5,4},{6,7},{7,6},{8,9},{9,8},{10,11... | collective-permute-start | bytes 258056 | tf_op jit(solution)/shard_map/ppermute | solution.py:819
  7.0 10.0 %collective-permute-start.3 = (f32[80,8,128]{2,1,0:T(8,128)S(1)}, f32[80,8,128]{2,1,0:T(8,128)S(1)}, u32[]{:S(2)}, u32[]{:S(2)}) collective-permute-start(f32[80,8,128]{2,1,0:T(8,128)S(1)} %get-tuple-element.22.refs_0_.refs_4_), channel_id=1, source_target_pairs={{0,2},{1,3},{2,0},{3,1},{4,6},{5,7},{6,4},{7,5},{8,10},{9,11},{10,... | collective-permute-start | bytes 983048 | tf_op jit(solution)/shard_map/ppermute | solution.py:820
  10.2 13.8 %all-to-all-start = ((f32[32,8,128]{2,1,0:T(8,128)}), f32[32,8,128]{2,1,0:T(8,128)S(1)}, u32[]{:S(2)}, u32[]{:S(2)}) async-start(f32[32,8,128]{2,1,0:T(8,128)} %get-tuple-element.24), calls=%async_computation | async-start | bytes 262144 | tf_op jit(solution)/shard_map/all_to_all | solution.py:841
  17.0 2.0 %copy-start = (f32[5,5]{1,0:T(8,128)S(1)}, f32[5,5]{1,0:T(8,128)}, u32[]{:S(2)}) copy-start(f32[5,5]{1,0:T(8,128)} %refs_4_.3) | copy-start | bytes 304
  17.0 1.3 %collective-permute-start.4 = (f32[20,8,128]{2,1,0:T(8,128)S(1)}, f32[20,8,128]{2,1,0:T(8,128)S(1)}, u32[]{:S(2)}, u32[]{:S(2)}) collective-permute-start(f32[20,8,128]{2,1,0:T(8,128)S(1)} %get-tuple-element.26), channel_id=1, source_target_pairs={{0,1},{1,0},{2,3},{3,2},{4,5},{5,4},{6,7},{7,6},{8,9},{9,8},{10,11... | collective-permute-start | bytes 245768 | tf_op jit(solution)/shard_map/ppermute | solution.py:844
  17.1 1.4 %collective-permute-start.5 = (f32[20,8,128]{2,1,0:T(8,128)S(1)}, f32[20,8,128]{2,1,0:T(8,128)S(1)}, u32[]{:S(2)}, u32[]{:S(2)}) collective-permute-start(f32[20,8,128]{2,1,0:T(8,128)S(1)} %get-tuple-element.27), channel_id=1, source_target_pairs={{0,1},{1,0},{2,3},{3,2},{4,5},{5,4},{6,7},{7,6},{8,9},{9,8},{10,11... | collective-permute-start | bytes 245768 | tf_op jit(solution)/shard_map/ppermute | solution.py:844
  17.6 1.3 %collective-permute-start.6 = (f32[20,8,128]{2,1,0:T(8,128)S(1)}, f32[20,8,128]{2,1,0:T(8,128)S(1)}, u32[]{:S(2)}, u32[]{:S(2)}) collective-permute-start(f32[20,8,128]{2,1,0:T(8,128)S(1)} %get-tuple-element.28), channel_id=1, source_target_pairs={{0,1},{1,0},{2,3},{3,2},{4,5},{5,4},{6,7},{7,6},{8,9},{9,8},{10,11... | collective-permute-start | bytes 245768 | tf_op jit(solution)/shard_map/ppermute | solution.py:844
  17.7 1.4 %collective-permute-start.7 = (f32[20,8,128]{2,1,0:T(8,128)S(1)}, f32[20,8,128]{2,1,0:T(8,128)S(1)}, u32[]{:S(2)}, u32[]{:S(2)}) collective-permute-start(f32[20,8,128]{2,1,0:T(8,128)S(1)} %get-tuple-element.29), channel_id=1, source_target_pairs={{0,1},{1,0},{2,3},{3,2},{4,5},{5,4},{6,7},{7,6},{8,9},{9,8},{10,11... | collective-permute-start | bytes 245768 | tf_op jit(solution)/shard_map/ppermute | solution.py:844

commit v8 on v7

--- a/solution.py
+++ b/solution.py
@@ -214,8 +214,15 @@
     return lax.broadcasted_iota(jnp.int32, shape, dim)
 
 
+def bits(size):
+    assert size & (size - 1) == 0
+    return size.bit_length() - 1
+
+
 def split_cell(cell, height, depth):
-    return cell // (height * depth), cell // depth % height, cell % depth
+    row_bits, column_bits = bits(height), bits(depth)
+    row = (cell >> column_bits) & (height - 1)
+    return cell >> (row_bits + column_bits), row, cell & (depth - 1)
 
 
 def neighbour_sum(field):
@@ -237,8 +244,8 @@
     lane = iota(receptors.shape, 1)
     allowed = jnp.zeros(receptors.shape, jnp.int32)
     for g in range(grids):
-        allowed = jnp.where(lane // FRINGE == g, counts[g, grid_index], allowed)
-    return jnp.where(lane % FRINGE < allowed, receptors + base, -1)
+        allowed = jnp.where(lane >> bits(FRINGE) == g, counts[g, grid_index], allowed)
+    return jnp.where((lane & (FRINGE - 1)) < allowed, receptors + base, -1)
 
 
 def receptor_mask(cell, total, height, depth):
@@ -303,7 +310,7 @@
     fields = jnp.concatenate([gain, mask], axis=1)
     donors = meta[0:1].astype(jnp.int32) - base
     twice = jnp.concatenate([donors, donors], axis=1)
-    step_z = iota(twice.shape, 1) // slots
+    step_z = iota(twice.shape, 1) >> bits(slots)
     plane, row, column = split_cell(twice, height, depth)
     onehot = jnp.where(iota((depth, LANES), 0) == column + step_z, 1.0, 0.0).astype(BF16)
     count = planes * (variables + 1) * height
@@ -335,14 +342,14 @@
     starts = jnp.broadcast_to(jnp.concatenate([meta[0:1], meta[0:1]], axis=1), (8, LANES))
     starts = pltpu.roll(starts, 8 * grid_index, 1)
     last = (sublane == 7) & (lane >= 64)
-    mine = last & (lane % 64 // 8 == grid_index)
+    mine = last & (((lane >> 3) & 7) == grid_index)
     for h in range(grids):
         tile = jnp.zeros((8, LANES), F32)
         for c in range(8):
             for k in (0, 1):
                 shift = (64 * k + 8 * c - (c % 2) * 64 - 8 * h) % LANES
                 moved = pltpu.roll(tiles[c // 2][k], shift, 1)
-                tile = jnp.where(lane // 8 == 8 * k + c, moved, tile)
+                tile = jnp.where(lane >> 3 == 8 * k + c, moved, tile)
         tile = jnp.where(last, cells, tile)
         out[h] = jnp.where(mine, pltpu.roll(starts, (LANES - 8 * h) % LANES, 1), tile)
 
@@ -361,7 +368,7 @@
     )
     find_corners(sizes, shared, corners)
     pair = jnp.where(
-        iota((2 * depth, depth), 0) // 2 == iota((2 * depth, depth), 1), 0.125, 0.0
+        iota((2 * depth, depth), 0) >> 1 == iota((2 * depth, depth), 1), 0.125, 0.0
     ).astype(BF16)
     count = step * variables
     for i, copy in enumerate(copies):
@@ -424,8 +431,8 @@
     grid_index = lax.axis_index("grid")
     count = planes * variables
     gather_rows(sizes, known, stage, rows)
-    pair[sub_index // 2] = known[0][...]
-    pair[1 - sub_index // 2] = known[1][...]
+    pair[sub_index >> 1] = known[0][...]
+    pair[1 - (sub_index >> 1)] = known[1][...]
     mask, _, _ = receptor_mask(rows[4:5, :].astype(jnp.int32), total, height, depth)
     mask_out[...] = mask
     wet[1 : total + 1] = mask
@@ -434,7 +441,7 @@
     add_planes(sizes, [own], plane_numbers(known[0][count], blocks), inner)
     add_planes(sizes, [joined], plane_numbers(known[2][count], blocks), inner)
     both[...] = padded[1 : total + 1]
-    core = sub_index % 2
+    core = sub_index & 1
     fields = []
     for k in range(2):
         start = (core + 2 * k) * planes
@@ -448,13 +455,13 @@
         fields.append(jnp.concatenate([restricted, swept], axis=1))
     half = jnp.concatenate([pair[0, count, :, 0:slots], pair[1, count, :, 0:slots]], axis=1)
     lane = iota((1, LANES), 1)
-    base = (core + 2 * (lane // slots)) * (planes * height * depth)
+    base = (core + 2 * (lane >> bits(slots))) * (planes * height * depth)
     values = interpolate(fields, half, base)
     empty = jnp.zeros((3, LANES), F32)
     first = jnp.concatenate([values[:variables], empty], axis=0)
     second = jnp.concatenate([values[variables:], empty], axis=0)
     second = pltpu.roll(second, 8 * grid_index, 1)
-    mine = iota((8, LANES), 1) % 64 // 8 == grid_index
+    mine = ((iota((8, LANES), 1) >> 3) & 7) == grid_index
     top = iota((8, LANES), 0) < variables
     for h in range(grids):
         tile = jnp.where(mine, pltpu.roll(second, (LANES - 8 * h) % LANES, 1), first)
@@ -473,12 +480,17 @@
     variables, blocks = sizes["coarse"][1], sizes["blocks"]
     width = min(pieces[0].shape[0] // variables, 2 * blocks)
     for q in range(blocks):
-        coarse = pl.ds(numbers[q] // 2, 1)
+        coarse = pl.ds(numbers[q] >> 1, 1)
         for k in range(2):
             i = k * blocks + q
             at = i % width * variables
             part = pieces[i // width][at : at + variables]
             both[coarse, pl.ds(k * variables, variables)] += part[None]
+
+
+def pass_kernel(sizes, source, out, last):
+    out[...] = source[...]
+    last[0] = source[source.shape[0] - 1]
 
 
 def join_kernel(sizes, *refs):
@@ -536,7 +548,7 @@
     plane, row, column = split_cell(jnp.maximum(cell, 0), height, depth)
     square = plane * plane + row * row + column * column
     square = jnp.where(cell >= 0, square, 1 << 15)
-    coarse = square // LANES * LANES
+    coarse = (square >> bits(LANES)) << bits(LANES)
     one = jnp.ones(cell.shape, jnp.int32)
     rows = [plane, row, column, one, one, one, -coarse, 2 + coarse - square]
     return jnp.concatenate([each.astype(F32) for each in rows], axis=0)
@@ -545,7 +557,7 @@
 def corner_features(cell, height, depth):
     plane, row, column = split_cell(cell, height, depth)
     square = plane * plane + row * row + column * column
-    coarse = square // LANES * LANES
+    coarse = (square >> bits(LANES)) << bits(LANES)
     one = jnp.ones(cell.shape, jnp.int32)
     rows = [2 * plane, 2 * row, 2 * column, -coarse, coarse - square, 0 * one, one, one]
     return jnp.concatenate([each.astype(F32) for each in rows], axis=0)
@@ -556,7 +568,7 @@
     _, _, height, depth = sizes["coarse"]
     lane = iota((8, LANES), 1)
     sublane = iota((8, LANES), 0)
-    group = lane % 64 // 8
+    group = (lane >> 3) & 7
     firsts = []
     for g in range(grids):
         halves = []
@@ -586,7 +598,7 @@
             cells[k] = jnp.where(sublane == g, pltpu.roll(high, (g + 1) % 8, 0), cells[k])
         scales.append(scale)
     targets, corners = [], []
-    step = ((group // 4) * height + group // 2 % 2) * depth + group % 2
+    step = ((group >> 2) * height + ((group >> 1) & 1)) * depth + (group & 1)
     for k in range(2):
         targets.append(jnp.where(group == sublane, -1.0, cells[k]))
         starts = jnp.where(group == sublane, cells[k], 0.0)
@@ -601,7 +613,7 @@
     corners = jnp.concatenate(corners, axis=1)
     theirs = target_features(targets, height, depth).T.astype(BF16)
     ours = corner_features(corners, height, depth)
-    which = iota(ours.shape, 0) % 8
+    which = iota(ours.shape, 0) & 7
     mine = [jnp.where(which == g, ours, 0.0).astype(BF16) for g in range(grids)]
     closeness = jnp.dot(theirs, jnp.concatenate(mine, axis=1), preferred_element_type=F32)
     closeness = closeness.astype(BF16)
@@ -626,7 +638,7 @@
         parts = values[k]
         for bit in (4, 2, 1):
             width = 8 * bit
-            lower = lane // width % 2 == 0
+            lower = (lane & width) == 0
             parts = [
                 jnp.where(
                     lower,
@@ -647,7 +659,7 @@
     pairs = values.shape[0] // 2
     plane, row, column = split_cell(cell, height, depth)
     onehot = jnp.where(iota((depth, count), 0) == column, 1.0, 0.0).astype(BF16)
-    row_here = (iota((2 * height, count), 0) % height == row) & (cell >= 0)
+    row_here = ((iota((2 * height, count), 0) & (height - 1)) == row) & (cell >= 0)
     tiles = []
     for i in range(pairs):
         twin = [jnp.broadcast_to(values[2 * i + k : 2 * i + k + 1], (height, count)) for k in (0, 1)]
@@ -697,16 +709,16 @@
     at_row = iota((variables, height, depth), 1)
     coarse_at = iota((depth, 2 * depth), 0)
     fine_at = iota((depth, 2 * depth), 1)
-    beside = fine_at // 2 - 1 + 2 * (fine_at % 2)
+    beside = (fine_at >> 1) - 1 + 2 * (fine_at & 1)
     widen = jnp.where(
-        coarse_at == fine_at // 2, 0.75, jnp.where(coarse_at == beside, 0.25, 0.0)
+        coarse_at == fine_at >> 1, 0.75, jnp.where(coarse_at == beside, 0.25, 0.0)
     ).astype(BF16)
     copies = []
     step = 2
     numbers = plane_numbers(parts[0][planes * variables], blocks)
     for q, number in enumerate(numbers):
-        coarse = number // 2
-        along = 0.75 * padded[coarse + 1] + 0.25 * padded[coarse + 2 * (number % 2)]
+        coarse = number >> 1
+        along = 0.75 * padded[coarse + 1] + 0.25 * padded[coarse + 2 * (number & 1)]
         below = jnp.where(at_row > 0, pltpu.roll(along, 1, 1), 0.0)
         above = jnp.where(at_row < height - 1, pltpu.roll(along, height - 1, 1), 0.0)
         block = slice(q * variables, (q + 1) * variables)
@@ -813,10 +825,17 @@
     )
     joined = lax.ppermute(joined, "sub", swap[1])
     own, partner = lax.optimization_barrier((own, partner))
-    partner = call(
-        join_kernel, "pass", jax.ShapeDtypeStruct(partner.shape, F32), partner, cost=pl.CostEstimate(flops=20_000_000_000, transcendentals=0, bytes_accessed=100_000_000)
-    )
-    known = (shared, partner, joined, lax.ppermute(partner, "sub", swap[1]))
+    partner, meta = call(
+        pass_kernel,
+        "pass",
+        [
+            jax.ShapeDtypeStruct(partner.shape, F32),
+            jax.ShapeDtypeStruct((1, height, depth), F32),
+        ],
+        partner,
+        cost=pl.CostEstimate(flops=20_000_000_000, transcendentals=0, bytes_accessed=100_000_000),
+    )
+    known = (shared, partner, joined, lax.ppermute(meta, "sub", swap[1]))
     across = lax.ppermute(own, "sub", swap[2])
     out, mask, both = call(
         partial_kernel,
@@ -842,13 +861,15 @@
     piece = jax.ShapeDtypeStruct((blocks // 2 * variables, height, depth), F32)
     pieces = call(split_kernel, "split", [piece] * 4, across)
     pieces = [lax.ppermute(each, "sub", swap[1]) for each in pieces]
+    last = lax.ppermute(partner, "sub", swap[1])
     both, source, gain = call(
         assemble_kernel,
         "assemble",
         [jax.ShapeDtypeStruct(both.shape, F32), full, full],
         both,
         across,
-        *known,
+        *known[:3],
+        last,
         *pieces,
         coupling,
         aliases={0: 0},

time: 27.4 us -> 27.2 us (level)
  waiting for transfers between devices: 6.82 us -> 6.51 us
    ppermute x1 -> x2, starting transfers between devices: 0.43 us -> 0.75 us  [the longest x1 0.43 us: fast_shards(): known = (shared, partner, joined, lax.ppermute(meta, 'sub', swap[1]))]
  transfers between devices with their start and end apart: 9 -> 10, of which waited for: 7 -> 7; matrix products, arithmetic and copies ran while one was open for 0% -> 0% of each run, Pallas kernels for 16% -> 16%
where the time goes in v8:
time: 27.2 us; the launch traced here: 27 us
  starting transfers between devices  12 us (44%)
  Pallas kernels  8.4 us (31%)
  waiting for transfers between devices  6.51 us (24%)
    pallas_call x8, Pallas kernels, call(): pl.pallas_call(functools.partial(kernel, sizes), out_shape=out_shape, in_...  8.4 us
    all_to_all x1, starting transfers between devices, fast_shards(): arrived = lax.all_to_all(out, ('grid', 'sub'), 0, 0, tiled=True)  5.42 us
    all_to_all x1, waiting for transfers between devices, fast_shards(): arrived = lax.all_to_all(out, ('grid', 'sub'), 0, 0, tiled=True)  4.39 us
    ppermute x1, starting transfers between devices, fast_shards(): partner = lax.ppermute(shared, 'sub', swap[2])  3.03 us
    ppermute x1, starting transfers between devices, fast_shards(): across = lax.ppermute(own, 'sub', swap[2])  1.66 us
    ppermute x4, starting transfers between devices, fast_shards(): pieces = [lax.ppermute(each, 'sub', swap[1]) for each in pieces]  1.08 us
    ppermute x1, waiting for transfers between devices, fast_shards(): across = lax.ppermute(own, 'sub', swap[2])  1.06 us
    ppermute x4, waiting for transfers between devices, fast_shards(): pieces = [lax.ppermute(each, 'sub', swap[1]) for each in pieces]  0.92 us
  transfers between devices with their start and end apart: 10, of which 7 were waited for; matrix products, arithmetic and copies ran while one was open for 0% of the time, Pallas kernels for 16%

profile of v8, /device:TPU:0, one launch (start us, length us, event | category | flops | bytes accessed | tf_op | source)
XLA Modules:
  0.0 27.0 jit_solution(11617696388942727359)
XLA Ops:
  0.0 1.0 %pack.1.shared.refs_1_.refs_0_ = f32[21,8,128]{2,1,0:T(8,128)S(1)} custom-call(s32[8,8]{1,0:T(8,128)} %counts.1, s32[1,8]{1,0:T(1,128)} %ids.1, f32[1,4,5,8,128]{4,3,2,1,0:T(8,128)} %diagonal.1, s32[1,1,64]{2,1,0:T(1,128)} %donors.1, f32[1,3,1,64]{3,2,1,0:T(1,128)} %bitcast.1, s32[1,1,64]{2,1,0:T(1,128)} %receptors.1), custom_call_target="tpu_custom_call" | custom-call | tf_op jit(solution)/shard_map/pack/pallas_call | solution.py:773
  1.0 3.0 %collective-permute-start = (f32[21,8,128]{2,1,0:T(8,128)S(1)}, f32[21,8,128]{2,1,0:T(8,128)S(1)}, u32[]{:S(2)}, u32[]{:S(2)}) collective-permute-start(f32[21,8,128]{2,1,0:T(8,128)S(1)} %pack.1.shared.refs_1_.refs_0_), channel_id=1, source_target_pairs={{0,2},{1,3},{2,0},{3,1},{4,6},{5,7},{6,4},{7,5},{8,10},{9,11},{10,... | collective-permute-start | bytes 258056 | tf_op jit(solution)/shard_map/ppermute | solution.py:803
  4.1 2.3 %restrict.1 = (f32[80,8,128]{2,1,0:T(8,128)S(1)}, f32[8,8,128]{2,1,0:T(8,128)S(1)}, f32[8,5,16,256]{3,2,1,0:T(8,128)S(1)}) custom-call(f32[1,8,5,16,256]{4,3,2,1,0:T(8,128)} %residual.1, f32[1,8,5,16,256]{4,3,2,1,0:T(8,128)} %fine.1, f32[21,8,128]{2,1,0:T(8,128)S(1)} %pack.1.shared.refs_1_.refs_0_), custom_call_target="tpu_custom_call" | custom-call | tf_op jit(solution)/shard_map/restrict/pallas_call | solution.py:773
  6.4 0.1 collective-permute-start.1
  6.5 0.1 collective-permute-done.source
  6.6 0.4 %collective-permute-start.2 = (f32[1,8,128]{2,1,0:T(8,128)S(1)}, f32[1,8,128]{2,1,0:T(8,128)S(1)}, u32[]{:S(2)}, u32[]{:S(2)}) collective-permute-start(f32[1,8,128]{2,1,0:T(8,128)S(1)} %get-tuple-element.25), channel_id=1, source_target_pairs={{0,1},{1,0},{2,3},{3,2},{4,5},{5,4},{6,7},{7,6},{8,9},{9,8},{10,11... | collective-permute-start | bytes 12296 | tf_op jit(solution)/shard_map/ppermute | solution.py:838
  7.0 1.7 %collective-permute-start.3 = (f32[80,8,128]{2,1,0:T(8,128)S(1)}, f32[80,8,128]{2,1,0:T(8,128)S(1)}, u32[]{:S(2)}, u32[]{:S(2)}) collective-permute-start(f32[80,8,128]{2,1,0:T(8,128)S(1)} %get-tuple-element.26.refs_0_.refs_4_), channel_id=1, source_target_pairs={{0,2},{1,3},{2,0},{3,1},{4,6},{5,7},{6,4},{7,5},{8,10},{9,11},{10,... | collective-permute-start | bytes 983048 | tf_op jit(solution)/shard_map/ppermute | solution.py:839
  8.7 0.0 collective-permute-done.2.refs_3_
  8.7 1.5 %partial.1 = (f32[32,8,128]{2,1,0:T(8,128)}, f32[16,1,8,128]{3,2,1,0:T(8,128)S(1)}, f32[16,10,8,128]{3,2,1,0:T(8,128)S(1)}) custom-call(f32[21,8,128]{2,1,0:T(8,128)S(1)} %pack.1.shared.refs_1_.refs_0_, f32[21,8,128]{2,1,0:T(8,128)S(1)} %get-tuple-element.24.refs_1_.partner, f32[101,8,128]{2,1,0:T(8,128)S(1)} %collective-permute-done.1.refs_2_.joined, ...), custom_call_target="tpu_custom_call" | custom-call | flops 20000000000 | bytes 100000000 | tf_op jit(solution)/shard_map/partial/pallas_call | solution.py:773
  10.2 5.4 %all-to-all-start = ((f32[32,8,128]{2,1,0:T(8,128)}), f32[32,8,128]{2,1,0:T(8,128)S(1)}, u32[]{:S(2)}, u32[]{:S(2)}) async-start(f32[32,8,128]{2,1,0:T(8,128)} %get-tuple-element.28), calls=%async_computation | async-start | bytes 262144 | tf_op jit(solution)/shard_map/all_to_all | solution.py:860
  15.6 0.3 %collective-permute-start.4 = (f32[21,8,128]{2,1,0:T(8,128)S(1)}, f32[21,8,128]{2,1,0:T(8,128)S(1)}, u32[]{:S(2)}, u32[]{:S(2)}) collective-permute-start(f32[21,8,128]{2,1,0:T(8,128)S(1)} %get-tuple-element.24.refs_1_.partner), channel_id=1, source_target_pairs={{0,1},{1,0},{2,3},{3,2},{4,5},{5,4},{6,7},{7,6},{8,9},{9,8},{10,11... | collective-permute-start | bytes 258056 | tf_op jit(solution)/shard_map/ppermute | solution.py:864
  15.9 1.1 %collective-permute-done.3.whole.across = f32[80,8,128]{2,1,0:T(8,128)S(1)} collective-permute-done((f32[80,8,128]{2,1,0:T(8,128)S(1)}, f32[80,8,128]{2,1,0:T(8,128)S(1)}, u32[]{:S(2)}, u32[]{:S(2)}) %collective-permute-start.3) | collective-permute-done | bytes 327712 | tf_op jit(solution)/shard_map/ppermute | solution.py:839
  17.0 0.0 copy-start
  17.0 0.1 collective-permute-start.5
  17.1 0.5 %collective-permute-start.6 = (f32[20,8,128]{2,1,0:T(8,128)S(1)}, f32[20,8,128]{2,1,0:T(8,128)S(1)}, u32[]{:S(2)}, u32[]{:S(2)}) collective-permute-start(f32[20,8,128]{2,1,0:T(8,128)S(1)} %get-tuple-element.31), channel_id=1, source_target_pairs={{0,1},{1,0},{2,3},{3,2},{4,5},{5,4},{6,7},{7,6},{8,9},{9,8},{10,11... | collective-permute-start | bytes 245768 | tf_op jit(solution)/shard_map/ppermute | solution.py:863
  17.6 0.1 collective-permute-start.7
  17.7 0.4 %collective-permute-start.8 = (f32[20,8,128]{2,1,0:T(8,128)S(1)}, f32[20,8,128]{2,1,0:T(8,128)S(1)}, u32[]{:S(2)}, u32[]{:S(2)}) collective-permute-start(f32[20,8,128]{2,1,0:T(8,128)S(1)} %get-tuple-element.33), channel_id=1, source_target_pairs={{0,1},{1,0},{2,3},{3,2},{4,5},{5,4},{6,7},{7,6},{8,9},{9,8},{10,11... | collective-permute-start | bytes 245768 | tf_op jit(solution)/shard_map/ppermute | solution.py:863
  18.1 0.3 collective-permute-done.5.refs_0_
  18.4 0.2 collective-permute-done.6.refs_1_
  18.5 0.4 %collective-permute-done.7.refs_2_ = f32[20,8,128]{2,1,0:T(8,128)S(1)} collective-permute-done((f32[20,8,128]{2,1,0:T(8,128)S(1)}, f32[20,8,128]{2,1,0:T(8,128)S(1)}, u32[]{:S(2)}, u32[]{:S(2)}) %collective-permute-start.7) | collective-permute-done | bytes 81952 | tf_op jit(solution)/shard_map/ppermute | solution.py:863
  18.9 0.2 collective-permute-done.8.refs_3_
  19.1 0.4 %assemble.1 = (f32[16,10,8,128]{3,2,1,0:T(8,128)S(1)}, f32[16,5,8,128]{3,2,1,0:T(8,128)S(1)}, f32[16,5,8,128]{3,2,1,0:T(8,128)S(1)}) custom-call(f32[16,10,8,128]{3,2,1,0:T(8,128)S(1)} %get-tuple-element.29.before, f32[80,8,128]{2,1,0:T(8,128)S(1)} %collective-permute-done.3.whole.across, ...), custom_call_target="tpu_custom_call", output_to_operand_aliasing={{0}: (0, {})} | custom-call | tf_op jit(solution)/shard_map/assemble/pallas_call | solution.py:773
  19.5 4.4 %all-to-all-done.refs_5_ = f32[32,8,128]{2,1,0:T(8,128)S(1)} async-done(((f32[32,8,128]{2,1,0:T(8,128)}), f32[32,8,128]{2,1,0:T(8,128)S(1)}, u32[]{:S(2)}, u32[]{:S(2)}) %all-to-all-start) | async-done | bytes 131104 | tf_op jit(solution)/shard_map/all_to_all | solution.py:860
  23.8 3.1 %finish.1 = f32[1,8,5,16,256]{4,3,2,1,0:T(8,128)} custom-call(f32[21,8,128]{2,1,0:T(8,128)S(1)} %pack.1.shared.refs_1_.refs_0_, f32[21,8,128]{2,1,0:T(8,128)S(1)} %get-tuple-element.24.refs_1_.partner, f32[101,8,128]{2,1,0:T(8,128)S(1)} %collective-permute-done.1.refs_2_.joined, f32[1,8,128]{2,1,0:T(8,128)S(1)} %collective-permute-done.2.refs_3_, ...), custom_call_target="tpu_custom_call" | custom-call | tf_op jit(solution)/shard_map/finish/pallas_call | solution.py:773
  (6 shorter events, 0.1 us)
Async XLA Ops:
  1.0 5.6 %collective-permute-start = (f32[21,8,128]{2,1,0:T(8,128)S(1)}, f32[21,8,128]{2,1,0:T(8,128)S(1)}, u32[]{:S(2)}, u32[]{:S(2)}) collective-permute-start(f32[21,8,128]{2,1,0:T(8,128)S(1)} %pack.1.shared.refs_1_.refs_0_), channel_id=1, source_target_pairs={{0,2},{1,3},{2,0},{3,1},{4,6},{5,7},{6,4},{7,5},{8,10},{9,11},{10,... | collective-permute-start | bytes 258056 | tf_op jit(solution)/shard_map/ppermute | solution.py:803
  6.4 2.3 %collective-permute-start.1 = (f32[101,8,128]{2,1,0:T(8,128)S(1)}, f32[101,8,128]{2,1,0:T(8,128)S(1)}, u32[]{:S(2)}, u32[]{:S(2)}) collective-permute-start(f32[101,8,128]{2,1,0:T(8,128)S(1)} %join.1), channel_id=1, source_target_pairs={{0,1},{1,0},{2,3},{3,2},{4,5},{5,4},{6,7},{7,6},{8,9},{9,8},{10,11... | collective-permute-start | bytes 1241096 | tf_op jit(solution)/shard_map/ppermute | solution.py:826
  6.6 2.1 %collective-permute-start.2 = (f32[1,8,128]{2,1,0:T(8,128)S(1)}, f32[1,8,128]{2,1,0:T(8,128)S(1)}, u32[]{:S(2)}, u32[]{:S(2)}) collective-permute-start(f32[1,8,128]{2,1,0:T(8,128)S(1)} %get-tuple-element.25), channel_id=1, source_target_pairs={{0,1},{1,0},{2,3},{3,2},{4,5},{5,4},{6,7},{7,6},{8,9},{9,8},{10,11... | collective-permute-start | bytes 12296 | tf_op jit(solution)/shard_map/ppermute | solution.py:838
  7.0 10.0 %collective-permute-start.3 = (f32[80,8,128]{2,1,0:T(8,128)S(1)}, f32[80,8,128]{2,1,0:T(8,128)S(1)}, u32[]{:S(2)}, u32[]{:S(2)}) collective-permute-start(f32[80,8,128]{2,1,0:T(8,128)S(1)} %get-tuple-element.26.refs_0_.refs_4_), channel_id=1, source_target_pairs={{0,2},{1,3},{2,0},{3,1},{4,6},{5,7},{6,4},{7,5},{8,10},{9,11},{10,... | collective-permute-start | bytes 983048 | tf_op jit(solution)/shard_map/ppermute | solution.py:839
  10.2 13.7 %all-to-all-start = ((f32[32,8,128]{2,1,0:T(8,128)}), f32[32,8,128]{2,1,0:T(8,128)S(1)}, u32[]{:S(2)}, u32[]{:S(2)}) async-start(f32[32,8,128]{2,1,0:T(8,128)} %get-tuple-element.28), calls=%async_computation | async-start | bytes 262144 | tf_op jit(solution)/shard_map/all_to_all | solution.py:860
  15.6 2.5 %collective-permute-start.4 = (f32[21,8,128]{2,1,0:T(8,128)S(1)}, f32[21,8,128]{2,1,0:T(8,128)S(1)}, u32[]{:S(2)}, u32[]{:S(2)}) collective-permute-start(f32[21,8,128]{2,1,0:T(8,128)S(1)} %get-tuple-element.24.refs_1_.partner), channel_id=1, source_target_pairs={{0,1},{1,0},{2,3},{3,2},{4,5},{5,4},{6,7},{7,6},{8,9},{9,8},{10,11... | collective-permute-start | bytes 258056 | tf_op jit(solution)/shard_map/ppermute | solution.py:864
  17.0 2.0 %copy-start = (f32[5,5]{1,0:T(8,128)S(1)}, f32[5,5]{1,0:T(8,128)}, u32[]{:S(2)}) copy-start(f32[5,5]{1,0:T(8,128)} %refs_4_.3) | copy-start | bytes 304
  17.0 1.3 %collective-permute-start.5 = (f32[20,8,128]{2,1,0:T(8,128)S(1)}, f32[20,8,128]{2,1,0:T(8,128)S(1)}, u32[]{:S(2)}, u32[]{:S(2)}) collective-permute-start(f32[20,8,128]{2,1,0:T(8,128)S(1)} %get-tuple-element.30), channel_id=1, source_target_pairs={{0,1},{1,0},{2,3},{3,2},{4,5},{5,4},{6,7},{7,6},{8,9},{9,8},{10,11... | collective-permute-start | bytes 245768 | tf_op jit(solution)/shard_map/ppermute | solution.py:863
  17.1 1.4 %collective-permute-start.6 = (f32[20,8,128]{2,1,0:T(8,128)S(1)}, f32[20,8,128]{2,1,0:T(8,128)S(1)}, u32[]{:S(2)}, u32[]{:S(2)}) collective-permute-start(f32[20,8,128]{2,1,0:T(8,128)S(1)} %get-tuple-element.31), channel_id=1, source_target_pairs={{0,1},{1,0},{2,3},{3,2},{4,5},{5,4},{6,7},{7,6},{8,9},{9,8},{10,11... | collective-permute-start | bytes 245768 | tf_op jit(solution)/shard_map/ppermute | solution.py:863
  17.6 1.3 %collective-permute-start.7 = (f32[20,8,128]{2,1,0:T(8,128)S(1)}, f32[20,8,128]{2,1,0:T(8,128)S(1)}, u32[]{:S(2)}, u32[]{:S(2)}) collective-permute-start(f32[20,8,128]{2,1,0:T(8,128)S(1)} %get-tuple-element.32), channel_id=1, source_target_pairs={{0,1},{1,0},{2,3},{3,2},{4,5},{5,4},{6,7},{7,6},{8,9},{9,8},{10,11... | collective-permute-start | bytes 245768 | tf_op jit(solution)/shard_map/ppermute | solution.py:863
  17.7 1.4 %collective-permute-start.8 = (f32[20,8,128]{2,1,0:T(8,128)S(1)}, f32[20,8,128]{2,1,0:T(8,128)S(1)}, u32[]{:S(2)}, u32[]{:S(2)}) collective-permute-start(f32[20,8,128]{2,1,0:T(8,128)S(1)} %get-tuple-element.33), channel_id=1, source_target_pairs={{0,1},{1,0},{2,3},{3,2},{4,5},{5,4},{6,7},{7,6},{8,9},{9,8},{10,11... | collective-permute-start | bytes 245768 | tf_op jit(solution)/shard_map/ppermute | solution.py:863

commit v9 on v8

--- a/solution.py
+++ b/solution.py
@@ -714,7 +714,7 @@
         coarse_at == fine_at >> 1, 0.75, jnp.where(coarse_at == beside, 0.25, 0.0)
     ).astype(BF16)
     copies = []
-    step = 2
+    step = 1
     numbers = plane_numbers(parts[0][planes * variables], blocks)
     for q, number in enumerate(numbers):
         coarse = number >> 1
@@ -893,7 +893,7 @@
             pltpu.VMEM((total + 2, variables, height, depth), F32),
             pltpu.VMEM((count, 2 * height, depth), F32),
             pltpu.VMEM(fine_solution.shape[1:], F32),
-            pltpu.SemaphoreType.DMA((blocks // 2,)),
+            pltpu.SemaphoreType.DMA((blocks,)),
         ],
         out_spec=HBM,
     )

time: 27.2 us -> 27.3 us (level)
  no operation moved by 1% of the time
where the time goes in v9:
time: 27.3 us; the launch traced here: 27.1 us
  starting transfers between devices  12 us (44%)
  Pallas kernels  8.48 us (31%)
  waiting for transfers between devices  6.51 us (24%)
    pallas_call x8, Pallas kernels, call(): pl.pallas_call(functools.partial(kernel, sizes), out_shape=out_shape, in_...  8.48 us
    all_to_all x1, starting transfers between devices, fast_shards(): arrived = lax.all_to_all(out, ('grid', 'sub'), 0, 0, tiled=True)  5.42 us
    all_to_all x1, waiting for transfers between devices, fast_shards(): arrived = lax.all_to_all(out, ('grid', 'sub'), 0, 0, tiled=True)  4.39 us
    ppermute x1, starting transfers between devices, fast_shards(): partner = lax.ppermute(shared, 'sub', swap[2])  3.03 us
    ppermute x1, starting transfers between devices, fast_shards(): across = lax.ppermute(own, 'sub', swap[2])  1.66 us
    ppermute x4, starting transfers between devices, fast_shards(): pieces = [lax.ppermute(each, 'sub', swap[1]) for each in pieces]  1.08 us
    ppermute x1, waiting for transfers between devices, fast_shards(): across = lax.ppermute(own, 'sub', swap[2])  1.06 us
    ppermute x4, waiting for transfers between devices, fast_shards(): pieces = [lax.ppermute(each, 'sub', swap[1]) for each in pieces]  0.92 us
  transfers between devices with their start and end apart: 10, of which 7 were waited for; matrix products, arithmetic and copies ran while one was open for 0% of the time, Pallas kernels for 16%

profile of v9, /device:TPU:0, one launch (start us, length us, event | category | flops | bytes accessed | tf_op | source)
XLA Modules:
  0.0 27.1 jit_solution(17311600447137242942)
XLA Ops:
  0.0 1.0 %pack.1.shared.refs_1_.refs_0_ = f32[21,8,128]{2,1,0:T(8,128)S(1)} custom-call(s32[8,8]{1,0:T(8,128)} %counts.1, s32[1,8]{1,0:T(1,128)} %ids.1, f32[1,4,5,8,128]{4,3,2,1,0:T(8,128)} %diagonal.1, s32[1,1,64]{2,1,0:T(1,128)} %donors.1, f32[1,3,1,64]{3,2,1,0:T(1,128)} %bitcast.1, s32[1,1,64]{2,1,0:T(1,128)} %receptors.1), custom_call_target="tpu_custom_call" | custom-call | tf_op jit(solution)/shard_map/pack/pallas_call | solution.py:773
  1.0 3.0 %collective-permute-start = (f32[21,8,128]{2,1,0:T(8,128)S(1)}, f32[21,8,128]{2,1,0:T(8,128)S(1)}, u32[]{:S(2)}, u32[]{:S(2)}) collective-permute-start(f32[21,8,128]{2,1,0:T(8,128)S(1)} %pack.1.shared.refs_1_.refs_0_), channel_id=1, source_target_pairs={{0,2},{1,3},{2,0},{3,1},{4,6},{5,7},{6,4},{7,5},{8,10},{9,11},{10,... | collective-permute-start | bytes 258056 | tf_op jit(solution)/shard_map/ppermute | solution.py:803
  4.1 2.3 %restrict.1 = (f32[80,8,128]{2,1,0:T(8,128)S(1)}, f32[8,8,128]{2,1,0:T(8,128)S(1)}, f32[8,5,16,256]{3,2,1,0:T(8,128)S(1)}) custom-call(f32[1,8,5,16,256]{4,3,2,1,0:T(8,128)} %residual.1, f32[1,8,5,16,256]{4,3,2,1,0:T(8,128)} %fine.1, f32[21,8,128]{2,1,0:T(8,128)S(1)} %pack.1.shared.refs_1_.refs_0_), custom_call_target="tpu_custom_call" | custom-call | tf_op jit(solution)/shard_map/restrict/pallas_call | solution.py:773
  6.4 0.1 collective-permute-start.1
  6.5 0.1 collective-permute-done.source
  6.6 0.4 %collective-permute-start.2 = (f32[1,8,128]{2,1,0:T(8,128)S(1)}, f32[1,8,128]{2,1,0:T(8,128)S(1)}, u32[]{:S(2)}, u32[]{:S(2)}) collective-permute-start(f32[1,8,128]{2,1,0:T(8,128)S(1)} %get-tuple-element.25), channel_id=1, source_target_pairs={{0,1},{1,0},{2,3},{3,2},{4,5},{5,4},{6,7},{7,6},{8,9},{9,8},{10,11... | collective-permute-start | bytes 12296 | tf_op jit(solution)/shard_map/ppermute | solution.py:838
  7.0 1.7 %collective-permute-start.3 = (f32[80,8,128]{2,1,0:T(8,128)S(1)}, f32[80,8,128]{2,1,0:T(8,128)S(1)}, u32[]{:S(2)}, u32[]{:S(2)}) collective-permute-start(f32[80,8,128]{2,1,0:T(8,128)S(1)} %get-tuple-element.26.refs_0_.refs_4_), channel_id=1, source_target_pairs={{0,2},{1,3},{2,0},{3,1},{4,6},{5,7},{6,4},{7,5},{8,10},{9,11},{10,... | collective-permute-start | bytes 983048 | tf_op jit(solution)/shard_map/ppermute | solution.py:839
  8.7 0.0 collective-permute-done.2.refs_3_
  8.7 1.5 %partial.1 = (f32[32,8,128]{2,1,0:T(8,128)}, f32[16,1,8,128]{3,2,1,0:T(8,128)S(1)}, f32[16,10,8,128]{3,2,1,0:T(8,128)S(1)}) custom-call(f32[21,8,128]{2,1,0:T(8,128)S(1)} %pack.1.shared.refs_1_.refs_0_, f32[21,8,128]{2,1,0:T(8,128)S(1)} %get-tuple-element.24.refs_1_.partner, f32[101,8,128]{2,1,0:T(8,128)S(1)} %collective-permute-done.1.refs_2_.joined, ...), custom_call_target="tpu_custom_call" | custom-call | flops 20000000000 | bytes 100000000 | tf_op jit(solution)/shard_map/partial/pallas_call | solution.py:773
  10.2 5.4 %all-to-all-start = ((f32[32,8,128]{2,1,0:T(8,128)}), f32[32,8,128]{2,1,0:T(8,128)S(1)}, u32[]{:S(2)}, u32[]{:S(2)}) async-start(f32[32,8,128]{2,1,0:T(8,128)} %get-tuple-element.28), calls=%async_computation | async-start | bytes 262144 | tf_op jit(solution)/shard_map/all_to_all | solution.py:860
  15.6 0.3 %collective-permute-start.4 = (f32[21,8,128]{2,1,0:T(8,128)S(1)}, f32[21,8,128]{2,1,0:T(8,128)S(1)}, u32[]{:S(2)}, u32[]{:S(2)}) collective-permute-start(f32[21,8,128]{2,1,0:T(8,128)S(1)} %get-tuple-element.24.refs_1_.partner), channel_id=1, source_target_pairs={{0,1},{1,0},{2,3},{3,2},{4,5},{5,4},{6,7},{7,6},{8,9},{9,8},{10,11... | collective-permute-start | bytes 258056 | tf_op jit(solution)/shard_map/ppermute | solution.py:864
  15.9 1.1 %collective-permute-done.3.whole.across = f32[80,8,128]{2,1,0:T(8,128)S(1)} collective-permute-done((f32[80,8,128]{2,1,0:T(8,128)S(1)}, f32[80,8,128]{2,1,0:T(8,128)S(1)}, u32[]{:S(2)}, u32[]{:S(2)}) %collective-permute-start.3) | collective-permute-done | bytes 327712 | tf_op jit(solution)/shard_map/ppermute | solution.py:839
  17.0 0.0 copy-start
  17.0 0.1 collective-permute-start.5
  17.1 0.5 %collective-permute-start.6 = (f32[20,8,128]{2,1,0:T(8,128)S(1)}, f32[20,8,128]{2,1,0:T(8,128)S(1)}, u32[]{:S(2)}, u32[]{:S(2)}) collective-permute-start(f32[20,8,128]{2,1,0:T(8,128)S(1)} %get-tuple-element.31), channel_id=1, source_target_pairs={{0,1},{1,0},{2,3},{3,2},{4,5},{5,4},{6,7},{7,6},{8,9},{9,8},{10,11... | collective-permute-start | bytes 245768 | tf_op jit(solution)/shard_map/ppermute | solution.py:863
  17.6 0.1 collective-permute-start.7
  17.7 0.4 %collective-permute-start.8 = (f32[20,8,128]{2,1,0:T(8,128)S(1)}, f32[20,8,128]{2,1,0:T(8,128)S(1)}, u32[]{:S(2)}, u32[]{:S(2)}) collective-permute-start(f32[20,8,128]{2,1,0:T(8,128)S(1)} %get-tuple-element.33), channel_id=1, source_target_pairs={{0,1},{1,0},{2,3},{3,2},{4,5},{5,4},{6,7},{7,6},{8,9},{9,8},{10,11... | collective-permute-start | bytes 245768 | tf_op jit(solution)/shard_map/ppermute | solution.py:863
  18.1 0.3 collective-permute-done.5.refs_0_
  18.4 0.2 collective-permute-done.6.refs_1_
  18.5 0.4 %collective-permute-done.7.refs_2_ = f32[20,8,128]{2,1,0:T(8,128)S(1)} collective-permute-done((f32[20,8,128]{2,1,0:T(8,128)S(1)}, f32[20,8,128]{2,1,0:T(8,128)S(1)}, u32[]{:S(2)}, u32[]{:S(2)}) %collective-permute-start.7) | collective-permute-done | bytes 81952 | tf_op jit(solution)/shard_map/ppermute | solution.py:863
  18.9 0.2 collective-permute-done.8.refs_3_
  19.1 0.4 %assemble.1 = (f32[16,10,8,128]{3,2,1,0:T(8,128)S(1)}, f32[16,5,8,128]{3,2,1,0:T(8,128)S(1)}, f32[16,5,8,128]{3,2,1,0:T(8,128)S(1)}) custom-call(f32[16,10,8,128]{3,2,1,0:T(8,128)S(1)} %get-tuple-element.29.before, f32[80,8,128]{2,1,0:T(8,128)S(1)} %collective-permute-done.3.whole.across, ...), custom_call_target="tpu_custom_call", output_to_operand_aliasing={{0}: (0, {})} | custom-call | tf_op jit(solution)/shard_map/assemble/pallas_call | solution.py:773
  19.5 4.4 %all-to-all-done.refs_5_ = f32[32,8,128]{2,1,0:T(8,128)S(1)} async-done(((f32[32,8,128]{2,1,0:T(8,128)}), f32[32,8,128]{2,1,0:T(8,128)S(1)}, u32[]{:S(2)}, u32[]{:S(2)}) %all-to-all-start) | async-done | bytes 131104 | tf_op jit(solution)/shard_map/all_to_all | solution.py:860
  23.8 3.2 %finish.1 = f32[1,8,5,16,256]{4,3,2,1,0:T(8,128)} custom-call(f32[21,8,128]{2,1,0:T(8,128)S(1)} %pack.1.shared.refs_1_.refs_0_, f32[21,8,128]{2,1,0:T(8,128)S(1)} %get-tuple-element.24.refs_1_.partner, f32[101,8,128]{2,1,0:T(8,128)S(1)} %collective-permute-done.1.refs_2_.joined, f32[1,8,128]{2,1,0:T(8,128)S(1)} %collective-permute-done.2.refs_3_, ...), custom_call_target="tpu_custom_call" | custom-call | tf_op jit(solution)/shard_map/finish/pallas_call | solution.py:773
  (6 shorter events, 0.1 us)
Async XLA Ops:
  1.0 5.6 %collective-permute-start = (f32[21,8,128]{2,1,0:T(8,128)S(1)}, f32[21,8,128]{2,1,0:T(8,128)S(1)}, u32[]{:S(2)}, u32[]{:S(2)}) collective-permute-start(f32[21,8,128]{2,1,0:T(8,128)S(1)} %pack.1.shared.refs_1_.refs_0_), channel_id=1, source_target_pairs={{0,2},{1,3},{2,0},{3,1},{4,6},{5,7},{6,4},{7,5},{8,10},{9,11},{10,... | collective-permute-start | bytes 258056 | tf_op jit(solution)/shard_map/ppermute | solution.py:803
  6.4 2.3 %collective-permute-start.1 = (f32[101,8,128]{2,1,0:T(8,128)S(1)}, f32[101,8,128]{2,1,0:T(8,128)S(1)}, u32[]{:S(2)}, u32[]{:S(2)}) collective-permute-start(f32[101,8,128]{2,1,0:T(8,128)S(1)} %join.1), channel_id=1, source_target_pairs={{0,1},{1,0},{2,3},{3,2},{4,5},{5,4},{6,7},{7,6},{8,9},{9,8},{10,11... | collective-permute-start | bytes 1241096 | tf_op jit(solution)/shard_map/ppermute | solution.py:826
  6.6 2.1 %collective-permute-start.2 = (f32[1,8,128]{2,1,0:T(8,128)S(1)}, f32[1,8,128]{2,1,0:T(8,128)S(1)}, u32[]{:S(2)}, u32[]{:S(2)}) collective-permute-start(f32[1,8,128]{2,1,0:T(8,128)S(1)} %get-tuple-element.25), channel_id=1, source_target_pairs={{0,1},{1,0},{2,3},{3,2},{4,5},{5,4},{6,7},{7,6},{8,9},{9,8},{10,11... | collective-permute-start | bytes 12296 | tf_op jit(solution)/shard_map/ppermute | solution.py:838
  7.0 10.0 %collective-permute-start.3 = (f32[80,8,128]{2,1,0:T(8,128)S(1)}, f32[80,8,128]{2,1,0:T(8,128)S(1)}, u32[]{:S(2)}, u32[]{:S(2)}) collective-permute-start(f32[80,8,128]{2,1,0:T(8,128)S(1)} %get-tuple-element.26.refs_0_.refs_4_), channel_id=1, source_target_pairs={{0,2},{1,3},{2,0},{3,1},{4,6},{5,7},{6,4},{7,5},{8,10},{9,11},{10,... | collective-permute-start | bytes 983048 | tf_op jit(solution)/shard_map/ppermute | solution.py:839
  10.2 13.7 %all-to-all-start = ((f32[32,8,128]{2,1,0:T(8,128)}), f32[32,8,128]{2,1,0:T(8,128)S(1)}, u32[]{:S(2)}, u32[]{:S(2)}) async-start(f32[32,8,128]{2,1,0:T(8,128)} %get-tuple-element.28), calls=%async_computation | async-start | bytes 262144 | tf_op jit(solution)/shard_map/all_to_all | solution.py:860
  15.6 2.5 %collective-permute-start.4 = (f32[21,8,128]{2,1,0:T(8,128)S(1)}, f32[21,8,128]{2,1,0:T(8,128)S(1)}, u32[]{:S(2)}, u32[]{:S(2)}) collective-permute-start(f32[21,8,128]{2,1,0:T(8,128)S(1)} %get-tuple-element.24.refs_1_.partner), channel_id=1, source_target_pairs={{0,1},{1,0},{2,3},{3,2},{4,5},{5,4},{6,7},{7,6},{8,9},{9,8},{10,11... | collective-permute-start | bytes 258056 | tf_op jit(solution)/shard_map/ppermute | solution.py:864
  17.0 2.0 %copy-start = (f32[5,5]{1,0:T(8,128)S(1)}, f32[5,5]{1,0:T(8,128)}, u32[]{:S(2)}) copy-start(f32[5,5]{1,0:T(8,128)} %refs_4_.3) | copy-start | bytes 304
  17.0 1.3 %collective-permute-start.5 = (f32[20,8,128]{2,1,0:T(8,128)S(1)}, f32[20,8,128]{2,1,0:T(8,128)S(1)}, u32[]{:S(2)}, u32[]{:S(2)}) collective-permute-start(f32[20,8,128]{2,1,0:T(8,128)S(1)} %get-tuple-element.30), channel_id=1, source_target_pairs={{0,1},{1,0},{2,3},{3,2},{4,5},{5,4},{6,7},{7,6},{8,9},{9,8},{10,11... | collective-permute-start | bytes 245768 | tf_op jit(solution)/shard_map/ppermute | solution.py:863
  17.1 1.4 %collective-permute-start.6 = (f32[20,8,128]{2,1,0:T(8,128)S(1)}, f32[20,8,128]{2,1,0:T(8,128)S(1)}, u32[]{:S(2)}, u32[]{:S(2)}) collective-permute-start(f32[20,8,128]{2,1,0:T(8,128)S(1)} %get-tuple-element.31), channel_id=1, source_target_pairs={{0,1},{1,0},{2,3},{3,2},{4,5},{5,4},{6,7},{7,6},{8,9},{9,8},{10,11... | collective-permute-start | bytes 245768 | tf_op jit(solution)/shard_map/ppermute | solution.py:863
  17.6 1.3 %collective-permute-start.7 = (f32[20,8,128]{2,1,0:T(8,128)S(1)}, f32[20,8,128]{2,1,0:T(8,128)S(1)}, u32[]{:S(2)}, u32[]{:S(2)}) collective-permute-start(f32[20,8,128]{2,1,0:T(8,128)S(1)} %get-tuple-element.32), channel_id=1, source_target_pairs={{0,1},{1,0},{2,3},{3,2},{4,5},{5,4},{6,7},{7,6},{8,9},{9,8},{10,11... | collective-permute-start | bytes 245768 | tf_op jit(solution)/shard_map/ppermute | solution.py:863
  17.7 1.4 %collective-permute-start.8 = (f32[20,8,128]{2,1,0:T(8,128)S(1)}, f32[20,8,128]{2,1,0:T(8,128)S(1)}, u32[]{:S(2)}, u32[]{:S(2)}) collective-permute-start(f32[20,8,128]{2,1,0:T(8,128)S(1)} %get-tuple-element.33), channel_id=1, source_target_pairs={{0,1},{1,0},{2,3},{3,2},{4,5},{5,4},{6,7},{7,6},{8,9},{9,8},{10,11... | collective-permute-start | bytes 245768 | tf_op jit(solution)/shard_map/ppermute | solution.py:863
